TPU v7x, 32 devices: a whole 2x2x4 slice. The times are simulated.
32 devices in a mesh: dp: 8 (over y, x, core), tensor: 4 (over z).
Axes of the slice: x: 2, y: 2, z: 4, core: 2. Of those that a mesh axis runs over, the one named last changes fastest.
Arguments:
- tokens: bfloat16 [2048, 2048], P('dp'), may hold values from -6 to 6
- cotangent: bfloat16 [2048, 2048], P('dp'), may hold values from -6 to 6
- attn_gain: float32 [2048], replicated, may hold values from 0.5 to 1.5
- q_weight: bfloat16 [2048, 3072], P(None, 'tensor'), may hold values from -0.125 to 0.125
- kv_down: bfloat16 [2048, 512], P(None, 'tensor'), may hold values from -0.125 to 0.125
- k_rope_weight: bfloat16 [2048, 64], P(None, 'tensor'), may hold values from -0.125 to 0.125
- kv_gain: float32 [512], replicated, may hold values from 0.5 to 1.5
- kv_up: bfloat16 [512, 4096], P(None, 'tensor'), may hold values from -0.25 to 0.25
- o_weight: bfloat16 [2048, 2048], P('tensor'), may hold values from -0.5 to 0.5
- ffn_gain: float32 [2048], replicated, may hold values from 0.5 to 1.5
- router_weight: float32 [2048, 32], replicated, may hold values from -0.0625 to 0.0625
- expert_ids: int32 [2048, 6], P('dp'), may hold values from 0 to 31, all different within a row; in each aligned block of 256 rows (0 to 255, 256 to 511, ...) at most 64 rows name the same one
- expert_gate: bfloat16 [32, 2048, 1408], P('dp', None, 'tensor'), may hold values from -0.125 to 0.125
- expert_up: bfloat16 [32, 2048, 1408], P('dp', None, 'tensor'), may hold values from -0.125 to 0.125
- expert_down: bfloat16 [32, 1408, 2048], P('dp', 'tensor'), may hold values from -6 to 6
- shared_gate: bfloat16 [2048, 2816], P(None, 'tensor'), may hold values from -0.125 to 0.125
- shared_up: bfloat16 [2048, 2816], P(None, 'tensor'), may hold values from -0.125 to 0.125
- shared_down: bfloat16 [2816, 2048], P('tensor'), may hold values from -0.109375 to 0.109375
Outputs:
- output: bfloat16 [2048, 2048], P('dp')
- input_grad: float32 [2048, 2048], P(('dp', 'tensor'))
- attn_gain_grad: float32 [2048], P(('dp', 'tensor'))
- q_weight_grad: float32 [2048, 3072], P('dp', 'tensor')
- kv_down_grad: float32 [2048, 512], P('dp', 'tensor')
- k_rope_grad: float32 [2048, 64], P('dp', 'tensor')
- kv_gain_grad: float32 [512], P(('dp', 'tensor'))
- kv_up_grad: float32 [512, 4096], P('dp', 'tensor')
- o_weight_grad: float32 [2048, 2048], P('tensor', 'dp')
- ffn_gain_grad: float32 [2048], P(('dp', 'tensor'))
- router_grad: float32 [2048, 32], P(('dp', 'tensor'))
- shared_gate_grad: float32 [2048, 2816], P('dp', 'tensor')
- shared_up_grad: float32 [2048, 2816], P('dp', 'tensor')
- shared_down_grad: float32 [2816, 2048], P('tensor', 'dp')
- expert_gate_grad: float32 [32, 2048, 1408], P('dp', None, 'tensor')
- expert_up_grad: float32 [32, 2048, 1408], P('dp', None, 'tensor')
- expert_down_grad: float32 [32, 1408, 2048], P('dp', 'tensor')
Inputs may be any that keep to these rules, and one draw needn't show every extreme that they name: `expert_ids`: each row names 6 different experts; among the 256 tokens of one index of dp no expert is named more than 64 times.
All inputs are finite; a program needn't handle non-finite values.
Results may differ from a plain program's by a relative error of at most 0.02.
Values may be sent and summed in bfloat16 or wider, within the bound.
No kernel may reach another device: no remote copies, remote signals or barrier semaphores. Data moves between devices by JAX's collectives and lax.ppermute only.
A program may use at most 320 MiB of HBM per device.

v0:
```python
import jax
import jax.numpy as jnp
from jax import lax
from jax.sharding import PartitionSpec as P

HD = 128
RD = 64
VD = 128
TOPK = 6
SEQ = 256
CAP = 64


EPSILON = 1e-06


def rope_tables(length, width):
    half_width = width // 2
    frequency = 10000.0 ** (-jnp.arange(half_width, dtype=jnp.float32) * (2.0 / width))
    angles = jnp.arange(length, dtype=jnp.float32)[:, None] * frequency[None, :]
    return (jnp.cos(angles), jnp.sin(angles))


def rotate(vector, cosine, sine_tab):
    half_width = vector.shape[-1] // 2
    lower_half = vector[..., :half_width]
    upper_half = vector[..., half_width:]
    return jnp.concatenate(
        [lower_half * cosine - upper_half * sine_tab, upper_half * cosine + lower_half * sine_tab],
        axis=-1,
    )


def unrotate(vector, cosine, sine_tab):
    half_width = vector.shape[-1] // 2
    lower_half = vector[..., :half_width]
    upper_half = vector[..., half_width:]
    return jnp.concatenate(
        [lower_half * cosine + upper_half * sine_tab, upper_half * cosine - lower_half * sine_tab],
        axis=-1,
    )


def rms_norm(values, gains):
    inv_rms = lax.rsqrt(jnp.mean(values * values, axis=-1, keepdims=True) + EPSILON)
    return (values * inv_rms * gains, inv_rms)


def rms_back(cotan, values, inv_rms, gains):
    weighted = cotan * gains
    inner_mean = jnp.mean(weighted * values, axis=-1, keepdims=True)
    value_grad = inv_rms * weighted - values * (inv_rms * inv_rms * inv_rms) * inner_mean
    gain_grad = jnp.sum(cotan * values * inv_rms, axis=0)
    return (value_grad, gain_grad)


def causal_scores(query_rot, key_full, factor):
    scores = (
        jnp.einsum("nqhd,nkhd->nhqk", query_rot, key_full, preferred_element_type=jnp.float32)
        * factor
    )
    length = query_rot.shape[1]
    causal = jnp.arange(length)[:, None] >= jnp.arange(length)[None, :]
    return jnp.where(causal, scores, -1e30)


def expert_backward(grad_in, rows_in, expert_gate, expert_up, expert_down):
    gate_hidden = jnp.einsum(
        "jscd,jdh->jsch", rows_in, expert_gate, preferred_element_type=jnp.float32
    )
    up_hidden = jnp.einsum("jscd,jdh->jsch", rows_in, expert_up, preferred_element_type=jnp.float32)
    sigmoid_h = jax.nn.sigmoid(gate_hidden)
    silu_h = gate_hidden * sigmoid_h
    activation = (silu_h * up_hidden).astype(jnp.bfloat16)
    dact = jnp.einsum("jscd,jhd->jsch", grad_in, expert_down, preferred_element_type=jnp.float32)
    gate_delta = (dact * up_hidden * sigmoid_h * (1.0 + gate_hidden * (1.0 - sigmoid_h))).astype(
        jnp.bfloat16
    )
    up_delta = (dact * silu_h).astype(jnp.bfloat16)
    row_grads = jnp.einsum(
        "jsch,jdh->jscd", gate_delta, expert_gate, preferred_element_type=jnp.float32
    )
    row_grads = (
        row_grads
        + jnp.einsum("jsch,jdh->jscd", up_delta, expert_up, preferred_element_type=jnp.float32)
    ).astype(jnp.bfloat16)
    back_rows = lax.all_to_all(row_grads, "dp", split_axis=1, concat_axis=1, tiled=True)
    return (back_rows, activation, gate_delta, up_delta)


def on_device(
    tokens,
    cotangent,
    attn_gain,
    q_weight,
    kv_down,
    k_rope_weight,
    kv_gain,
    kv_up,
    o_weight,
    ffn_gain,
    router_weight,
    expert_ids,
    expert_gate,
    expert_up,
    expert_down,
    shared_gate,
    shared_up,
    shared_down,
):
    tensor_count = lax.axis_size("tensor")
    data_count = lax.axis_size("dp")
    tensor_index = lax.axis_index("tensor")
    tok_rows = tokens.shape[0]
    model_width = tokens.shape[1]
    seq_count = tok_rows // SEQ
    local_heads = q_weight.shape[1] // (HD + RD)
    experts_all = router_weight.shape[1]
    experts_here = expert_gate.shape[0]
    factor = (HD + RD) ** (-0.5)
    cosine, sine_tab = rope_tables(SEQ, RD)
    head_cos = cosine[:, None, :]
    head_sin = sine_tab[:, None, :]
    tokens_f = tokens.astype(jnp.float32)
    normed_f, inv_first = rms_norm(tokens_f, attn_gain)
    normed = normed_f.astype(jnp.bfloat16)
    query_raw = jnp.dot(normed, q_weight, preferred_element_type=jnp.float32).reshape(
        seq_count, SEQ, local_heads, HD + RD
    )
    query_rot = jnp.concatenate(
        [query_raw[..., :HD], rotate(query_raw[..., HD:], head_cos, head_sin)], axis=-1
    ).astype(jnp.bfloat16)
    latent_own = jnp.dot(normed, kv_down, preferred_element_type=jnp.float32).astype(jnp.bfloat16)
    rope_own = jnp.dot(normed, k_rope_weight, preferred_element_type=jnp.float32).astype(
        jnp.bfloat16
    )
    latent, rope_key = (
        lax.all_gather(latent_own, "tensor", axis=1, tiled=True),
        lax.all_gather(rope_own, "tensor", axis=1, tiled=True),
    )
    latent_f = latent.astype(jnp.float32)
    latent_normed_f, inv_latent = rms_norm(latent_f, kv_gain)
    latent_normed = latent_normed_f.astype(jnp.bfloat16)
    key_value = (
        jnp.dot(latent_normed, kv_up, preferred_element_type=jnp.float32)
        .astype(jnp.bfloat16)
        .reshape(seq_count, SEQ, local_heads, HD + VD)
    )
    rope_rot = rotate(
        rope_key.astype(jnp.float32).reshape(seq_count, SEQ, RD), cosine, sine_tab
    ).astype(jnp.bfloat16)
    key_full = jnp.concatenate(
        [
            key_value[..., :HD],
            jnp.broadcast_to(rope_rot[:, :, None, :], (seq_count, SEQ, local_heads, RD)),
        ],
        axis=-1,
    )
    values = key_value[..., HD:]
    scores = causal_scores(query_rot, key_full, factor)
    top_score = jnp.max(scores, axis=-1, keepdims=True)
    log_total = top_score + jnp.log(jnp.sum(jnp.exp(scores - top_score), axis=-1, keepdims=True))
    weights = jnp.exp(scores - log_total).astype(jnp.bfloat16)
    attended = (
        jnp.einsum("nhqk,nkhd->nqhd", weights, values, preferred_element_type=jnp.float32)
        .astype(jnp.bfloat16)
        .reshape(tok_rows, local_heads * VD)
    )
    attn_sum = lax.psum(jnp.dot(attended, o_weight, preferred_element_type=jnp.float32), "tensor")
    hidden_one = tokens_f + attn_sum
    ffn_normed_f, inv_second = rms_norm(hidden_one, ffn_gain)
    ffn_normed = ffn_normed_f.astype(jnp.bfloat16)
    logits = jnp.dot(ffn_normed.astype(jnp.float32), router_weight, precision=lax.Precision.HIGHEST)
    router_prob = jax.nn.softmax(logits, axis=-1)
    chosen = expert_ids[:, :, None] == jnp.arange(experts_all, dtype=jnp.int32)[None, None, :]
    gate_vals = jnp.sum(jnp.where(chosen, router_prob[:, None, :], 0.0), axis=-1)
    flat_hits = chosen.reshape(tok_rows * TOPK, experts_all).astype(jnp.int32)
    earlier = jnp.cumsum(flat_hits, axis=0) - flat_hits
    slot_rank = jnp.sum(earlier * flat_hits, axis=1)
    flat_ids = expert_ids.reshape(-1)
    position = (flat_ids % experts_here * data_count + flat_ids // experts_here) * CAP + slot_rank
    buffer_rows = experts_here * data_count * CAP
    routed_in = jnp.repeat(ffn_normed, TOPK, axis=0)
    send_rows = (
        jnp.zeros((buffer_rows, model_width), jnp.bfloat16)
        .at[position]
        .set(routed_in)
        .reshape(experts_here, data_count, CAP, model_width)
    )
    received = lax.all_to_all(send_rows, "dp", split_axis=1, concat_axis=1, tiled=True)
    gate_hidden = jnp.einsum(
        "jscd,jdh->jsch", received, expert_gate, preferred_element_type=jnp.float32
    )
    up_hidden = jnp.einsum(
        "jscd,jdh->jsch", received, expert_up, preferred_element_type=jnp.float32
    )
    activation = (jax.nn.silu(gate_hidden) * up_hidden).astype(jnp.bfloat16)
    partial_out = jnp.einsum(
        "jsch,jhd->jscd", activation, expert_down, preferred_element_type=jnp.float32
    ).astype(jnp.bfloat16)
    returned = lax.all_to_all(partial_out, "dp", split_axis=1, concat_axis=1, tiled=True)
    outcome = returned
    returned = outcome
    routed_out = returned.reshape(buffer_rows, model_width)[position].reshape(
        tok_rows, TOPK, model_width
    )
    routed_sum = jnp.sum(gate_vals[:, :, None] * routed_out, axis=1)
    shared_gate_h = jnp.dot(ffn_normed, shared_gate, preferred_element_type=jnp.float32)
    shared_up_h = jnp.dot(ffn_normed, shared_up, preferred_element_type=jnp.float32)
    shared_act = (jax.nn.silu(shared_gate_h) * shared_up_h).astype(jnp.bfloat16)
    shared_out = jnp.dot(shared_act, shared_down, preferred_element_type=jnp.float32)
    ffn_sum = lax.psum(routed_sum + shared_out, "tensor")
    output = (hidden_one + ffn_sum).astype(jnp.bfloat16)
    out_grad = cotangent.astype(jnp.float32)
    gate_grad_part = jnp.sum(routed_out * out_grad[:, None, :], axis=-1)
    routed_grad = (
        (gate_vals[:, :, None] * out_grad[:, None, :])
        .astype(jnp.bfloat16)
        .reshape(tok_rows * TOPK, model_width)
    )
    grad_rows = (
        jnp.zeros((buffer_rows, model_width), jnp.bfloat16)
        .at[position]
        .set(routed_grad)
        .reshape(experts_here, data_count, CAP, model_width)
    )
    pieces = (
        lax.all_to_all(grad_rows, "dp", split_axis=1, concat_axis=1, tiled=True),
        lax.all_to_all(send_rows, "dp", split_axis=1, concat_axis=1, tiled=True),
    )
    results = expert_backward(pieces[0], pieces[1], expert_gate, expert_up, expert_down)
    back_rows, activation, gate_delta, up_delta, grad_recv, rows_recv = results + (
        pieces[0],
        pieces[1],
    )
    expert_gate_grad = jnp.einsum(
        "jscd,jsch->jdh", rows_recv, gate_delta, preferred_element_type=jnp.float32
    )
    expert_up_grad = jnp.einsum(
        "jscd,jsch->jdh", rows_recv, up_delta, preferred_element_type=jnp.float32
    )
    expert_down_grad = jnp.einsum(
        "jsch,jscd->jhd", activation, grad_recv, preferred_element_type=jnp.float32
    )
    routed_back = back_rows.reshape(buffer_rows, model_width)[position].reshape(
        tok_rows, TOPK, model_width
    )
    routed_dx = jnp.sum(routed_back.astype(jnp.float32), axis=1)
    shared_dact = jnp.dot(cotangent, shared_down.T, preferred_element_type=jnp.float32)
    sigmoid_s = jax.nn.sigmoid(shared_gate_h)
    silu_s = shared_gate_h * sigmoid_s
    shared_gate_delta = (
        shared_dact * shared_up_h * sigmoid_s * (1.0 + shared_gate_h * (1.0 - sigmoid_s))
    ).astype(jnp.bfloat16)
    shared_up_delta = (shared_dact * silu_s).astype(jnp.bfloat16)
    shared_down_grad = jnp.dot(shared_act.T, cotangent, preferred_element_type=jnp.float32)
    shared_gate_grad = jnp.dot(ffn_normed.T, shared_gate_delta, preferred_element_type=jnp.float32)
    shared_up_grad = jnp.dot(ffn_normed.T, shared_up_delta, preferred_element_type=jnp.float32)
    shared_dx = jnp.dot(
        shared_gate_delta, shared_gate.T, preferred_element_type=jnp.float32
    ) + jnp.dot(shared_up_delta, shared_up.T, preferred_element_type=jnp.float32)
    ffn_normed_sum, gate_grad = lax.psum((shared_dx + routed_dx, gate_grad_part), "tensor")
    prob_grad = jnp.sum(jnp.where(chosen, gate_grad[:, :, None], 0.0), axis=1)
    logit_grad = (
        router_prob * (prob_grad - jnp.sum(router_prob * prob_grad, axis=-1, keepdims=True))
    ).astype(jnp.bfloat16)
    router_grad = jnp.dot(ffn_normed.T, logit_grad, preferred_element_type=jnp.float32)
    ffn_normed_grad = ffn_normed_sum + jnp.dot(
        logit_grad.astype(jnp.float32), router_weight.T, precision=lax.Precision.HIGHEST
    )
    hidden_norm_grad, ffn_gain_grad = rms_back(ffn_normed_grad, hidden_one, inv_second, ffn_gain)
    hidden_grad = out_grad + hidden_norm_grad
    hidden_grad_b = hidden_grad.astype(jnp.bfloat16)
    o_weight_grad = jnp.dot(attended.T, hidden_grad_b, preferred_element_type=jnp.float32)
    attended_grad = (
        jnp.dot(hidden_grad_b, o_weight.T, preferred_element_type=jnp.float32)
        .astype(jnp.bfloat16)
        .reshape(seq_count, SEQ, local_heads, VD)
    )
    attn_probs = jnp.exp(causal_scores(query_rot, key_full, factor) - log_total)
    value_grad = jnp.einsum(
        "nhqk,nqhd->nkhd",
        attn_probs.astype(jnp.bfloat16),
        attended_grad,
        preferred_element_type=jnp.float32,
    )
    prob_dot = jnp.einsum(
        "nqhd,nkhd->nhqk", attended_grad, values, preferred_element_type=jnp.float32
    )
    score_grad = (
        attn_probs * (prob_dot - jnp.sum(attn_probs * prob_dot, axis=-1, keepdims=True)) * factor
    ).astype(jnp.bfloat16)
    query_grad = jnp.einsum(
        "nhqk,nkhd->nqhd", score_grad, key_full, preferred_element_type=jnp.float32
    )
    key_grad = jnp.einsum(
        "nhqk,nqhd->nkhd", score_grad, query_rot, preferred_element_type=jnp.float32
    )
    query_grad_b = (
        jnp.concatenate(
            [query_grad[..., :HD], unrotate(query_grad[..., HD:], head_cos, head_sin)], axis=-1
        )
        .astype(jnp.bfloat16)
        .reshape(tok_rows, local_heads * (HD + RD))
    )
    kv_grad = (
        jnp.concatenate([key_grad[..., :HD], value_grad], axis=-1)
        .astype(jnp.bfloat16)
        .reshape(tok_rows, local_heads * (HD + VD))
    )
    kv_up_grad = jnp.dot(latent_normed.T, kv_grad, preferred_element_type=jnp.float32)
    rope_part = jnp.sum(key_grad[..., HD:], axis=2).reshape(tok_rows, RD)
    latent_sum, rope_sum = lax.psum(
        (jnp.dot(kv_grad, kv_up.T, preferred_element_type=jnp.float32), rope_part), "tensor"
    )
    latent_grad, kv_gain_grad = rms_back(latent_sum, latent_f, inv_latent, kv_gain)
    rope_grad = unrotate(rope_sum.reshape(seq_count, SEQ, RD), cosine, sine_tab).reshape(
        tok_rows, RD
    )
    latent_cols = kv_down.shape[1]
    rope_cols = k_rope_weight.shape[1]
    latent_mine = lax.dynamic_slice_in_dim(
        latent_grad, tensor_index * latent_cols, latent_cols, 1
    ).astype(jnp.bfloat16)
    rope_mine = lax.dynamic_slice_in_dim(rope_grad, tensor_index * rope_cols, rope_cols, 1).astype(
        jnp.bfloat16
    )
    q_weight_grad = jnp.dot(normed.T, query_grad_b, preferred_element_type=jnp.float32)
    kv_down_grad = jnp.dot(normed.T, latent_mine, preferred_element_type=jnp.float32)
    k_rope_grad = jnp.dot(normed.T, rope_mine, preferred_element_type=jnp.float32)
    normed_part = jnp.dot(query_grad_b, q_weight.T, preferred_element_type=jnp.float32)
    normed_part = normed_part + jnp.dot(latent_mine, kv_down.T, preferred_element_type=jnp.float32)
    normed_part = normed_part + jnp.dot(
        rope_mine, k_rope_weight.T, preferred_element_type=jnp.float32
    )
    normed_grad = lax.psum(normed_part, "tensor")
    input_norm_grad, attn_gain_grad = rms_back(normed_grad, tokens_f, inv_first, attn_gain)
    input_grad = hidden_grad + input_norm_grad
    share_rows = tok_rows // tensor_count
    input_share = lax.dynamic_slice_in_dim(input_grad, tensor_index * share_rows, share_rows, 0)
    summed = (
        lax.psum_scatter(attn_gain_grad, "dp", scatter_dimension=0, tiled=True),
        lax.psum_scatter(q_weight_grad, "dp", scatter_dimension=0, tiled=True),
        lax.psum_scatter(kv_down_grad, "dp", scatter_dimension=0, tiled=True),
        lax.psum_scatter(k_rope_grad, "dp", scatter_dimension=0, tiled=True),
        lax.psum_scatter(kv_gain_grad, "dp", scatter_dimension=0, tiled=True),
        lax.psum_scatter(kv_up_grad, "dp", scatter_dimension=0, tiled=True),
        lax.psum_scatter(o_weight_grad, "dp", scatter_dimension=1, tiled=True),
        lax.psum_scatter(ffn_gain_grad, "dp", scatter_dimension=0, tiled=True),
        lax.psum_scatter(router_grad, "dp", scatter_dimension=0, tiled=True),
        lax.psum_scatter(shared_gate_grad, "dp", scatter_dimension=0, tiled=True),
        lax.psum_scatter(shared_up_grad, "dp", scatter_dimension=0, tiled=True),
        lax.psum_scatter(shared_down_grad, "dp", scatter_dimension=1, tiled=True),
    )

    def own_slice(whole_grad):
        piece_rows = whole_grad.shape[0] // tensor_count
        return lax.dynamic_slice_in_dim(whole_grad, tensor_index * piece_rows, piece_rows, 0)

    return (
        output,
        input_share,
        own_slice(summed[0]),
        summed[1],
        summed[2],
        summed[3],
        own_slice(summed[4]),
        summed[5],
        summed[6],
        own_slice(summed[7]),
        own_slice(summed[8]),
        summed[9],
        summed[10],
        summed[11],
        expert_gate_grad,
        expert_up_grad,
        expert_down_grad,
    )


def solution(mesh):
    in_specs = (
        P("dp", None),
        P("dp", None),
        P(),
        P(None, "tensor"),
        P(None, "tensor"),
        P(None, "tensor"),
        P(),
        P(None, "tensor"),
        P("tensor", None),
        P(),
        P(),
        P("dp", None),
        P("dp", None, "tensor"),
        P("dp", None, "tensor"),
        P("dp", "tensor", None),
        P(None, "tensor"),
        P(None, "tensor"),
        P("tensor", None),
    )
    out_specs = (
        P("dp", None),
        P(("dp", "tensor"), None),
        P(("dp", "tensor")),
        P("dp", "tensor"),
        P("dp", "tensor"),
        P("dp", "tensor"),
        P(("dp", "tensor")),
        P("dp", "tensor"),
        P("tensor", "dp"),
        P(("dp", "tensor")),
        P(("dp", "tensor"), None),
        P("dp", "tensor"),
        P("dp", "tensor"),
        P("tensor", "dp"),
        P("dp", None, "tensor"),
        P("dp", None, "tensor"),
        P("dp", "tensor", None),
    )
    return jax.shard_map(
        on_device, mesh=mesh, in_specs=in_specs, out_specs=out_specs, check_vma=False
    )
```

profile of v0, /device:TPU:0, one launch (start us, length us, event | category | flops | bytes accessed | tf_op | source)
XLA Modules:
  0.0 1403.2 jit_solution(12650072786706320196)
XLA Ops:
  55.7 15.9 %reduce-window.6 = s32[32,12,128]{2,1,0:T(8,128)S(1)} reduce-window(s32[32,12,128]{2,1,0:T(8,128)} %fusion.63, s32[]{:T(128)} %constant.73.clone.1), window={size=1x1x128 pad=0_0x0_0x127_0}, to_apply=%region_9.10 | reduce-window | flops 6242304 | bytes 393220 | tf_op jit(solution)/shard_map/reduce-window
  74.0 67.4 %all-reduce.11.cloned.1.call-done = f32[256,2048]{1,0:T(8,128)} async-done(((f32[256,2048]{1,0:T(8,128)}), f32[256,2048]{1,0:T(8,128)}) %all-reduce.11.cloned.1.call-update) | async-done | bytes 2097168 | tf_op jit(solution)/shard_map/psum | solution.py:169
  163.3 15.6 %scatter_custom_fusion = bf16[2048,2048]{1,0:T(8,128)(2,1)} fusion(s32[1536]{0:T(1024)S(1)} %fusion.89, bf16[1536,2048]{1,0:T(8,128)(2,1)} %reshape.589, bf16[]{:T(256)} %constant.72.clone.1), kind=kCustom, calls=%fused_computation.32 | custom fusion | bytes 8389120 | tf_op jit(solution)/shard_map/scatter | solution.py:187
  201.5 15.7 %mul.675 = f32[1536,2048]{1,0:T(8,128)} reshape(f32[256,6,2048]{2,1,0:T(8,128)} %mul.674) | data formatting | bytes 25165824 | tf_op jit(solution)/shard_map/mul | solution.py:217
  220.4 16.3 %scatter_custom_fusion.1 = bf16[2048,2048]{1,0:T(8,128)(2,1)} fusion(s32[1536]{0:T(1024)S(1)} %fusion.89, f32[1536,2048]{1,0:T(8,128)} %mul.675, f32[1536]{0:T(1024)S(1)} %mul.672, bf16[]{:T(256)} %constant.72.clone.1), kind=kCustom, calls=%fused_computation.17 | custom fusion | flops 6291456 | bytes 20979714 | tf_op jit(solution)/shard_map/scatter | solution.py:224
  245.2 41.2 %all-to-all-done = bf16[4,8,64,2048]{3,2,0,1:T(8,128)(2,1)} async-done(((bf16[4,8,64,2048]{3,2,0,1:T(8,128)(2,1)}), bf16[4,8,64,2048]{3,2,0,1:T(8,128)(2,1)}, u32[]{:S(2)}, u32[]{:S(2)}) %all-to-all-start) | async-done | bytes 8388640 | tf_op jit(solution)/shard_map/all_to_all | solution.py:190
  314.0 71.5 %all-to-all-done.2 = bf16[4,8,64,2048]{3,2,0,1:T(8,128)(2,1)} async-done(((bf16[4,8,64,2048]{3,2,0,1:T(8,128)(2,1)}), bf16[4,8,64,2048]{3,2,0,1:T(8,128)(2,1)}, u32[]{:S(2)}, u32[]{:S(2)}) %all-to-all-start.2) | async-done | bytes 8388640 | tf_op jit(solution)/shard_map/all_to_all | solution.py:228
  413.4 15.8 %add_convert_fusion = bf16[4,8,64,2048]{3,2,1,0:T(8,128)(2,1)} fusion(f32[4,8,64,2048]{3,2,1,0:T(8,128)} %fusion.13, bf16[4,8,64,352]{3,2,1,0:T(8,128)(2,1)} %get-tuple-element.36, bf16[4,2048,352]{1,2,0:T(8,128)(2,1)} %param.31), kind=kOutput, calls=%fused_computation.6 | convolution fusion | flops 2961178624 | bytes 32374784 | tf_op jit(solution)/shard_map/jsch,jdh->jscd/dot_general | solution.py:85
  462.2 74.5 %all-to-all-done.3 = bf16[4,8,64,2048]{3,2,0,1:T(8,128)(2,1)} async-done(((bf16[4,8,64,2048]{3,2,0,1:T(8,128)(2,1)}), bf16[4,8,64,2048]{3,2,0,1:T(8,128)(2,1)}, u32[]{:S(2)}, u32[]{:S(2)}) %all-to-all-start.3) | async-done | bytes 8388640 | tf_op jit(solution)/shard_map/all_to_all | solution.py:87
  561.1 17.2 %gather_fusion.1 = bf16[1536,2048]{1,0:T(8,128)(2,1)} fusion(bf16[2048,2048]{1,0:T(8,128)(2,1)} %bitcast.156, s32[2048]{0:T(1024)S(1)} %pad_clamp_fusion), kind=kCustom, calls=%fused_computation.1 | custom fusion | bytes 12589056 | tf_op jit(solution)/shard_map/gather | solution.py:245
  609.2 27.0 %all-to-all-done.1 = bf16[4,8,64,2048]{3,2,0,1:T(8,128)(2,1)} async-done(((bf16[4,8,64,2048]{3,2,0,1:T(8,128)(2,1)}), bf16[4,8,64,2048]{3,2,0,1:T(8,128)(2,1)}, u32[]{:S(2)}, u32[]{:S(2)}) %all-to-all-start.1) | async-done | bytes 8388640 | tf_op jit(solution)/shard_map/all_to_all | solution.py:201
  644.6 17.2 %gather_fusion = bf16[1536,2048]{1,0:T(8,128)(2,1)} fusion(bf16[2048,2048]{1,0:T(8,128)(2,1)} %bitcast.155, s32[2048]{0:T(1024)S(1)} %pad_clamp_fusion), kind=kCustom, calls=%fused_computation | custom fusion | bytes 12589056 | tf_op jit(solution)/shard_map/gather | solution.py:204
  685.8 19.9 %psum.52 = f32[256,6]{1,0:T(8,128)S(1)} all-reduce(f32[256,6]{1,0:T(8,128)} %get-tuple-element.17), channel_id=1, replica_groups=mesh['dp'=8,'tensor'=4] {'tensor'}, use_global_device_ids=true, to_apply=%region_19.20 | all-reduce | flops 1536 | bytes 12288 | tf_op jit(solution)/shard_map/psum | solution.py:262
  748.4 22.4 %all-reduce.17.cloned.1.call-done = (f32[256,512]{1,0:T(8,128)}, f32[1,256,64]{1,2,0:T(8,128)}) async-done(((f32[256,512]{1,0:T(8,128)}, f32[1,256,64]{1,2,0:T(8,128)}), (f32[256,512]{1,0:T(8,128)}, f32[1,256,64]{1,2,0:T(8,128)})) %all-reduce.17.cloned.1.call-update) | async-done | bytes 589840 | tf_op jit(solution)/shard_map/psum | solution.py:313
  851.2 113.3 %all-reduce.15.cloned.1.call-done = (f32[256,2048]{1,0:T(8,128)}, f32[256,2048]{1,0:T(8,128)}) async-done(((f32[256,2048]{1,0:T(8,128)}, f32[256,2048]{1,0:T(8,128)}), (f32[256,2048]{1,0:T(8,128)}, f32[256,2048]{1,0:T(8,128)})) %all-reduce.15.cloned.1.call-update) | async-done | bytes 4194320 | tf_op jit(solution)/shard_map/psum | solution.py:212
  968.2 24.0 %all-reduce.3 = (f32[2048]{0:T(1024)S(1)}, f32[512]{0:T(512)S(1)}, f32[2048]{0:T(1024)S(1)}) all-reduce(f32[2048]{0:T(1024)S(1)} %get-tuple-element.21, f32[512]{0:T(512)S(1)} %get-tuple-element.23, f32[2048]{0:T(1024)S(1)} %copy-done.54), channel_id=2, replica_groups=mesh['dp'=8,'tensor'=4] {'dp'}, use_global_device_ids=true, to_apply=%region_31.32.clone | all-reduce | flops 4608 | bytes 36864
  999.2 27.3 %reduce-scatter.22.cloned.1.call-done = f32[256,704]{0,1:T(8,128)} async-done(((f32[2048,704]{0,1:T(8,128)}), f32[256,704]{0,1:T(8,128)}) %reduce-scatter.22.cloned.1.call-update) | async-done | bytes 720912 | tf_op jit(solution)/shard_map/reduce_scatter | solution.py:351
  1026.5 63.4 %reduce-scatter.24.cloned.1.call-done = f32[256,704]{0,1:T(8,128)} async-done(((f32[2048,704]{0,1:T(8,128)}), f32[256,704]{0,1:T(8,128)}) %reduce-scatter.24.cloned.1.call-update) | async-done | bytes 720912 | tf_op jit(solution)/shard_map/reduce_scatter | solution.py:352
  1089.9 63.1 %reduce-scatter.26.cloned.1.call-done = f32[704,256]{1,0:T(8,128)} async-done(((f32[704,2048]{1,0:T(8,128)}), f32[704,256]{1,0:T(8,128)}) %reduce-scatter.26.cloned.1.call-update) | async-done | bytes 720912 | tf_op jit(solution)/shard_map/reduce_scatter | solution.py:353
  1153.0 37.2 %reduce-scatter.14.cloned.1.call-done = f32[256,16]{0,1:T(8,128)} async-done(((f32[2048,16]{0,1:T(8,128)}), f32[256,16]{0,1:T(8,128)}) %reduce-scatter.14.cloned.1.call-update) | async-done | bytes 16400 | tf_op jit(solution)/shard_map/reduce_scatter | solution.py:345
  1190.2 39.7 %reduce-scatter.12.cloned.1.call-done = f32[256,128]{1,0:T(8,128)} async-done(((f32[2048,128]{1,0:T(8,128)}), f32[256,128]{1,0:T(8,128)}) %reduce-scatter.12.cloned.1.call-update) | async-done | bytes 131088 | tf_op jit(solution)/shard_map/reduce_scatter | solution.py:344
  1229.9 45.1 %reduce-scatter.16.cloned.1.call-done = f32[64,1024]{1,0:T(8,128)} async-done(((f32[512,1024]{1,0:T(8,128)}), f32[64,1024]{1,0:T(8,128)}) %reduce-scatter.16.cloned.1.call-update) | async-done | bytes 262160 | tf_op jit(solution)/shard_map/reduce_scatter | solution.py:347
  1275.0 55.5 %reduce-scatter.18.cloned.1.call-done = f32[512,256]{1,0:T(8,128)} async-done(((f32[512,2048]{1,0:T(8,128)}), f32[512,256]{1,0:T(8,128)}) %reduce-scatter.18.cloned.1.call-update) | async-done | bytes 524304 | tf_op jit(solution)/shard_map/reduce_scatter | solution.py:348
  1330.5 65.7 %reduce-scatter.10.cloned.1.call-done = f32[256,768]{1,0:T(8,128)} async-done(((f32[2048,768]{1,0:T(8,128)}), f32[256,768]{1,0:T(8,128)}) %reduce-scatter.10.cloned.1.call-update) | async-done | bytes 786448 | tf_op jit(solution)/shard_map/reduce_scatter | solution.py:343
  (297 shorter events, 414.7 us)
Async XLA Ops:
  7.2 39.8 %copy-start = (bf16[2048,768]{1,0:T(8,128)(2,1)S(1)}, bf16[2048,768]{1,0:T(8,128)(2,1)}, u32[]{:S(2)}) copy-start(bf16[2048,768]{1,0:T(8,128)(2,1)} %param.21) | copy-start | bytes 9437188
  7.2 134.2 %all-reduce.11.cloned.1.call-start = ((), (), s32[]{:S(2)}) async-start(), calls=%async_computation.13 | async-start | bytes 4194304 | tf_op jit(solution)/shard_map/psum | solution.py:169
  7.3 39.4 %copy-start.64 = (f32[32]{0:T(128)}, f32[32]{0:T(128)S(1)}, u32[]{:S(2)}) copy-start(f32[32]{0:T(128)S(1)} %multiply_power_fusion) | copy-start | bytes 388
  9.6 37.4 %copy-start.55 = (f32[256]{0:T(256)}, f32[256]{0:T(256)S(1)}, u32[]{:S(2)}) copy-start(f32[256]{0:T(256)S(1)} %get-tuple-element.51) | copy-start | bytes 3076
  73.8 71.2 %copy-start.39 = (f32[2048]{0:T(1024)S(1)}, f32[2048]{0:T(1024)}, u32[]{:S(2)}) copy-start(f32[2048]{0:T(1024)} %param.27) | copy-start | bytes 24580
  187.3 99.1 %all-to-all-start = ((bf16[4,8,64,2048]{3,2,0,1:T(8,128)(2,1)}), bf16[4,8,64,2048]{3,2,0,1:T(8,128)(2,1)}, u32[]{:S(2)}, u32[]{:S(2)}) async-start(bf16[4,8,64,2048]{3,2,0,1:T(8,128)(2,1)} %copy.161), calls=%async_computation | async-start | bytes 16777216 | tf_op jit(solution)/shard_map/all_to_all | solution.py:190
  286.4 99.0 %all-to-all-start.2 = ((bf16[4,8,64,2048]{3,2,0,1:T(8,128)(2,1)}), bf16[4,8,64,2048]{3,2,0,1:T(8,128)(2,1)}, u32[]{:S(2)}, u32[]{:S(2)}) async-start(bf16[4,8,64,2048]{3,2,0,1:T(8,128)(2,1)} %copy.167), calls=%async_computation.2 | async-start | bytes 16777216 | tf_op jit(solution)/shard_map/all_to_all | solution.py:228
  437.7 99.0 %all-to-all-start.3 = ((bf16[4,8,64,2048]{3,2,0,1:T(8,128)(2,1)}), bf16[4,8,64,2048]{3,2,0,1:T(8,128)(2,1)}, u32[]{:S(2)}, u32[]{:S(2)}) async-start(bf16[4,8,64,2048]{3,2,0,1:T(8,128)(2,1)} %copy.169), calls=%async_computation.3 | async-start | bytes 16777216 | tf_op jit(solution)/shard_map/all_to_all | solution.py:87
  536.7 99.4 %all-to-all-start.1 = ((bf16[4,8,64,2048]{3,2,0,1:T(8,128)(2,1)}), bf16[4,8,64,2048]{3,2,0,1:T(8,128)(2,1)}, u32[]{:S(2)}, u32[]{:S(2)}) async-start(bf16[4,8,64,2048]{3,2,0,1:T(8,128)(2,1)} %copy.164), calls=%async_computation.1 | async-start | bytes 16777216 | tf_op jit(solution)/shard_map/all_to_all | solution.py:201
  542.1 166.6 %all-reduce.13.cloned.1.call-start = ((), (), s32[]{:S(2)}) async-start(), calls=%async_computation.14 | async-start | bytes 4194304 | tf_op jit(solution)/shard_map/psum | solution.py:262
  549.5 50.3 %copy-start.23 = (bf16[256,704]{0,1:T(8,128)(2,1)}, bf16[256,704]{0,1:T(8,128)(2,1)S(1)}, u32[]{:S(2)}) copy-start(bf16[256,704]{0,1:T(8,128)(2,1)S(1)} %get-tuple-element.39) | copy-start | bytes 1081348
  605.3 165.5 %all-reduce.17.cloned.1.call-start = ((), (), s32[]{:S(2)}) async-start(), calls=%async_computation.25 | async-start | bytes 1179648 | tf_op jit(solution)/shard_map/psum | solution.py:313
  673.6 35.1 %copy-start.40 = (f32[2048]{0:T(1024)S(1)}, f32[2048]{0:T(1024)}, u32[]{:S(2)}) copy-start(f32[2048]{0:T(1024)} %param.27) | copy-start | bytes 24580
  734.2 115.7 %reduce-scatter.20.cloned.1.call-start = ((), (), s32[]{:S(2)}) async-start(), calls=%async_computation.20 | async-start | bytes 294912 | tf_op jit(solution)/shard_map/reduce_scatter | solution.py:350
  741.6 222.9 %all-reduce.15.cloned.1.call-start = ((), (), s32[]{:S(2)}) async-start(), calls=%async_computation.24 | async-start | bytes 8388608 | tf_op jit(solution)/shard_map/psum | solution.py:212
  777.2 249.3 %reduce-scatter.22.cloned.1.call-start = ((), (), s32[]{:S(2)}) async-start(), calls=%async_computation.21 | async-start | bytes 6488064 | tf_op jit(solution)/shard_map/reduce_scatter | solution.py:351
  782.0 307.9 %reduce-scatter.24.cloned.1.call-start = ((), (), s32[]{:S(2)}) async-start(), calls=%async_computation.22 | async-start | bytes 6488064 | tf_op jit(solution)/shard_map/reduce_scatter | solution.py:352
  786.8 366.2 %reduce-scatter.26.cloned.1.call-start = ((), (), s32[]{:S(2)}) async-start(), calls=%async_computation.23 | async-start | bytes 6488064 | tf_op jit(solution)/shard_map/reduce_scatter | solution.py:353
  791.6 398.6 %reduce-scatter.14.cloned.1.call-start = ((), (), s32[]{:S(2)}) async-start(), calls=%async_computation.17 | async-start | bytes 147456 | tf_op jit(solution)/shard_map/reduce_scatter | solution.py:345
  794.6 435.3 %reduce-scatter.12.cloned.1.call-start = ((), (), s32[]{:S(2)}) async-start(), calls=%async_computation.16 | async-start | bytes 1179648 | tf_op jit(solution)/shard_map/reduce_scatter | solution.py:344
  797.6 477.4 %reduce-scatter.16.cloned.1.call-start = ((), (), s32[]{:S(2)}) async-start(), calls=%async_computation.18 | async-start | bytes 2359296 | tf_op jit(solution)/shard_map/reduce_scatter | solution.py:347
  800.7 529.8 %reduce-scatter.18.cloned.1.call-start = ((), (), s32[]{:S(2)}) async-start(), calls=%async_computation.19 | async-start | bytes 4718592 | tf_op jit(solution)/shard_map/reduce_scatter | solution.py:348
  805.1 591.1 %reduce-scatter.10.cloned.1.call-start = ((), (), s32[]{:S(2)}) async-start(), calls=%async_computation.15 | async-start | bytes 7077888 | tf_op jit(solution)/shard_map/reduce_scatter | solution.py:343
  849.8 118.3 %copy-start.54 = (f32[2048]{0:T(1024)S(1)}, f32[2048]{0:T(1024)}, u32[]{:S(2)}) copy-start(f32[2048]{0:T(1024)} %get-tuple-element.19) | copy-start | bytes 24580
  (63 other events, 447.0 us)
Sparse Core Ops, SparseCore 0:
  54.5 86.8 all-reduce.10
  605.4 86.9 all-reduce.12
  734.3 36.4 all-reduce.16
  773.7 32.9 reduce-scatter.19
  809.1 155.3 all-reduce.14
  968.4 58.0 reduce-scatter.21
  1030.9 58.9 reduce-scatter.23
  1093.9 59.0 reduce-scatter.25
  1156.9 33.3 reduce-scatter.13
  1193.8 36.0 reduce-scatter.11
  1233.7 41.1 reduce-scatter.15
  1279.1 51.2 reduce-scatter.17
  1334.4 61.7 reduce-scatter.9
where the time goes:
time: 1420 us; the launch traced here: 1400 us
  waiting for transfers between devices  815 us (57%)
  matrix products  202 us (14%)
  local copies, waits for them, and re-layouts  190 us (13%)
  other arithmetic  87.2 us (6%)
  blocking collectives  71.5 us (5%)
  starting transfers between devices  21.7 us (2%)
  between operations  16.6 us (1%)
    psum x1, waiting for transfers between devices, on_device(): ffn_sum = lax.psum(routed_sum + shared_out, 'tensor')  113 us
    all_to_all x1, waiting for transfers between devices, expert_backward(): lax.all_to_all(row_grads, 'dp', split_axis=1, concat_axis=1, tiled=True)  74.5 us
    all_to_all x1, waiting for transfers between devices, on_device(): lax.all_to_all(grad_rows, 'dp', split_axis=1, concat_axis=1, tiled=True)  71.5 us
    psum x1, waiting for transfers between devices, on_device(): lax.psum(jnp.dot(attended, o_weight, preferred_element_type=jnp.float32),...  67.4 us
    reduce_scatter x1, waiting for transfers between devices, on_device(): lax.psum_scatter(q_weight_grad, 'dp', scatter_dimension=0, tiled=True)  65.7 us
    reduce_scatter x1, waiting for transfers between devices, on_device(): lax.psum_scatter(shared_up_grad, 'dp', scatter_dimension=0, tiled=True)  63.4 us
    reduce_scatter x1, waiting for transfers between devices, on_device(): lax.psum_scatter(shared_down_grad, 'dp', scatter_dimension=1, tiled=True)  63.1 us
    reduce_scatter x1, waiting for transfers between devices, on_device(): lax.psum_scatter(o_weight_grad, 'dp', scatter_dimension=1, tiled=True)  55.5 us
  transfers between devices with their start and end apart: 17, of which 15 were waited for; matrix products, arithmetic and copies ran while one was open for 24% of the time, Pallas kernels for 0%

commit v1 on v0

v1 whole, which is shorter than its diff:
```python
import functools

import jax
import jax.numpy as jnp
from jax import lax
from jax.experimental import pallas as pl
from jax.experimental.pallas import tpu as pltpu
from jax.sharding import PartitionSpec as P

HD = 128
RD = 64
VD = 128
TOPK = 6
SEQ = 256
CAP = 64
LANES = 128
EPSILON = 1e-06
MIB = 1 << 20

bf16 = jnp.bfloat16
f32 = jnp.float32


def dot(a, b):
    return lax.dot_general(a, b, (((1,), (0,)), ((), ())), preferred_element_type=f32)


def dot_nt(a, b):
    return lax.dot_general(a, b, (((1,), (1,)), ((), ())), preferred_element_type=f32)


def dot_tn(a, b):
    return lax.dot_general(a, b, (((0,), (0,)), ((), ())), preferred_element_type=f32)


def rope_tables(length, width):
    half_width = width // 2
    frequency = 10000.0 ** (-jnp.arange(half_width, dtype=f32) * (2.0 / width))
    angles = jnp.arange(length, dtype=f32)[:, None] * frequency[None, :]
    return (jnp.cos(angles), jnp.sin(angles))


def rotate(vector, cosine, sine_tab):
    half_width = vector.shape[-1] // 2
    lower_half = vector[..., :half_width]
    upper_half = vector[..., half_width:]
    return jnp.concatenate(
        [lower_half * cosine - upper_half * sine_tab, upper_half * cosine + lower_half * sine_tab],
        axis=-1,
    )


def unrotate(vector, cosine, sine_tab):
    return rotate(vector, cosine, -sine_tab)


def rms_norm(values, gains):
    inv_rms = lax.rsqrt(jnp.mean(values * values, axis=-1, keepdims=True) + EPSILON)
    return (values * inv_rms * gains, inv_rms)


def rms_back(cotan, values, inv_rms, gains):
    weighted = cotan * gains
    inner_mean = jnp.mean(weighted * values, axis=-1, keepdims=True)
    value_grad = inv_rms * weighted - values * (inv_rms * inv_rms * inv_rms) * inner_mean
    gain_grad = jnp.sum(cotan * values * inv_rms, axis=0)
    return (value_grad, gain_grad)


def causal_scores(query_rot, key_full, factor):
    scores = (
        jnp.einsum("nqhd,nkhd->nhqk", query_rot, key_full, preferred_element_type=f32) * factor
    )
    length = query_rot.shape[1]
    causal = jnp.arange(length)[:, None] >= jnp.arange(length)[None, :]
    return jnp.where(causal, scores, -1e30)


def swap(array, axis, bits):
    count = lax.axis_size(axis)
    return lax.ppermute(array, axis, [(i, i ^ bits) for i in range(count)])


def block_at(array, index, size, dim):
    return lax.dynamic_slice_in_dim(array, index * size, size, dim)


def by_partner(array, axis, dim):
    count = lax.axis_size(axis)
    own = lax.axis_index(axis)
    size = array.shape[dim] // count
    return [block_at(array, own ^ r, size, dim) for r in range(count)]


def reorder(array, axis, dim):
    return jnp.concatenate(by_partner(array, axis, dim), axis=dim)


def share(array, axis):
    return [array] + [swap(array, axis, r) for r in range(1, lax.axis_size(axis))]


def share_dp(array):
    count = lax.axis_size("dp")
    same_core = [array] + [swap(array, "dp", r) for r in range(2, count, 2)]
    other_core = [swap(block, "dp", 1) for block in same_core]
    return [block for pair in zip(same_core, other_core) for block in pair]


def trade(blocks, axis):
    return [blocks[0]] + [swap(blocks[r], axis, r) for r in range(1, len(blocks))]


def total(blocks):
    return functools.reduce(jnp.add, [block.astype(f32) for block in blocks])


def pick_matrix(slots):
    toks = slots.shape[1]
    place = lax.broadcasted_iota(jnp.int32, (CAP, toks), 0)
    return jnp.concatenate(
        [
            jnp.where(place == slots[e : e + 1, :], 1.0, 0.0).astype(bf16)
            for e in range(slots.shape[0])
        ],
        axis=0,
    )


def fetch(refs, buffer, sems):
    step = pl.program_id(0)

    @pl.when(step == 0)
    def _():
        for i, ref in enumerate(refs):
            pltpu.make_async_copy(ref, buffer.at[i], sems.at[i]).start()

    pltpu.make_async_copy(refs[0], buffer.at[step], sems.at[step]).wait()
    return buffer.at[step]


def pick_grad_kernel(count, slots_ref, down_ref, *refs):
    rows_ref, dact_ref, buffer, sems = refs[count:]
    block = fetch(refs[:count], buffer, sems)
    slots = slots_ref[0]
    picked = dot(pick_matrix(slots), block[...]).astype(bf16)
    for e in range(slots.shape[0]):
        rows_ref[e] = picked[e * CAP : (e + 1) * CAP]
    dact_ref[...] = dot_nt(block[...], down_ref[...])


def pick_kernel(count, experts_all, slots_ref, router_ref, weights_ref, dact_ref, *refs):
    rows_ref, gate_ref, act_ref, delta_ref, buffer, sems = refs[count:]
    block = fetch(refs[:count], buffer, sems)
    slots = slots_ref[0]
    experts = slots.shape[0]
    picks = pick_matrix(slots)
    picked = dot(picks, block[...]).astype(bf16)
    for e in range(experts):
        rows_ref[e] = picked[e * CAP : (e + 1) * CAP]
    parts = dot_nt(router_ref[...], block[...])
    logits = parts[:experts_all] + parts[experts_all : 2 * experts_all] + parts[2 * experts_all :]
    spread = jnp.exp(logits - jnp.max(logits, axis=0, keepdims=True))
    prob = spread / jnp.sum(spread, axis=0, keepdims=True)
    for e in range(experts):
        chosen = picks[e * CAP : (e + 1) * CAP].astype(f32) * prob[e : e + 1, :]
        gate_ref[e] = jnp.broadcast_to(jnp.sum(chosen, axis=1, keepdims=True), (CAP, LANES))
    hidden = dot(block[...], weights_ref[...])
    width = hidden.shape[1] // 2
    act, gate_delta, up_delta = gated(hidden[:, :width], hidden[:, width:], dact_ref[...])
    act_ref[...] = act.astype(bf16)
    delta_ref[:, :width] = gate_delta.astype(bf16)
    delta_ref[:, width:] = up_delta.astype(bf16)


def gated(gate_h, up_h, dact):
    sigmoid_h = jax.nn.sigmoid(gate_h)
    silu_h = gate_h * sigmoid_h
    gate_delta = dact * up_h * sigmoid_h * (1.0 + gate_h * (1.0 - sigmoid_h))
    return silu_h * up_h, gate_delta, dact * silu_h


def hidden_kernel(
    first_ref,
    rows_ref,
    grads_ref,
    gate_ref,
    expert_gate_ref,
    expert_up_ref,
    expert_down_ref,
    act_ref,
    gate_delta_ref,
    up_delta_ref,
    score_ref,
):
    rows = rows_ref[0]
    gate_h = dot(rows, expert_gate_ref[0])
    up_h = dot(rows, expert_up_ref[0])
    dact = dot_nt(grads_ref[0], expert_down_ref[0])
    gate = gate_ref[0][:, :1]
    act, gate_delta, up_delta = gated(gate_h, up_h, dact)
    act_ref[0] = (act * gate).astype(bf16)
    gate_delta_ref[0] = (gate_delta * gate).astype(bf16)
    up_delta_ref[0] = (up_delta * gate).astype(bf16)
    score = jnp.sum(act * dact, axis=1, keepdims=True)
    high = score.astype(bf16).astype(f32)
    lanes = score_ref.shape[2]
    lane = lax.broadcasted_iota(jnp.int32, (rows.shape[0], lanes), 1)
    mine = first_ref[0] + pl.program_id(0)
    score_ref[0] = jnp.where(
        lane == mine, high, jnp.where(lane == mine + lanes // 2, score - high, 0.0)
    ).astype(bf16)


def return_kernel(spec, slots_ref, *refs):
    transposed, pairs, added, split = spec
    deltas, weights = refs[:pairs], refs[pairs : 2 * pairs]
    shared_ref, shared_weight_ref = refs[2 * pairs : 2 * pairs + 2]
    rest = refs[2 * pairs + 2 :]
    other_ref = rest[0] if added else None
    rest = rest[1:] if added else rest
    outs, picks, rows = rest[:-2], rest[-2], rest[-1]
    sources, slot_rows, _ = rows.shape
    experts = slot_rows // CAP
    toks = picks.shape[2]
    product = dot_nt if transposed else dot

    @pl.when(pl.program_id(0) == 0)
    def _():
        for s in range(sources):
            picks[s] = pick_matrix(slots_ref[s])

    for e in range(experts):
        back = functools.reduce(
            jnp.add, [product(d[e], w[e]) for d, w in zip(deltas, weights)]
        ).astype(bf16)
        for s in range(sources):
            rows[s, e * CAP : (e + 1) * CAP, :] = back[s * CAP : (s + 1) * CAP]
    for s in range(sources):
        summed = dot_tn(picks[s], rows[s]) + product(
            shared_ref[s * toks : (s + 1) * toks], shared_weight_ref[...]
        )
        if added:
            summed = summed + other_ref[s].astype(f32)
        if split:
            outs[s][...] = summed.astype(bf16)
        else:
            outs[0][s] = summed.astype(bf16)


def score_kernel(slots_ref, score_ref, out_ref):
    for s in range(slots_ref.shape[0]):
        rows = jnp.concatenate(
            [score_ref[e, s * CAP : (s + 1) * CAP] for e in range(score_ref.shape[0])], axis=0
        )
        out_ref[s] = dot_tn(pick_matrix(slots_ref[s]), rows).astype(bf16)


def expert_grad_kernel(
    rows_ref,
    grads_ref,
    act_ref,
    gate_delta_ref,
    up_delta_ref,
    gate_grad_ref,
    up_grad_ref,
    down_grad_ref,
):
    rows = rows_ref[0]
    gate_grad_ref[0] = dot_tn(rows, gate_delta_ref[0])
    up_grad_ref[0] = dot_tn(rows, up_delta_ref[0])
    down_grad_ref[0] = dot_tn(act_ref[0], grads_ref[0])


def shared_grad_kernel(count, delta_ref, act_ref, *refs):
    rows, grads = refs[:count], refs[count : 2 * count]
    in_ref, down_ref, row_buf, grad_buf, in_acc, down_acc, row_sems, grad_sems = refs[2 * count :]
    step = pl.program_id(0)
    row = fetch(rows, row_buf, row_sems)
    grad = fetch(grads, grad_buf, grad_sems)

    @pl.when(step == 0)
    def _():
        in_acc[...] = jnp.zeros_like(in_acc)
        down_acc[...] = jnp.zeros_like(down_acc)

    in_acc[...] += dot_tn(row[...], delta_ref[...])
    down_acc[...] += dot_tn(act_ref[...], grad[...])

    @pl.when(step == count - 1)
    def _():
        in_ref[...] = in_acc[...].astype(bf16)
        down_ref[...] = down_acc[...].astype(bf16)


ANYWHERE = pl.BlockSpec(memory_space=pl.ANY)


def whole(array):
    rank = len(array.shape)
    return pl.BlockSpec(array.shape, lambda *_: (0,) * rank)


def params(mib):
    return pltpu.CompilerParams(vmem_limit_bytes=mib * MIB)


def cost(flops, bytes_accessed, transcendentals=0):
    return pl.CostEstimate(
        flops=int(flops), bytes_accessed=int(bytes_accessed), transcendentals=int(transcendentals)
    )


def pick_grads(blocks, slots, shared_down):
    count = len(blocks)
    toks, width = blocks[0].shape
    experts = slots.shape[1]
    shared = shared_down.shape[0]
    return pl.pallas_call(
        functools.partial(pick_grad_kernel, count),
        grid=(count,),
        in_specs=[pl.BlockSpec((1, experts, toks), lambda s: (s, 0, 0)), whole(shared_down)]
        + [ANYWHERE] * count,
        out_specs=[
            pl.BlockSpec((experts, CAP, width), lambda s: (0, s, 0)),
            pl.BlockSpec((toks, shared), lambda s: (s, 0)),
        ],
        out_shape=[
            jax.ShapeDtypeStruct((experts, count * CAP, width), bf16),
            jax.ShapeDtypeStruct((count * toks, shared), f32),
        ],
        scratch_shapes=[
            pltpu.VMEM((count, toks, width), bf16),
            pltpu.SemaphoreType.DMA((count,)),
        ],
        compiler_params=params(48),
        cost_estimate=cost(
            2 * count * toks * width * (experts * CAP + shared), 4 * count * toks * width
        ),
    )(slots, shared_down, *blocks)


def pick_rows(blocks, slots, router, weights, dact, experts_all):
    count = len(blocks)
    toks, width = blocks[0].shape
    experts = slots.shape[1]
    shared = dact.shape[1]
    return pl.pallas_call(
        functools.partial(pick_kernel, count, experts_all),
        grid=(count,),
        in_specs=[
            pl.BlockSpec((1, experts, toks), lambda s: (s, 0, 0)),
            whole(router),
            whole(weights),
            pl.BlockSpec((toks, shared), lambda s: (s, 0)),
        ]
        + [ANYWHERE] * count,
        out_specs=[
            pl.BlockSpec((experts, CAP, width), lambda s: (0, s, 0)),
            pl.BlockSpec((experts, CAP, LANES), lambda s: (0, s, 0)),
            pl.BlockSpec((toks, shared), lambda s: (s, 0)),
            pl.BlockSpec((toks, 2 * shared), lambda s: (s, 0)),
        ],
        out_shape=[
            jax.ShapeDtypeStruct((experts, count * CAP, width), bf16),
            jax.ShapeDtypeStruct((experts, count * CAP, LANES), f32),
            jax.ShapeDtypeStruct((count * toks, shared), bf16),
            jax.ShapeDtypeStruct((count * toks, 2 * shared), bf16),
        ],
        scratch_shapes=[
            pltpu.VMEM((count, toks, width), bf16),
            pltpu.SemaphoreType.DMA((count,)),
        ],
        compiler_params=params(48),
        cost_estimate=cost(
            2 * count * toks * width * (experts * CAP + router.shape[0] + 2 * shared),
            4 * count * toks * width,
        ),
    )(slots, router, weights, dact, *blocks)


def expert_hidden(first, rows, grads, gate, expert_gate, expert_up, expert_down, lanes):
    experts, slot_rows, width = rows.shape
    hidden = expert_gate.shape[2]

    def per_expert(array):
        return pl.BlockSpec((1,) + array.shape[1:], lambda e: (e, 0, 0))

    narrow = jax.ShapeDtypeStruct((experts, slot_rows, hidden), bf16)
    score = jax.ShapeDtypeStruct((experts, slot_rows, lanes), bf16)
    return pl.pallas_call(
        hidden_kernel,
        grid=(experts,),
        in_specs=[pl.BlockSpec(memory_space=pltpu.SMEM)]
        + [per_expert(a) for a in (rows, grads, gate, expert_gate, expert_up, expert_down)],
        out_specs=[per_expert(narrow)] * 3 + [per_expert(score)],
        out_shape=[narrow] * 3 + [score],
        compiler_params=params(56),
        cost_estimate=cost(
            6 * experts * slot_rows * width * hidden,
            experts * (4 * slot_rows * width + 6 * hidden * width),
            experts * slot_rows * hidden,
        ),
    )(first, rows, grads, gate, expert_gate, expert_up, expert_down)


def return_rows(half, slots, deltas, weights, shared, shared_weight, transposed, start, size, other):
    experts, slot_rows, hidden = deltas[0].shape
    sources = slots.shape[0] // 2
    toks = slots.shape[2]
    chunk = min(512, size)
    steps = size // chunk
    first = start // chunk
    split = half == 1
    if transposed:
        weight_spec = pl.BlockSpec((experts, chunk, hidden), lambda n: (0, n + first, 0))
        shared_spec = pl.BlockSpec((chunk, shared.shape[1]), lambda n: (n + first, 0))
    else:
        weight_spec = pl.BlockSpec((experts, hidden, chunk), lambda n: (0, 0, n + first))
        shared_spec = pl.BlockSpec((shared.shape[1], chunk), lambda n: (0, n + first))
    many = pl.BlockSpec((sources, toks, chunk), lambda n: (0, 0, n))
    in_specs = (
        [pl.BlockSpec((sources,) + slots.shape[1:], lambda n: (half, 0, 0))]
        + [pl.BlockSpec((experts, slot_rows // 2, hidden), lambda n: (0, half, 0))] * len(deltas)
        + [weight_spec] * len(weights)
        + [pl.BlockSpec((sources * toks, shared.shape[1]), lambda n: (half, 0)), shared_spec]
    )
    operands = [slots, *deltas, *weights, shared, shared_weight]
    if other is not None:
        in_specs.append(many)
        operands.append(other)
    if split:
        out_specs = [pl.BlockSpec((toks, chunk), lambda n: (0, n))] * sources
        out_shape = [jax.ShapeDtypeStruct((toks, size), bf16)] * sources
    else:
        out_specs, out_shape = [many], [jax.ShapeDtypeStruct((sources, toks, size), bf16)]
    return pl.pallas_call(
        functools.partial(
            return_kernel, (transposed, len(deltas), other is not None, split)
        ),
        grid=(steps,),
        in_specs=in_specs,
        out_specs=out_specs,
        out_shape=out_shape,
        scratch_shapes=[
            pltpu.VMEM((sources, experts * CAP, toks), bf16),
            pltpu.VMEM((sources, experts * CAP, chunk), bf16),
        ],
        compiler_params=params(48),
        cost_estimate=cost(
            2 * experts * slot_rows // 2 * size * (hidden * len(deltas) + toks)
            + 2 * sources * toks * size * shared.shape[1],
            2 * size * (experts * hidden * len(deltas) + sources * toks),
        ),
    )(*operands)


def return_scores(slots, score):
    sources, _, toks = slots.shape
    out = jax.ShapeDtypeStruct((sources, toks, score.shape[2]), bf16)
    return pl.pallas_call(
        score_kernel,
        grid=(1,),
        in_specs=[whole(slots), whole(score)],
        out_specs=whole(out),
        out_shape=out,
        compiler_params=params(32),
    )(slots, score)


def expert_grads(rows, grads, act, gate_delta, up_delta):
    experts, slot_rows, width = rows.shape
    hidden = act.shape[2]

    def per_expert(array):
        return pl.BlockSpec((1,) + array.shape[1:], lambda e: (e, 0, 0))

    outs = [
        jax.ShapeDtypeStruct((experts, width, hidden), f32),
        jax.ShapeDtypeStruct((experts, width, hidden), f32),
        jax.ShapeDtypeStruct((experts, hidden, width), f32),
    ]
    return pl.pallas_call(
        expert_grad_kernel,
        grid=(experts,),
        in_specs=[per_expert(a) for a in (rows, grads, act, gate_delta, up_delta)],
        out_specs=[per_expert(o) for o in outs],
        out_shape=outs,
        compiler_params=params(56),
        cost_estimate=cost(
            6 * experts * slot_rows * width * hidden,
            experts * (4 * slot_rows * width + 12 * hidden * width),
        ),
    )(rows, grads, act, gate_delta, up_delta)


def shared_grads(blocks, grads, delta, act):
    count = len(blocks)
    toks, width = blocks[0].shape
    outs = [
        jax.ShapeDtypeStruct((width, delta.shape[1]), bf16),
        jax.ShapeDtypeStruct((act.shape[1], width), bf16),
    ]
    return pl.pallas_call(
        functools.partial(shared_grad_kernel, count),
        grid=(count,),
        in_specs=[
            pl.BlockSpec((toks, delta.shape[1]), lambda s: (s, 0)),
            pl.BlockSpec((toks, act.shape[1]), lambda s: (s, 0)),
        ]
        + [ANYWHERE] * (2 * count),
        out_specs=[whole(o) for o in outs],
        out_shape=outs,
        scratch_shapes=[
            pltpu.VMEM((count, toks, width), bf16),
            pltpu.VMEM((count, toks, width), bf16),
            pltpu.VMEM(outs[0].shape, f32),
            pltpu.VMEM(outs[1].shape, f32),
            pltpu.SemaphoreType.DMA((count,)),
            pltpu.SemaphoreType.DMA((count,)),
        ],
        compiler_params=params(56),
        cost_estimate=cost(
            2 * count * toks * width * (delta.shape[1] + act.shape[1]), 4 * count * toks * width
        ),
    )(delta, act, *blocks, *grads)


def on_device(
    tokens,
    cotangent,
    attn_gain,
    q_weight,
    kv_down,
    k_rope_weight,
    kv_gain,
    kv_up,
    o_weight,
    ffn_gain,
    router_weight,
    expert_ids,
    expert_gate,
    expert_up,
    expert_down,
    shared_gate,
    shared_up,
    shared_down,
):
    n_t = lax.axis_size("tensor")
    n_d = lax.axis_size("dp")
    t_index = lax.axis_index("tensor")
    d_index = lax.axis_index("dp")
    toks, width = tokens.shape
    own_toks = toks // n_t
    heads = q_weight.shape[1] // (HD + RD)
    experts_all = router_weight.shape[1]
    experts = expert_gate.shape[0]
    factor = (HD + RD) ** (-0.5)
    cosine, sine_tab = rope_tables(SEQ, RD)
    head_cos = cosine[:, None, :]
    head_sin = sine_tab[:, None, :]
    order = [r for r in range(n_d) if r % 2 == 1] + [r for r in range(n_d) if r % 2 == 0]
    lat_cols = kv_down.shape[1]
    rope_cols = k_rope_weight.shape[1]

    tokens_p = by_partner(tokens, "tensor", 0)
    tokens_own = tokens_p[0].astype(f32)
    cot_p = by_partner(cotangent, "tensor", 0)
    cot_own = cot_p[0].astype(f32)
    cot_blocks = share_dp(jnp.concatenate(cot_p, axis=0))
    ids = reorder(expert_ids, "tensor", 0)
    every = jnp.arange(experts_all, dtype=jnp.int32)
    member = jnp.any(ids.T[:, None, :] == every[None, :, None], axis=0)
    before = (jnp.arange(toks)[:, None] < jnp.arange(toks)[None, :]).astype(bf16)
    rank = dot(member.astype(bf16), before)
    slots_own = jnp.where(member, rank, -1.0).astype(bf16)
    slot_blocks = [block_at(s, d_index, experts, 0) for s in share_dp(slots_own)]
    slots = jnp.stack([slot_blocks[r] for r in order]).astype(jnp.int32)
    router_t = jnp.roll(router_weight.T, -d_index * experts, axis=0)
    router_parts = []
    rest = router_t
    for _ in range(3):
        part = lax.reduce_precision(rest, 8, 7)
        router_parts.append(part.astype(bf16))
        rest = rest - part
    router_parts = jnp.concatenate(router_parts, axis=0)
    shared_cols = shared_gate.shape[1] // n_d
    shared_pad = -(-shared_cols // LANES) * LANES - shared_cols
    shared_in = jnp.concatenate(
        [
            jnp.pad(block_at(w, d_index, shared_cols, 1), ((0, 0), (0, shared_pad)))
            for w in (shared_gate, shared_up)
        ],
        axis=1,
    )
    shared_out = jnp.pad(
        block_at(shared_down, d_index, shared_cols, 0), ((0, shared_pad), (0, 0))
    )
    grad_rows, shared_dact = pick_grads([cot_blocks[r] for r in order], slots, shared_out)

    tokens_f = tokens.astype(f32)
    normed_f, inv_first = rms_norm(tokens_f, attn_gain)
    normed = normed_f.astype(bf16)
    query_raw = dot(normed, q_weight).reshape(1, toks, heads, HD + RD)
    query_rot = jnp.concatenate(
        [query_raw[..., :HD], rotate(query_raw[..., HD:], head_cos, head_sin)], axis=-1
    ).astype(bf16)
    down_weight = jnp.concatenate([kv_down, k_rope_weight], axis=1)
    lat_blocks = reorder(
        jnp.stack(share(dot(normed, down_weight).astype(bf16), "tensor")), "tensor", 0
    )
    latent = jnp.concatenate([lat_blocks[j, :, :lat_cols] for j in range(n_t)], axis=1)
    rope_key = jnp.concatenate([lat_blocks[j, :, lat_cols:] for j in range(n_t)], axis=1)
    latent_f = latent.astype(f32)
    latent_normed_f, inv_latent = rms_norm(latent_f, kv_gain)
    latent_normed = latent_normed_f.astype(bf16)
    key_value = dot(latent_normed, kv_up).astype(bf16).reshape(1, toks, heads, HD + VD)
    rope_rot = rotate(rope_key.astype(f32), cosine, sine_tab).astype(bf16)
    key_full = jnp.concatenate(
        [
            key_value[..., :HD],
            jnp.broadcast_to(rope_rot[None, :, None, :], (1, toks, heads, RD)),
        ],
        axis=-1,
    )
    values = key_value[..., HD:]
    scores = causal_scores(query_rot, key_full, factor)
    top_score = jnp.max(scores, axis=-1, keepdims=True)
    log_total = top_score + jnp.log(jnp.sum(jnp.exp(scores - top_score), axis=-1, keepdims=True))
    weights = jnp.exp(scores - log_total).astype(bf16)
    attended = (
        jnp.einsum("nhqk,nkhd->nqhd", weights, values, preferred_element_type=f32)
        .astype(bf16)
        .reshape(toks, heads * VD)
    )
    attended_p = reorder(attended, "tensor", 0)
    attn_part = dot(attended_p, o_weight).reshape(n_t, own_toks, width)
    attn_sum = attn_part[0] + total(
        trade([attn_part[r].astype(bf16) for r in range(n_t)], "tensor")[1:]
    )
    hidden_one = tokens_own + attn_sum
    ffn_normed_f, inv_second = rms_norm(hidden_one, ffn_gain)
    ffn_own = ffn_normed_f.astype(bf16)
    blocks = share_dp(jnp.concatenate(share(ffn_own, "tensor"), axis=0))
    blocks_o = [blocks[r] for r in order]

    rows, gate, shared_act, shared_delta = pick_rows(
        blocks_o, slots, router_parts, shared_in, shared_dact, experts_all
    )
    lanes = -(-2 * experts_all // LANES) * LANES
    first = (d_index * experts).astype(jnp.int32).reshape(1)
    act, gate_delta, up_delta, score = expert_hidden(
        first, rows, grad_rows, gate, expert_gate, expert_up, expert_down, lanes
    )

    def sum_over(deltas, weights_, shared, shared_weight, transposed, start, size):
        other = return_rows(
            0, slots, deltas, weights_, shared, shared_weight, transposed, start, size, None
        )[0]
        other = swap(other, "dp", 1)
        mine = return_rows(
            1, slots, deltas, weights_, shared, shared_weight, transposed, start, size, other
        )
        return sum_blocks(mine)

    def sum_blocks(mine):
        arrived = [mine[0]] + [swap(mine[i], "dp", 2 * i) for i in range(1, len(mine))]
        parts = [
            total([a[k * own_toks : (k + 1) * own_toks] for a in arrived]).astype(bf16)
            for k in range(n_t)
        ]
        return total(trade(parts, "tensor"))

    score_sums = return_scores(slots, score)
    half = n_d // 2
    score_other = swap(score_sums[:half], "dp", 1)
    score_sum = sum_blocks(
        [(score_sums[half + i].astype(f32) + score_other[i].astype(f32)).astype(bf16) for i in range(half)]
    )
    pieces = 2
    size = width // pieces
    back_sum = jnp.concatenate(
        [
            sum_over(
                [gate_delta, up_delta],
                [expert_gate, expert_up],
                shared_delta,
                shared_in,
                True,
                i * size,
                size,
            )
            for i in range(pieces)
        ],
        axis=1,
    )
    out_sum = sum_over([act], [expert_down], shared_act, shared_out, False, 0, width)
    expert_gate_grad, expert_up_grad, expert_down_grad = expert_grads(
        rows, grad_rows, act, gate_delta, up_delta
    )
    shared_in_grad, shared_out_grad = shared_grads(
        blocks_o, [cot_blocks[r] for r in order], shared_delta, shared_act
    )
    output_own = (hidden_one + out_sum).astype(bf16)
    output = reorder(jnp.concatenate(share(output_own, "tensor"), axis=0), "tensor", 0)

    pad_cols = shared_cols + shared_pad
    in_blocks = lax.all_to_all(
        jnp.concatenate(
            [shared_in_grad[:, :shared_cols], shared_in_grad[:, pad_cols : pad_cols + shared_cols]],
            axis=1,
        ).reshape(n_d, width // n_d, 2 * shared_cols),
        "dp",
        0,
        0,
        tiled=True,
    )
    in_blocks = in_blocks.transpose(1, 0, 2).astype(f32)
    rows_d = width // n_d
    shared_gate_grad = in_blocks[:, :, :shared_cols].reshape(rows_d, n_d * shared_cols)
    shared_up_grad = in_blocks[:, :, shared_cols:].reshape(rows_d, n_d * shared_cols)
    shared_down_grad = (
        lax.all_to_all(
            shared_out_grad[:shared_cols].reshape(shared_cols, n_d, rows_d).transpose(1, 0, 2),
            "dp",
            0,
            0,
            tiled=True,
        )
        .reshape(n_d * shared_cols, rows_d)
        .astype(f32)
    )

    logits = jnp.dot(ffn_own.astype(f32), router_weight, precision=lax.Precision.HIGHEST)
    router_prob = jax.nn.softmax(logits, axis=-1)
    prob_grad = score_sum[:, :experts_all] + score_sum[:, lanes // 2 : lanes // 2 + experts_all]
    logit_grad = (
        router_prob * (prob_grad - jnp.sum(router_prob * prob_grad, axis=-1, keepdims=True))
    ).astype(bf16)
    ffn_normed_grad = back_sum + jnp.dot(
        logit_grad.astype(f32), router_weight.T, precision=lax.Precision.HIGHEST
    )
    hidden_norm_grad, ffn_gain_part = rms_back(ffn_normed_grad, hidden_one, inv_second, ffn_gain)
    hidden_grad = cot_own + hidden_norm_grad
    hidden_grad_p = jnp.concatenate(share(hidden_grad.astype(bf16), "tensor"), axis=0)
    logit_blocks = share_dp(jnp.concatenate(share(logit_grad, "tensor"), axis=0))
    device = d_index * n_t + t_index
    own_rows = width // (n_d * n_t)
    router_grad = dot_tn(
        jnp.concatenate([block_at(b, device, own_rows, 1) for b in blocks], axis=0),
        jnp.concatenate(logit_blocks, axis=0),
    )

    attended_grad = (
        reorder(dot_nt(hidden_grad_p, o_weight).astype(bf16), "tensor", 0).reshape(1, toks, heads, VD)
    )
    o_weight_grad = dot_tn(
        jnp.concatenate(share_dp(attended_p), axis=0),
        jnp.concatenate(trade(by_partner(hidden_grad_p, "dp", 1), "dp"), axis=0),
    )
    attn_probs = jnp.exp(causal_scores(query_rot, key_full, factor) - log_total)
    value_grad = jnp.einsum(
        "nhqk,nqhd->nkhd", attn_probs.astype(bf16), attended_grad, preferred_element_type=f32
    )
    prob_dot = jnp.einsum("nqhd,nkhd->nhqk", attended_grad, values, preferred_element_type=f32)
    score_grad = (
        attn_probs * (prob_dot - jnp.sum(attn_probs * prob_dot, axis=-1, keepdims=True)) * factor
    ).astype(bf16)
    query_grad = jnp.einsum("nhqk,nkhd->nqhd", score_grad, key_full, preferred_element_type=f32)
    key_grad = jnp.einsum("nhqk,nqhd->nkhd", score_grad, query_rot, preferred_element_type=f32)
    query_grad_b = (
        jnp.concatenate(
            [query_grad[..., :HD], unrotate(query_grad[..., HD:], head_cos, head_sin)], axis=-1
        )
        .astype(bf16)
        .reshape(toks, heads * (HD + RD))
    )
    kv_grad = (
        jnp.concatenate([key_grad[..., :HD], value_grad], axis=-1)
        .astype(bf16)
        .reshape(toks, heads * (HD + VD))
    )
    rope_part = unrotate(jnp.sum(key_grad[0, ..., HD:], axis=1), cosine, sine_tab)
    latent_part, kv_gain_part = rms_back(dot_nt(kv_grad, kv_up), latent_f, inv_latent, kv_gain)
    latent_trade = [
        jnp.concatenate(pair, axis=1)
        for pair in zip(by_partner(latent_part, "tensor", 1), by_partner(rope_part, "tensor", 1))
    ]
    latent_mine = latent_trade[0] + total(
        trade([b.astype(bf16) for b in latent_trade], "tensor")[1:]
    )
    narrow_p = reorder(
        jnp.concatenate([query_grad_b, latent_mine.astype(bf16)], axis=1), "tensor", 0
    )
    weight_in = jnp.concatenate([q_weight, down_weight], axis=1)
    normed_part = dot_nt(narrow_p, weight_in)
    tokens_pf = jnp.concatenate(tokens_p, axis=0).astype(f32)
    inv_first_p = reorder(inv_first, "tensor", 0)
    attn_gain_part = jnp.sum(normed_part * tokens_pf * inv_first_p, axis=0)
    normed_blocks = normed_part.reshape(n_t, own_toks, width)
    normed_grad = normed_blocks[0] + total(
        trade([normed_blocks[r].astype(bf16) for r in range(n_t)], "tensor")[1:]
    )
    input_norm_grad, _ = rms_back(normed_grad, tokens_own, inv_first_p[:own_toks], attn_gain)
    input_grad = hidden_grad + input_norm_grad

    normed_cols = trade(by_partner(reorder(normed, "tensor", 0), "dp", 1), "dp")
    in_grad = dot_tn(
        jnp.concatenate(normed_cols, axis=0), jnp.concatenate(share_dp(narrow_p), axis=0)
    )
    q_cols = q_weight.shape[1]
    q_weight_grad = in_grad[:, :q_cols]
    kv_down_grad = in_grad[:, q_cols : q_cols + lat_cols]
    k_rope_grad = in_grad[:, q_cols + lat_cols :]
    kv_up_grad = total(
        trade([b.astype(bf16) for b in by_partner(dot_tn(latent_normed, kv_grad), "dp", 0)], "dp")
    )

    gains = jnp.concatenate(
        [
            part.reshape(n_d, n_t, -1)
            for part in (attn_gain_part, ffn_gain_part, kv_gain_part)
        ],
        axis=2,
    )
    gains = total([b[:, 0] for b in trade(by_partner(gains, "tensor", 1), "tensor")])
    gains = total([b[0] for b in trade(by_partner(gains, "dp", 0), "dp")])
    attn_gain_grad = gains[:own_rows]
    ffn_gain_grad = gains[own_rows : 2 * own_rows]
    kv_gain_grad = gains[2 * own_rows :]

    return (
        output,
        input_grad,
        attn_gain_grad,
        q_weight_grad,
        kv_down_grad,
        k_rope_grad,
        kv_gain_grad,
        kv_up_grad,
        o_weight_grad,
        ffn_gain_grad,
        router_grad,
        shared_gate_grad,
        shared_up_grad,
        shared_down_grad,
        expert_gate_grad,
        expert_up_grad,
        expert_down_grad,
    )


def solution(mesh):
    in_specs = (
        P("dp", None),
        P("dp", None),
        P(),
        P(None, "tensor"),
        P(None, "tensor"),
        P(None, "tensor"),
        P(),
        P(None, "tensor"),
        P("tensor", None),
        P(),
        P(),
        P("dp", None),
        P("dp", None, "tensor"),
        P("dp", None, "tensor"),
        P("dp", "tensor", None),
        P(None, "tensor"),
        P(None, "tensor"),
        P("tensor", None),
    )
    out_specs = (
        P("dp", None),
        P(("dp", "tensor"), None),
        P(("dp", "tensor")),
        P("dp", "tensor"),
        P("dp", "tensor"),
        P("dp", "tensor"),
        P(("dp", "tensor")),
        P("dp", "tensor"),
        P("tensor", "dp"),
        P(("dp", "tensor")),
        P(("dp", "tensor"), None),
        P("dp", "tensor"),
        P("dp", "tensor"),
        P("tensor", "dp"),
        P("dp", None, "tensor"),
        P("dp", None, "tensor"),
        P("dp", "tensor", None),
    )
    return jax.shard_map(
        on_device, mesh=mesh, in_specs=in_specs, out_specs=out_specs, check_vma=False
    )
```

time: 1420 us -> 690 us (0.49)
  waiting for transfers between devices: 815 us -> 220 us
  matrix products: 202 us -> 37.4 us
  Pallas kernels: 0 us -> 118 us
  starting transfers between devices: 21.7 us -> 137 us
  blocking collectives: 71.5 us -> 0 us
  local copies, waits for them, and re-layouts: 190 us -> 120 us
  other arithmetic: 87.2 us -> 42.7 us
    reduce_scatter x9 -> x0, waiting for transfers between devices: 397 us -> none  [the longest x1 65.7 us: on_device(): lax.psum_scatter(q_weight_grad, 'dp', scatter_dimension=0, tiled=True)]
    ppermute x0 -> x125, waiting for transfers between devices: none -> 220 us  [swap(): return lax.ppermute(array, axis, [(i, i ^ bits) for i in range(count)])]
    all_to_all x4 -> x2, waiting for transfers between devices: 214 us -> 0.01 us  [the longest x1 0.01 us: on_device(): lax.all_to_all(shared_out_grad[:shared_cols].reshape(shared_cols, n_d, ro...]
    psum x4 -> x0, waiting for transfers between devices: 203 us -> none  [the longest x1 113 us: on_device(): ffn_sum = lax.psum(routed_sum + shared_out, 'tensor')]
    dot_general x38 -> x16, matrix products: 192 us -> 28.5 us  [the longest x5 9.92 us: dot(): lax.dot_general(a, b, (((1,), (0,)), ((), ())), preferred_element_type=f32)]
    ppermute x0 -> x125, starting transfers between devices: none -> 129 us  [swap(): return lax.ppermute(array, axis, [(i, i ^ bits) for i in range(count)])]
    pallas_call x0 -> x12, Pallas kernels: none -> 118 us  [the longest x6 43.3 us: return_rows(): pl.pallas_call(functools.partial(return_kernel, (transposed, len(deltas),...]
    unnamed x142 -> x357, local copies, waits for them, and re-layouts: 9.66 us -> 80.8 us
  transfers between devices with their start and end apart: 17 -> 127, of which waited for: 15 -> 47; matrix products, arithmetic and copies ran while one was open for 24% -> 23% of each run, Pallas kernels for 0% -> 13%
where the time goes in v1:
time: 690 us; the launch traced here: 679 us
  waiting for transfers between devices  220 us (32%)
  starting transfers between devices  137 us (20%)
  local copies, waits for them, and re-layouts  120 us (17%)
  Pallas kernels  118 us (17%)
  other arithmetic  42.7 us (6%)
  matrix products  37.4 us (5%)
    ppermute x125, waiting for transfers between devices, swap(): return lax.ppermute(array, axis, [(i, i ^ bits) for i in range(count)])  220 us
    ppermute x125, starting transfers between devices, swap(): return lax.ppermute(array, axis, [(i, i ^ bits) for i in range(count)])  129 us
    unnamed x357, local copies, waits for them, and re-layouts  80.8 us
    pallas_call x6, Pallas kernels, return_rows(): pl.pallas_call(functools.partial(return_kernel, (transposed, len(deltas),...  43.3 us
    pallas_call x1, Pallas kernels, expert_grads(): pl.pallas_call(expert_grad_kernel, grid=(experts,), in_specs=[per_expert(...  21.2 us
    pallas_call x1, Pallas kernels, expert_hidden(): pl.pallas_call(hidden_kernel, grid=(experts,), in_specs=[pl.BlockSpec(mem...  20.6 us
  transfers between devices with their start and end apart: 127, of which 47 were waited for; matrix products, arithmetic and copies ran while one was open for 23% of the time, Pallas kernels for 13%

profile of v1, /device:TPU:0, one launch (start us, length us, event | category | flops | bytes accessed | tf_op | source)
XLA Modules:
  0.0 678.9 jit_solution(11664552631295212929)
XLA Ops:
  64.7 9.2 %collective-permute-done.4 = bf16[64,2048]{1,0:T(8,128)(2,1)} collective-permute-done((bf16[64,2048]{1,0:T(8,128)(2,1)}, bf16[64,2048]{1,0:T(8,128)(2,1)}, u32[]{:S(2)}, u32[]{:S(2)}) %collective-permute-start.4) | collective-permute-done | bytes 262176 | tf_op jit(solution)/shard_map/ppermute | solution.py:81
  106.1 12.9 %collective-permute-done.21 = bf16[64,2048]{1,0:T(8,128)(2,1)S(1)} collective-permute-done((bf16[64,2048]{1,0:T(8,128)(2,1)S(1)}, bf16[64,2048]{1,0:T(8,128)(2,1)S(1)}, u32[]{:S(2)}, u32[]{:S(2)}) %collective-permute-start.21) | collective-permute-done | bytes 262176 | tf_op jit(solution)/shard_map/ppermute | solution.py:81
  120.9 8.9 %copy.153.expert_gate_ref.refs_2_ = bf16[4,2048,352]{2,1,0:T(8,128)(2,1)} copy(bf16[4,2048,352]{1,2,0:T(8,128)(2,1)} %param.30) | data formatting | bytes 11534336 | tf_op args[12]
  129.8 8.5 %copy.154.expert_up_ref.refs_3_ = bf16[4,2048,352]{2,1,0:T(8,128)(2,1)} copy(bf16[4,2048,352]{1,2,0:T(8,128)(2,1)} %param.31) | data formatting | bytes 11534336 | tf_op args[13]
  150.7 18.7 %collective-permute-done.28.refs_7_ = bf16[256,2048]{1,0:T(8,128)(2,1)} collective-permute-done((bf16[256,2048]{1,0:T(8,128)(2,1)S(1)}, bf16[256,2048]{1,0:T(8,128)(2,1)}, u32[]{:S(2)}, u32[]{:S(2)}) %collective-permute-start.28) | collective-permute-done | bytes 1048608 | tf_op jit(solution)/shard_map/ppermute | solution.py:81
  169.4 21.6 %collective-permute-done.26.refs_6_ = bf16[256,2048]{1,0:T(8,128)(2,1)} collective-permute-done((bf16[256,2048]{1,0:T(8,128)(2,1)S(1)}, bf16[256,2048]{1,0:T(8,128)(2,1)}, u32[]{:S(2)}, u32[]{:S(2)}) %collective-permute-start.26) | collective-permute-done | bytes 1048608 | tf_op jit(solution)/shard_map/ppermute | solution.py:81
  204.3 8.8 %shard_map.305 = (bf16[4,512,2048]{2,1,0:T(8,128)(2,1)}, f32[2048,128]{1,0:T(8,128)S(1)}) custom-call(s32[8,4,256]{2,1,0:T(4,128)S(1)} %convert_element_type.580.slots_ref, bf16[128,2048]{1,0:T(8,128)(2,1)S(1)} %pad.13.down_ref.refs_3_, bf16[256,2048]{1,0:T(8,128)(2,1)} %collective-permute-done.13.refs_0_.refs_8_, ...), custom_call_target="tpu_custom_call" | custom-call | flops 3221225472 | bytes 16777216 | tf_op jit(solution)/shard_map/pallas_call | solution.py:319
  213.2 10.5 %shard_map.306 = (bf16[4,512,2048]{2,1,0:T(8,128)(2,1)}, f32[4,512,128]{2,1,0:T(8,128)S(1)}, bf16[2048,128]{1,0:T(8,128)(2,1)S(1)}, bf16[2048,256]{1,0:T(8,128)(2,1)S(1)}) custom-call(s32[8,4,256]{2,1,0:T(4,128)S(1)} %convert_element_type.580.slots_ref, bf16[96,2048]{1,0:T(8,128)(2,1)S(1)} %copy-done.20, bf16[2048,256]{1,0:T(8,128)(2,1)S(1)} %fusion.19.weights_ref.refs_5_, ...), custom_call_target="tpu_custom_call" | custom-call | flops 5100273664 | bytes 16777216 | tf_op jit(solution)/shard_map/pallas_call | solution.py:348
  224.7 20.6 %shard_map.307 = (bf16[4,512,352]{2,1,0:T(8,128)(2,1)}, bf16[4,512,352]{2,1,0:T(8,128)(2,1)}, bf16[4,512,352]{2,1,0:T(8,128)(2,1)}, bf16[4,512,128]{2,1,0:T(8,128)(2,1)}) custom-call(s32[1]{0:T(128)} %bitcast.32.first_ref, bf16[4,512,2048]{2,1,0:T(8,128)(2,1)} %get-tuple-element.45.rows_ref, bf16[4,512,2048]{2,1,0:T(8,128)(2,1)} %get-tuple-element.46.grads_ref, ...), custom_call_target="tpu_custom_call" | custom-call | flops 8858370048 | bytes 34078720 | tf_op jit(solution)/shard_map/pallas_call | solution.py:391
  248.1 8.1 %shard_map.308 = bf16[4,256,2048]{2,1,0:T(8,128)(2,1)} custom-call(s32[8,4,256]{2,1,0:T(4,128)S(1)} %convert_element_type.580.slots_ref, bf16[4,512,352]{2,1,0:T(8,128)(2,1)S(1)} %copy-done.8, bf16[4,352,2048]{2,1,0:T(8,128)(2,1)} %refs_1_.3, bf16[2048,128]{1,0:T(8,128)(2,1)S(1)} %get-tuple-element.49.refs_2_.act_ref, bf16[128,2048]{1,0:T(8,128)(2,1)S(1)} %pad.13.down_ref.refs_3_), custom_call_target="tpu_custom_call" | custom-call | flops 3087007744 | bytes 9961472 | tf_op jit(solution)/shard_map/pallas_call | solution.py:437
  256.5 21.2 %shard_map.316 = (f32[4,2048,352]{2,1,0:T(8,128)}, f32[4,2048,352]{2,1,0:T(8,128)}, f32[4,352,2048]{2,1,0:T(8,128)}) custom-call(bf16[4,512,2048]{2,1,0:T(8,128)(2,1)} %get-tuple-element.45.rows_ref, bf16[4,512,2048]{2,1,0:T(8,128)(2,1)} %get-tuple-element.46.grads_ref, bf16[4,512,352]{2,1,0:T(8,128)(2,1)} %get-tuple-element.48.refs_0_.act_ref, ...), custom_call_target="tpu_custom_call" | custom-call | flops 8858370048 | bytes 51380224 | tf_op jit(solution)/shard_map/pallas_call | solution.py:483
  277.7 6.9 %shard_map.310 = bf16[4,256,1024]{2,1,0:T(8,128)(2,1)} custom-call(s32[8,4,256]{2,1,0:T(4,128)S(1)} %convert_element_type.580.slots_ref, bf16[4,512,352]{2,1,0:T(8,128)(2,1)S(1)} %copy-done.4, bf16[4,512,352]{2,1,0:T(8,128)(2,1)S(1)} %copy-done.7, bf16[4,2048,352]{2,1,0:T(8,128)(2,1)} %copy.153.expert_gate_ref.refs_2_, ...), custom_call_target="tpu_custom_call" | custom-call | flops 2550136832 | bytes 7864320 | tf_op jit(solution)/shard_map/pallas_call | solution.py:437
  284.8 12.8 %shard_map.315 = (bf16[2048,256]{1,0:T(8,128)(2,1)}, bf16[128,2048]{1,0:T(8,128)(2,1)}) custom-call(bf16[2048,256]{1,0:T(8,128)(2,1)} %copy-done.2, bf16[2048,128]{1,0:T(8,128)(2,1)} %copy-done.9, bf16[256,2048]{1,0:T(8,128)(2,1)} %copy-done.13, bf16[256,2048]{1,0:T(8,128)(2,1)} %collective-permute-done.25.refs_1_, ...), custom_call_target="tpu_custom_call" | custom-call | flops 3221225472 | bytes 16777216 | tf_op jit(solution)/shard_map/pallas_call | solution.py:504
  301.5 6.7 shard_map.312
  346.9 12.2 %copy.185 = f32[4,2048,352]{1,2,0:T(8,128)} copy(f32[4,2048,352]{2,1,0:T(8,128)} %get-tuple-element.136) | data formatting | bytes 23068672
  359.1 12.2 %copy.186 = f32[4,2048,352]{1,2,0:T(8,128)} copy(f32[4,2048,352]{2,1,0:T(8,128)} %get-tuple-element.137) | data formatting | bytes 23068672
  411.1 8.9 %shard_map.309 = (bf16[256,2048]{1,0:T(8,128)(2,1)S(1)}, bf16[256,2048]{1,0:T(8,128)(2,1)}, bf16[256,2048]{1,0:T(8,128)(2,1)}, bf16[256,2048]{1,0:T(8,128)(2,1)S(1)}) custom-call(s32[8,4,256]{2,1,0:T(4,128)S(1)} %convert_element_type.580.slots_ref, bf16[4,512,352]{2,1,0:T(8,128)(2,1)} %get-tuple-element.48.refs_0_.act_ref, bf16[4,352,2048]{2,1,0:T(8,128)(2,1)} %refs_1_.3, ...), custom_call_target="tpu_custom_call" | custom-call | flops 3087007744 | bytes 9961472 | tf_op jit(solution)/shard_map/pallas_call | solution.py:437
  423.5 8.5 %collective-permute-done.48 = bf16[256,1024]{1,0:T(8,128)(2,1)S(1)} collective-permute-done((bf16[256,1024]{1,0:T(8,128)(2,1)S(1)}, bf16[256,1024]{1,0:T(8,128)(2,1)S(1)}, u32[]{:S(2)}, u32[]{:S(2)}) %collective-permute-start.48) | collective-permute-done | bytes 524320 | tf_op jit(solution)/shard_map/ppermute | solution.py:81
  435.2 9.0 %collective-permute-done.50 = bf16[256,1024]{1,0:T(8,128)(2,1)S(1)} collective-permute-done((bf16[256,1024]{1,0:T(8,128)(2,1)S(1)}, bf16[256,1024]{1,0:T(8,128)(2,1)S(1)}, u32[]{:S(2)}, u32[]{:S(2)}) %collective-permute-start.50) | collective-permute-done | bytes 524320 | tf_op jit(solution)/shard_map/ppermute | solution.py:81
  471.8 16.9 %collective-permute-done.33 = bf16[256,2048]{1,0:T(8,128)(2,1)} collective-permute-done((bf16[256,2048]{1,0:T(8,128)(2,1)S(1)}, bf16[256,2048]{1,0:T(8,128)(2,1)}, u32[]{:S(2)}, u32[]{:S(2)}) %collective-permute-start.33) | collective-permute-done | bytes 1048608 | tf_op jit(solution)/shard_map/ppermute | solution.py:81
  506.4 10.4 %collective-permute-done.35 = bf16[64,2048]{1,0:T(8,128)(2,1)S(1)} collective-permute-done((bf16[64,2048]{1,0:T(8,128)(2,1)S(1)}, bf16[64,2048]{1,0:T(8,128)(2,1)S(1)}, u32[]{:S(2)}, u32[]{:S(2)}) %collective-permute-start.35) | collective-permute-done | bytes 262176 | tf_op jit(solution)/shard_map/ppermute | solution.py:81
  529.7 10.6 %collective-permute-start.37 = (bf16[64,2048]{1,0:T(8,128)(2,1)S(1)}, bf16[64,2048]{1,0:T(8,128)(2,1)}, u32[]{:S(2)}, u32[]{:S(2)}) collective-permute-start(bf16[64,2048]{1,0:T(8,128)(2,1)S(1)} %get-tuple-element.222), channel_id=1, source_target_pairs={{0,1},{1,0},{2,3},{3,2},{4,5},{5,4},{6,7},{7,6},{8,9},{9,8},{10,11... | collective-permute-start | bytes 786440 | tf_op jit(solution)/shard_map/ppermute | solution.py:81
  540.2 14.4 %collective-permute-done.62 = bf16[64,2048]{1,0:T(8,128)(2,1)} collective-permute-done((bf16[64,2048]{1,0:T(8,128)(2,1)S(1)}, bf16[64,2048]{1,0:T(8,128)(2,1)}, u32[]{:S(2)}, u32[]{:S(2)}) %collective-permute-start.62) | collective-permute-done | bytes 262176 | tf_op jit(solution)/shard_map/ppermute | solution.py:81
  644.2 12.7 %collective-permute-done.68 = bf16[64,2048]{1,0:T(8,128)(2,1)S(1)} collective-permute-done((bf16[64,2048]{1,0:T(8,128)(2,1)S(1)}, bf16[64,2048]{1,0:T(8,128)(2,1)S(1)}, u32[]{:S(2)}, u32[]{:S(2)}) %collective-permute-start.68) | collective-permute-done | bytes 262176 | tf_op jit(solution)/shard_map/ppermute | solution.py:81
  (747 shorter events, 384.5 us)
Async XLA Ops:
  2.5 52.4 %collective-permute-start.11 = (bf16[32,256]{1,0:T(8,128)(2,1)}, bf16[32,256]{1,0:T(8,128)(2,1)}, u32[]{:S(2)}, u32[]{:S(2)}) collective-permute-start(bf16[32,256]{1,0:T(8,128)(2,1)} %fusion.18), channel_id=1, source_target_pairs={{0,24},{4,28},{8,16},{12,20},{16,8},{20,12},{24,0},{28,4},{1,25},{... | collective-permute-start | bytes 49160 | tf_op jit(solution)/shard_map/ppermute | solution.py:81
  6.4 49.2 %collective-permute-start.9 = (bf16[32,256]{1,0:T(8,128)(2,1)}, bf16[32,256]{1,0:T(8,128)(2,1)}, u32[]{:S(2)}, u32[]{:S(2)}) collective-permute-start(bf16[32,256]{1,0:T(8,128)(2,1)} %fusion.18), channel_id=1, source_target_pairs={{0,16},{4,20},{8,24},{12,28},{16,0},{20,4},{24,8},{28,12},{1,17},{... | collective-permute-start | bytes 49160 | tf_op jit(solution)/shard_map/ppermute | solution.py:81
  91.6 51.1 %collective-permute-start.18 = (bf16[256,2048]{1,0:T(8,128)(2,1)}, bf16[256,2048]{1,0:T(8,128)(2,1)}, u32[]{:S(2)}, u32[]{:S(2)}) collective-permute-start(bf16[256,2048]{1,0:T(8,128)(2,1)} %pad_maximum_fusion.refs_4_.refs_12_), channel_id=1, source_target_pairs={{0,24},{4,28},{8,16},{12,20},{16,8},{20,12},{24,0},{28,4},{1,25},{... | collective-permute-start | bytes 3145736 | tf_op jit(solution)/shard_map/ppermute | solution.py:81
  103.9 43.0 %collective-permute-start.16 = (bf16[256,2048]{1,0:T(8,128)(2,1)}, bf16[256,2048]{1,0:T(8,128)(2,1)}, u32[]{:S(2)}, u32[]{:S(2)}) collective-permute-start(bf16[256,2048]{1,0:T(8,128)(2,1)} %pad_maximum_fusion.refs_4_.refs_12_), channel_id=1, source_target_pairs={{0,16},{4,20},{8,24},{12,28},{16,0},{20,4},{24,8},{28,12},{1,17},{... | collective-permute-start | bytes 3145736 | tf_op jit(solution)/shard_map/ppermute | solution.py:81
  104.8 42.6 %collective-permute-start.14 = (bf16[256,2048]{1,0:T(8,128)(2,1)}, bf16[256,2048]{1,0:T(8,128)(2,1)}, u32[]{:S(2)}, u32[]{:S(2)}) collective-permute-start(bf16[256,2048]{1,0:T(8,128)(2,1)} %pad_maximum_fusion.refs_4_.refs_12_), channel_id=1, source_target_pairs={{0,8},{4,12},{8,0},{12,4},{16,24},{20,28},{24,16},{28,20},{1,9},{5... | collective-permute-start | bytes 3145736 | tf_op jit(solution)/shard_map/ppermute | solution.py:81
  106.1 41.3 %collective-permute-start.13 = (bf16[256,2048]{1,0:T(8,128)(2,1)}, bf16[256,2048]{1,0:T(8,128)(2,1)}, u32[]{:S(2)}, u32[]{:S(2)}) collective-permute-start(bf16[256,2048]{1,0:T(8,128)(2,1)} %pad_maximum_fusion.refs_4_.refs_12_), channel_id=1, source_target_pairs={{0,4},{4,0},{8,12},{12,8},{16,20},{20,16},{24,28},{28,24},{1,5},{5... | collective-permute-start | bytes 3145736 | tf_op jit(solution)/shard_map/ppermute | solution.py:81
  142.7 48.3 %collective-permute-start.26 = (bf16[256,2048]{1,0:T(8,128)(2,1)S(1)}, bf16[256,2048]{1,0:T(8,128)(2,1)}, u32[]{:S(2)}, u32[]{:S(2)}) collective-permute-start(bf16[256,2048]{1,0:T(8,128)(2,1)S(1)} %pad_maximum_fusion.1.refs_4_), channel_id=1, source_target_pairs={{0,16},{4,20},{8,24},{12,28},{16,0},{20,4},{24,8},{28,12},{1,17},{... | collective-permute-start | bytes 3145736 | tf_op jit(solution)/shard_map/ppermute | solution.py:81
  146.9 44.1 %collective-permute-start.24 = (bf16[256,2048]{1,0:T(8,128)(2,1)S(1)}, bf16[256,2048]{1,0:T(8,128)(2,1)}, u32[]{:S(2)}, u32[]{:S(2)}) collective-permute-start(bf16[256,2048]{1,0:T(8,128)(2,1)S(1)} %pad_maximum_fusion.1.refs_4_), channel_id=1, source_target_pairs={{0,8},{4,12},{8,0},{12,4},{16,24},{20,28},{24,16},{28,20},{1,9},{5... | collective-permute-start | bytes 3145736 | tf_op jit(solution)/shard_map/ppermute | solution.py:81
  147.3 44.3 %collective-permute-start.23 = (bf16[256,2048]{1,0:T(8,128)(2,1)S(1)}, bf16[256,2048]{1,0:T(8,128)(2,1)S(1)}, u32[]{:S(2)}, u32[]{:S(2)}) collective-permute-start(bf16[256,2048]{1,0:T(8,128)(2,1)S(1)} %pad_maximum_fusion.1.refs_4_), channel_id=1, source_target_pairs={{0,4},{4,0},{8,12},{12,8},{16,20},{20,16},{24,28},{28,24},{1,5},{5... | collective-permute-start | bytes 3145736 | tf_op jit(solution)/shard_map/ppermute | solution.py:81
  147.3 44.4 %collective-permute-start.19 = (bf16[256,2048]{1,0:T(8,128)(2,1)}, bf16[256,2048]{1,0:T(8,128)(2,1)S(1)}, u32[]{:S(2)}, u32[]{:S(2)}) collective-permute-start(bf16[256,2048]{1,0:T(8,128)(2,1)} %collective-permute-done.18.refs_7_.refs_15_), channel_id=1, source_target_pairs={{0,4},{4,0},{8,12},{12,8},{16,20},{20,16},{24,28},{28,24},{1,5},{5... | collective-permute-start | bytes 3145736 | tf_op jit(solution)/shard_map/ppermute | solution.py:81
  247.8 52.0 %collective-permute-start.54 = (bf16[4,256,128]{2,1,0:T(8,128)(2,1)S(1)}, bf16[4,256,128]{2,1,0:T(8,128)(2,1)S(1)}, u32[]{:S(2)}, u32[]{:S(2)}) collective-permute-start(bf16[4,256,128]{2,1,0:T(8,128)(2,1)S(1)} %slice.542), channel_id=1, source_target_pairs={{0,4},{4,0},{8,12},{12,8},{16,20},{20,16},{24,28},{28,24},{1,5},{5... | collective-permute-start | bytes 786440 | tf_op jit(solution)/shard_map/ppermute | solution.py:81
  256.2 154.8 %collective-permute-start.30 = (bf16[4,256,2048]{2,1,0:T(8,128)(2,1)}, bf16[4,256,2048]{2,1,0:T(8,128)(2,1)}, u32[]{:S(2)}, u32[]{:S(2)}) collective-permute-start(bf16[4,256,2048]{2,1,0:T(8,128)(2,1)} %shard_map.308), channel_id=1, source_target_pairs={{0,4},{4,0},{8,12},{12,8},{16,20},{20,16},{24,28},{28,24},{1,5},{5... | collective-permute-start | bytes 12582920 | tf_op jit(solution)/shard_map/ppermute | solution.py:81
  284.6 87.3 %collective-permute-start.40 = (bf16[4,256,1024]{2,1,0:T(8,128)(2,1)}, bf16[4,256,1024]{2,1,0:T(8,128)(2,1)}, u32[]{:S(2)}, u32[]{:S(2)}) collective-permute-start(bf16[4,256,1024]{2,1,0:T(8,128)(2,1)} %shard_map.310), channel_id=1, source_target_pairs={{0,4},{4,0},{8,12},{12,8},{16,20},{20,16},{24,28},{28,24},{1,5},{5... | collective-permute-start | bytes 6291464 | tf_op jit(solution)/shard_map/ppermute | solution.py:81
  308.9 73.7 %all-to-all-start.1 = ((bf16[8,88,256]{2,1,0:T(8,128)(2,1)}), bf16[8,88,256]{2,1,0:T(8,128)(2,1)}, u32[]{:S(2)}, u32[]{:S(2)}) async-start(bf16[8,88,256]{2,1,0:T(8,128)(2,1)} %bitcast.209), calls=%async_computation.1 | async-start | bytes 720896 | tf_op jit(solution)/shard_map/all_to_all | solution.py:723
  313.0 79.9 %collective-permute-start.47 = (bf16[4,256,1024]{2,1,0:T(8,128)(2,1)}, bf16[4,256,1024]{2,1,0:T(8,128)(2,1)}, u32[]{:S(2)}, u32[]{:S(2)}) collective-permute-start(bf16[4,256,1024]{2,1,0:T(8,128)(2,1)} %shard_map.312), channel_id=1, source_target_pairs={{0,4},{4,0},{8,12},{12,8},{16,20},{20,16},{24,28},{28,24},{1,5},{5... | collective-permute-start | bytes 6291464 | tf_op jit(solution)/shard_map/ppermute | solution.py:81
  382.6 73.7 %all-to-all-start = ((bf16[8,256,176]{1,2,0:T(8,128)(2,1)}), bf16[8,256,176]{1,2,0:T(8,128)(2,1)}, u32[]{:S(2)}, u32[]{:S(2)}) async-start(bf16[8,256,176]{1,2,0:T(8,128)(2,1)} %copy.181), calls=%async_computation | async-start | bytes 1441792 | tf_op jit(solution)/shard_map/all_to_all | solution.py:708
  420.0 51.8 %collective-permute-start.31 = (bf16[256,2048]{1,0:T(8,128)(2,1)}, bf16[256,2048]{1,0:T(8,128)(2,1)}, u32[]{:S(2)}, u32[]{:S(2)}) collective-permute-start(bf16[256,2048]{1,0:T(8,128)(2,1)} %get-tuple-element.51), channel_id=1, source_target_pairs={{0,8},{4,12},{8,0},{12,4},{16,24},{20,28},{24,16},{28,20},{1,9},{5... | collective-permute-start | bytes 3145736 | tf_op jit(solution)/shard_map/ppermute | solution.py:81
  422.0 49.8 %collective-permute-start.32 = (bf16[256,2048]{1,0:T(8,128)(2,1)}, bf16[256,2048]{1,0:T(8,128)(2,1)}, u32[]{:S(2)}, u32[]{:S(2)}) collective-permute-start(bf16[256,2048]{1,0:T(8,128)(2,1)} %get-tuple-element.52), channel_id=1, source_target_pairs={{0,16},{4,20},{8,24},{12,28},{16,0},{20,4},{24,8},{28,12},{1,17},{... | collective-permute-start | bytes 3145736 | tf_op jit(solution)/shard_map/ppermute | solution.py:81
  432.0 56.8 %collective-permute-start.33 = (bf16[256,2048]{1,0:T(8,128)(2,1)S(1)}, bf16[256,2048]{1,0:T(8,128)(2,1)}, u32[]{:S(2)}, u32[]{:S(2)}) collective-permute-start(bf16[256,2048]{1,0:T(8,128)(2,1)S(1)} %get-tuple-element.53), channel_id=1, source_target_pairs={{0,24},{4,28},{8,16},{12,20},{16,8},{20,12},{24,0},{28,4},{1,25},{... | collective-permute-start | bytes 3145736 | tf_op jit(solution)/shard_map/ppermute | solution.py:81
  520.7 34.0 %collective-permute-start.62 = (bf16[64,2048]{1,0:T(8,128)(2,1)S(1)}, bf16[64,2048]{1,0:T(8,128)(2,1)}, u32[]{:S(2)}, u32[]{:S(2)}) collective-permute-start(bf16[64,2048]{1,0:T(8,128)(2,1)S(1)} %get-tuple-element.145), channel_id=1, source_target_pairs={{0,2},{1,3},{2,0},{3,1},{4,6},{5,7},{6,4},{7,5},{8,10},{9,11},{10,... | collective-permute-start | bytes 786440 | tf_op jit(solution)/shard_map/ppermute | solution.py:81
  520.7 34.0 %collective-permute-start.61 = (bf16[64,2048]{1,0:T(8,128)(2,1)S(1)}, bf16[64,2048]{1,0:T(8,128)(2,1)}, u32[]{:S(2)}, u32[]{:S(2)}) collective-permute-start(bf16[64,2048]{1,0:T(8,128)(2,1)S(1)} %get-tuple-element.145), channel_id=1, source_target_pairs={{0,1},{1,0},{2,3},{3,2},{4,5},{5,4},{6,7},{7,6},{8,9},{9,8},{10,11... | collective-permute-start | bytes 786440 | tf_op jit(solution)/shard_map/ppermute | solution.py:81
  524.2 48.8 %collective-permute-start.39 = (bf16[64,2048]{1,0:T(8,128)(2,1)S(1)}, bf16[64,2048]{1,0:T(8,128)(2,1)}, u32[]{:S(2)}, u32[]{:S(2)}) collective-permute-start(bf16[64,2048]{1,0:T(8,128)(2,1)S(1)} %get-tuple-element.222), channel_id=1, source_target_pairs={{0,3},{1,2},{2,1},{3,0},{4,7},{5,6},{6,5},{7,4},{8,11},{9,10},{10,... | collective-permute-start | bytes 786440 | tf_op jit(solution)/shard_map/ppermute | solution.py:81
  526.3 46.7 %collective-permute-start.38 = (bf16[64,2048]{1,0:T(8,128)(2,1)S(1)}, bf16[64,2048]{1,0:T(8,128)(2,1)}, u32[]{:S(2)}, u32[]{:S(2)}) collective-permute-start(bf16[64,2048]{1,0:T(8,128)(2,1)S(1)} %get-tuple-element.222), channel_id=1, source_target_pairs={{0,2},{1,3},{2,0},{3,1},{4,6},{5,7},{6,4},{7,5},{8,10},{9,11},{10,... | collective-permute-start | bytes 786440 | tf_op jit(solution)/shard_map/ppermute | solution.py:81
  529.7 43.4 %collective-permute-start.37 = (bf16[64,2048]{1,0:T(8,128)(2,1)S(1)}, bf16[64,2048]{1,0:T(8,128)(2,1)}, u32[]{:S(2)}, u32[]{:S(2)}) collective-permute-start(bf16[64,2048]{1,0:T(8,128)(2,1)S(1)} %get-tuple-element.222), channel_id=1, source_target_pairs={{0,1},{1,0},{2,3},{3,2},{4,5},{5,4},{6,7},{7,6},{8,9},{9,8},{10,11... | collective-permute-start | bytes 786440 | tf_op jit(solution)/shard_map/ppermute | solution.py:81
  (264 other events, 3560.9 us)

commit v2 on v1

v2 whole, which is shorter than its diff:
```python
import functools

import jax
import jax.numpy as jnp
import numpy as np
from jax import lax
from jax.experimental import pallas as pl
from jax.experimental.pallas import tpu as pltpu
from jax.sharding import PartitionSpec as P

HD = 128
RD = 64
VD = 128
TOPK = 6
SEQ = 256
CAP = 64
LANES = 128
EPSILON = 1e-06
HEAD = 256
KV = HD + VD
MIB = 1 << 20
VMEM = 60

bf16 = jnp.bfloat16
f32 = jnp.float32


def dot(a, b):
    return lax.dot_general(a, b, (((1,), (0,)), ((), ())), preferred_element_type=f32)


def dot_nt(a, b):
    return lax.dot_general(a, b, (((1,), (1,)), ((), ())), preferred_element_type=f32)


def dot_tn(a, b):
    return lax.dot_general(a, b, (((0,), (0,)), ((), ())), preferred_element_type=f32)


def rope_tables():
    frequency = np.float32(10000.0) ** (-np.arange(RD // 2, dtype=np.float32) * np.float32(2.0 / RD))
    angles = np.arange(SEQ, dtype=np.float32)[:, None] * frequency[None, :]
    blank = np.zeros((SEQ, LANES - RD), np.float32)
    cosine, sine = np.cos(angles), np.sin(angles)
    return (
        jnp.asarray(np.concatenate([cosine, cosine, blank], axis=1)),
        jnp.asarray(np.concatenate([-sine, sine, blank], axis=1)),
    )


def rotate(vector, cosines, sines):
    lane = lax.broadcasted_iota(jnp.int32, vector.shape, 1)
    swapped = jnp.where(
        lane < RD // 2, pltpu.roll(vector, LANES - RD // 2, 1), pltpu.roll(vector, RD // 2, 1)
    )
    return vector * cosines + swapped * sines


def rms_norm(values, gains):
    inv_rms = lax.rsqrt(jnp.mean(values * values, axis=-1, keepdims=True) + EPSILON)
    return (values * inv_rms * gains, inv_rms)


def rms_back(cotan, values, inv_rms, gains):
    weighted = cotan * gains
    inner_mean = jnp.mean(weighted * values, axis=-1, keepdims=True)
    value_grad = inv_rms * weighted - values * (inv_rms * inv_rms * inv_rms) * inner_mean
    gain_grad = jnp.sum(cotan * values * inv_rms, axis=0)
    return (value_grad, gain_grad)


def swap(array, axis, bits):
    count = lax.axis_size(axis)
    return lax.ppermute(array, axis, [(i, i ^ bits) for i in range(count)])


def chip_bits(core):
    bits = [2 << i for i in range((lax.axis_size("dp") // 2).bit_length() - 1)]
    return bits[::-1] if core else bits


def partner_list(core):
    partners = [0]
    for bit in chip_bits(core):
        partners = partners + [p + bit for p in partners]
    return partners


def swap_chips(array, step):
    count = lax.axis_size("dp")
    return lax.ppermute(array, "dp", [(i, i ^ chip_bits(i % 2)[step]) for i in range(count)])


def partner_order():
    core = lax.axis_index("dp") % 2
    lists = jnp.array([partner_list(0), partner_list(1)], jnp.int32)
    return jnp.concatenate([lists[1 - core] ^ 1, lists[core]])


def block_at(array, index, size, dim):
    return lax.dynamic_slice_in_dim(array, index * size, size, dim)


def by_partner(array, axis, dim):
    count = lax.axis_size(axis)
    own = lax.axis_index(axis)
    size = array.shape[dim] // count
    return [block_at(array, own ^ r, size, dim) for r in range(count)]


def reorder(array, axis, dim):
    return jnp.concatenate(by_partner(array, axis, dim), axis=dim)


def share(array, axis):
    blocks = {0: array}
    bit = lax.axis_size(axis) // 2
    while bit:
        blocks.update({r ^ bit: swap(block, axis, bit) for r, block in blocks.items()})
        bit //= 2
    return [blocks[r] for r in range(len(blocks))]


def trade(blocks, axis):
    return [blocks[0]] + [swap(blocks[r], axis, r) for r in range(1, len(blocks))]


def gather_chips(block):
    own = [block]
    for step in range(len(chip_bits(0))):
        own = own + [swap_chips(have, step) for have in own]
    return own


def both_cores(own):
    return [swap(have, "dp", 1) for have in own] + list(own)


def gather_dp(block):
    return both_cores(gather_chips(block))


def sum_chips(pairs):
    arrivals = []
    for step in reversed(range(len(chip_bits(0)))):
        got = [swap_chips(send, step) for _, send in pairs]
        arrivals.append(got)
        size = got[0].shape[0]
        sums = [keep.astype(f32) + g.astype(f32) for (keep, _), g in zip(pairs, got)]
        pairs = [(s[: size // 2], s[size // 2 :].astype(bf16)) for s in sums]
    return [s[0] for s in sums], arrivals


def sum_dp(far, near):
    here = (near.astype(f32) + swap(far, "dp", 1).astype(f32)).astype(bf16)
    half = here.shape[0] // 2
    return sum_chips([(here[:half], here[half:])])[0][0]


def total(blocks):
    return functools.reduce(jnp.add, [block.astype(f32) for block in blocks])


def after(values, *others):
    return lax.optimization_barrier((values, others))[0]


def pick_matrix(slots):
    toks = slots.shape[1]
    place = lax.broadcasted_iota(jnp.int32, (CAP, toks), 0)
    return jnp.concatenate(
        [
            jnp.where(place == slots[e : e + 1, :], 1.0, 0.0).astype(bf16)
            for e in range(slots.shape[0])
        ],
        axis=0,
    )


def fetch(refs, buffer, sems):
    step = pl.program_id(0)

    @pl.when(step == 0)
    def _():
        for i, ref in enumerate(refs):
            pltpu.make_async_copy(ref, buffer.at[i], sems.at[i]).start()

    pltpu.make_async_copy(refs[0], buffer.at[step], sems.at[step]).wait()
    return buffer.at[step]


def by_place(array, tensor, parts):
    size = array.shape[0] // parts
    return [array[pl.ds(pl.multiple_of((tensor ^ r) * size, size), size), :] for r in range(parts)]


def pick_grad_kernel(parts, src_ref, tensor_ref, slots_ref, block_ref, down_ref, rows_ref, dact_ref, placed):
    slots = slots_ref[0]
    blocks = by_place(block_ref.at[0], tensor_ref[0], parts)
    for r, block in enumerate(blocks):
        placed[r * block.shape[0] : (r + 1) * block.shape[0]] = block
    picked = dot(pick_matrix(slots), placed[...]).astype(bf16)
    for e in range(slots.shape[0]):
        rows_ref[e] = picked[e * CAP : (e + 1) * CAP]
    dact_ref[...] = dot_nt(placed[...], down_ref[...])


def pick_kernel(count, experts_all, aliased, slots_ref, router_ref, weights_ref, dact_ref, *refs):
    rows_ref, gate_ref, act_ref, delta_ref, buffer, sems = refs[count + aliased :]
    block = fetch(refs[:count], buffer, sems)
    slots = slots_ref[0]
    experts = slots.shape[0]
    picks = pick_matrix(slots)
    picked = dot(picks, block[...]).astype(bf16)
    for e in range(experts):
        rows_ref[e] = picked[e * CAP : (e + 1) * CAP]
    parts = dot_nt(router_ref[...], block[...])
    logits = parts[:experts_all] + parts[experts_all : 2 * experts_all] + parts[2 * experts_all :]
    spread = jnp.exp(logits - jnp.max(logits, axis=0, keepdims=True))
    prob = spread / jnp.sum(spread, axis=0, keepdims=True)
    for e in range(experts):
        chosen = picks[e * CAP : (e + 1) * CAP].astype(f32) * prob[e : e + 1, :]
        gate_ref[e] = jnp.broadcast_to(jnp.sum(chosen, axis=1, keepdims=True), (CAP, LANES))
    hidden = dot_nt(block[...], weights_ref[...])
    width = hidden.shape[1] // 2
    act, gate_delta, up_delta = gated(hidden[:, :width], hidden[:, width:], dact_ref[...])
    act_ref[...] = act.astype(bf16)
    delta_ref[:, :width] = gate_delta.astype(bf16)
    delta_ref[:, width:] = up_delta.astype(bf16)


def gated(gate_h, up_h, dact):
    sigmoid_h = jax.nn.sigmoid(gate_h)
    silu_h = gate_h * sigmoid_h
    gate_delta = dact * up_h * sigmoid_h * (1.0 + gate_h * (1.0 - sigmoid_h))
    return silu_h * up_h, gate_delta, dact * silu_h


def hidden_kernel(
    first_ref,
    rows_ref,
    grads_ref,
    gate_ref,
    expert_gate_ref,
    expert_up_ref,
    expert_down_ref,
    act_ref,
    gate_delta_ref,
    up_delta_ref,
    score_ref,
):
    rows = rows_ref[0]
    gate_h = dot_nt(rows, expert_gate_ref[0])
    up_h = dot_nt(rows, expert_up_ref[0])
    dact = dot_nt(grads_ref[0], expert_down_ref[0])
    gate = gate_ref[0][:, :1]
    act, gate_delta, up_delta = gated(gate_h, up_h, dact)
    act_ref[0] = (act * gate).astype(bf16)
    gate_delta_ref[0] = (gate_delta * gate).astype(bf16)
    up_delta_ref[0] = (up_delta * gate).astype(bf16)
    score = jnp.sum(act * dact, axis=1, keepdims=True)
    high = score.astype(bf16).astype(f32)
    lanes = score_ref.shape[2]
    lane = lax.broadcasted_iota(jnp.int32, (rows.shape[0], lanes), 1)
    mine = first_ref[0] + pl.program_id(0)
    score_ref[0] = jnp.where(
        lane == mine, high, jnp.where(lane == mine + lanes // 2, score - high, 0.0)
    ).astype(bf16)


def return_kernel(spec, slots_ref, *refs):
    pairs, scored, added, outputs, steps = spec
    deltas, weights = refs[:pairs], refs[pairs : 2 * pairs]
    shared_ref, shared_weight_ref = refs[2 * pairs : 2 * pairs + 2]
    rest = refs[2 * pairs + 2 :]
    score_ref, rest = (rest[0], rest[1:]) if scored else (None, rest)
    other_ref, rest = (rest[0], rest[1:]) if added else (None, rest)
    outs, picks, rows = rest[:outputs], rest[outputs], rest[outputs + 1]
    sources, _, chunk = rows.shape
    experts = slots_ref.shape[1]
    toks = picks.shape[2]
    step = pl.program_id(0)

    def store(s, columns, value):
        if added:
            value = value + other_ref[s, :, columns].astype(f32)
        out = outs[s // (sources // outputs)]
        out[s % (sources // outputs), :, columns] = value.astype(bf16)

    @pl.when(step == 0)
    def _():
        for s in range(sources):
            picks[s] = pick_matrix(slots_ref[s])
        if scored:
            for s in range(sources):
                score = jnp.concatenate(
                    [score_ref[e, s * CAP : (s + 1) * CAP] for e in range(experts)], axis=0
                )
                store(s, pl.ds(steps * chunk, score.shape[1]), dot_tn(picks[s], score))

    for e in range(experts):
        back = functools.reduce(
            jnp.add, [dot(d[e], w[e]) for d, w in zip(deltas, weights)]
        ).astype(bf16)
        for s in range(sources):
            rows[s, e * CAP : (e + 1) * CAP, :] = back[s * CAP : (s + 1) * CAP]
    columns = pl.ds(pl.multiple_of(step * chunk, chunk), chunk)
    for s in range(sources):
        summed = dot_tn(picks[s], rows[s]) + dot(
            shared_ref[s * toks : (s + 1) * toks], shared_weight_ref[...]
        )
        store(s, columns, summed)


def expert_grad_kernel(
    rows_ref,
    grads_ref,
    act_ref,
    gate_delta_ref,
    up_delta_ref,
    gate_grad_ref,
    up_grad_ref,
    down_grad_ref,
):
    rows = rows_ref[0]
    gate_grad_ref[0] = dot_tn(gate_delta_ref[0], rows)
    up_grad_ref[0] = dot_tn(up_delta_ref[0], rows)
    down_grad_ref[0] = dot_tn(act_ref[0], grads_ref[0])


def shared_grad_kernel(count, parts, src_ref, tensor_ref, delta_ref, act_ref, grad_ref, *refs):
    out_ref, buffer, placed, in_acc, down_acc, sems = refs[count:]
    step = pl.program_id(0)
    block = fetch(refs[:count], buffer, sems)
    rows = placed.shape[0] // parts
    for r, part in enumerate(by_place(grad_ref.at[0], tensor_ref[0], parts)):
        placed[r * rows : (r + 1) * rows] = part

    @pl.when(step == 0)
    def _():
        in_acc[...] = jnp.zeros_like(in_acc)
        down_acc[...] = jnp.zeros_like(down_acc)

    in_acc[...] += dot_tn(delta_ref[...], block[...])
    down_acc[...] += dot_tn(act_ref[...], placed[...])

    @pl.when(step == count - 1)
    def _():
        devices, rows, columns = out_ref.shape
        rows //= 3
        middle = in_acc.shape[0] // 2
        for j in range(devices):
            here = slice(j * columns, (j + 1) * columns)
            out_ref[j, :rows] = in_acc[:rows, here].astype(bf16)
            out_ref[j, rows : 2 * rows] = in_acc[middle : middle + rows, here].astype(bf16)
            out_ref[j, 2 * rows :] = down_acc[:rows, here].astype(bf16)


def rows_grad_kernel(src_ref, left_ref, right_ref, far_ref, near_ref):
    half, rows, _ = far_ref.shape
    for i in range(2 * half):
        start = pl.multiple_of(src_ref[i] * rows, rows)
        product = dot_tn(left_ref[:, pl.ds(start, rows)], right_ref[...]).astype(bf16)
        if i < half:
            far_ref[i] = product
        else:
            near_ref[i - half] = product


def columns_grad_kernel(parts, flat, src_ref, left_ref, logits_ref, block_ref, gain_ref, *refs):
    far_ref, near_ref, grads = refs[parts:]
    rows = left_ref.shape[0] // parts
    for r in range(parts):
        grads[r * rows : (r + 1) * rows] = refs[r][:rows]
    half, height, width = far_ref.shape
    wide, experts_all = left_ref.shape[1], logits_ref.shape[1]
    for i in range(2 * half):
        columns = pl.ds(pl.multiple_of(src_ref[i] * width, width), width)
        out = far_ref.at[i] if i < half else near_ref.at[i - half]
        out[:wide] = dot_tn(left_ref[...], grads[:, columns]).astype(bf16)
        router = dot_tn(logits_ref[...], block_ref[:, columns])
        rest = jnp.concatenate(
            [router, jnp.broadcast_to(gain_ref[:, columns], (height - wide - experts_all, width))],
            axis=0,
        )
        out[wide:] = rest.astype(bf16)


def normed_kernel(tokens_ref, gain_ref, down_ref, rope_ref, normed_ref, inv_ref, narrow_ref):
    normed, inv = rms_norm(tokens_ref[...].astype(f32), gain_ref[...])
    normed = normed.astype(bf16)
    normed_ref[...] = normed
    inv_ref[...] = inv
    cols = down_ref.shape[1]
    narrow_ref[:, :cols] = dot(normed, down_ref[...]).astype(bf16)
    narrow_ref[:, cols:] = dot_nt(normed, rope_ref[...]).astype(bf16)


def query_kernel(normed_ref, weight_ref, cosines_ref, sines_ref, query_ref):
    raw = dot(normed_ref[...], weight_ref[...])
    toks = raw.shape[0]
    for h in range(raw.shape[1] // (HD + RD)):
        start = h * (HD + RD)
        rope = jnp.concatenate(
            [raw[:, start + HD : start + HD + RD], jnp.zeros((toks, LANES - RD), f32)], axis=1
        )
        query_ref[:, h * HEAD : h * HEAD + HD] = raw[:, start : start + HD].astype(bf16)
        query_ref[:, h * HEAD + HD : (h + 1) * HEAD] = rotate(
            rope, cosines_ref[...], sines_ref[...]
        ).astype(bf16)


def causal(scores):
    later = lax.broadcasted_iota(jnp.int32, scores.shape, 1) > lax.broadcasted_iota(
        jnp.int32, scores.shape, 0
    )
    return jnp.where(later, -1e30, scores)


def attention_kernel(
    parts,
    tensor_ref,
    query_ref,
    cosines_ref,
    sines_ref,
    place_ref,
    gain_ref,
    up_ref,
    out_weight_ref,
    *refs,
):
    narrow = [ref[...] for ref in refs[:parts]]
    sums = refs[parts : 2 * parts]
    attended_ref, latent_ref, latent_normed_ref, inv_ref, kv_ref, rope_ref, lse_ref, natural = refs[
        2 * parts :
    ]
    toks = query_ref.shape[0]
    heads = query_ref.shape[1] // HEAD
    cols = up_ref.shape[0] // parts
    latent = jnp.concatenate([n[:, :cols] for n in narrow], axis=1)
    latent_ref[...] = latent
    normed, inv = rms_norm(latent.astype(f32), gain_ref[...])
    normed = normed.astype(bf16)
    latent_normed_ref[...] = normed
    inv_ref[...] = inv
    rope = dot(jnp.concatenate([n[:, cols:] for n in narrow], axis=1), place_ref[...])
    rope = rotate(rope, cosines_ref[...], sines_ref[...]).astype(bf16)
    rope_ref[...] = rope
    kv_ref[...] = dot(normed, up_ref[...]).astype(bf16)
    lane = lax.broadcasted_iota(jnp.int32, (toks, LANES), 1)
    lses = jnp.zeros((toks, LANES), f32)
    for h in range(heads):
        key = jnp.concatenate([kv_ref[:, h * KV : h * KV + HD], rope], axis=1)
        scores = causal(dot_nt(query_ref[:, h * HEAD : (h + 1) * HEAD], key) * (HD + RD) ** -0.5)
        top = jnp.max(scores, axis=1, keepdims=True)
        lse = top + jnp.log(jnp.sum(jnp.exp(scores - top), axis=1, keepdims=True))
        lses = jnp.where(lane == h, lse, lses)
        weights = jnp.exp(scores - lse).astype(bf16)
        natural[:, h * VD : (h + 1) * VD] = dot(
            weights, kv_ref[:, h * KV + HD : (h + 1) * KV]
        ).astype(bf16)
    lse_ref[...] = lses
    rows = toks // parts
    for r, block in enumerate(by_place(natural, tensor_ref[0], parts)):
        attended_ref[r * rows : (r + 1) * rows] = block
    for r in range(parts):
        product = dot(attended_ref[r * rows : (r + 1) * rows], out_weight_ref[...])
        sums[r][...] = product.astype(sums[r].dtype)


def attention_back_kernel(
    parts,
    tensor_ref,
    src_ref,
    query_ref,
    kv_ref,
    rope_ref,
    lse_ref,
    latent_ref,
    latent_normed_ref,
    inv_ref,
    cosines_ref,
    sines_ref,
    place_ref,
    gain_ref,
    up_ref,
    out_weight_ref,
    *refs,
):
    grads = refs[:parts]
    narrow = refs[parts : 2 * parts]
    query_grad_ref, up_far_ref, up_near_ref, natural, query_nat, kv_grad, narrow_nat, up_part = refs[
        2 * parts :
    ]
    toks = query_ref.shape[0]
    heads = query_ref.shape[1] // HEAD
    rows = toks // parts
    factor = (HD + RD) ** -0.5
    tensor = tensor_ref[0]
    for r in range(parts):
        place = pl.ds(pl.multiple_of((tensor ^ r) * rows, rows), rows)
        natural[place, :] = dot_nt(grads[r][:rows], out_weight_ref[...]).astype(bf16)
    rope = rope_ref[...]
    rope_sum = jnp.zeros((toks, LANES), f32)
    for h in range(heads):
        grad = natural[:, h * VD : (h + 1) * VD]
        query = query_ref[:, h * HEAD : (h + 1) * HEAD]
        key = jnp.concatenate([kv_ref[:, h * KV : h * KV + HD], rope], axis=1)
        scores = causal(dot_nt(query, key) * factor)
        probs = jnp.exp(scores - lse_ref[:, h : h + 1])
        kv_grad[:, h * KV + HD : (h + 1) * KV] = dot_tn(probs.astype(bf16), grad).astype(bf16)
        prob_dot = dot_nt(grad, kv_ref[:, h * KV + HD : (h + 1) * KV])
        inner = jnp.sum(probs * prob_dot, axis=1, keepdims=True)
        score_grad = (probs * (prob_dot - inner) * factor).astype(bf16)
        query_grad = dot(score_grad, key)
        start = h * (HD + RD)
        query_nat[:, start : start + HD] = query_grad[:, :HD].astype(bf16)
        query_nat[:, start + HD : start + HD + RD] = rotate(
            query_grad[:, HD:], cosines_ref[...], -sines_ref[...]
        )[:, :RD].astype(bf16)
        key_grad = dot_tn(score_grad, query)
        kv_grad[:, h * KV : h * KV + HD] = key_grad[:, :HD].astype(bf16)
        rope_sum = rope_sum + key_grad[:, HD:]
    for r, block in enumerate(by_place(query_nat, tensor, parts)):
        query_grad_ref[r * rows : (r + 1) * rows] = block
    latent_grad, _ = rms_back(
        dot_nt(kv_grad[...], up_ref[...]), latent_ref[...].astype(f32), inv_ref[...], gain_ref[...]
    )
    rope_sum = rotate(rope_sum, cosines_ref[...], -sines_ref[...]).astype(bf16)
    rope_sum = dot_nt(rope_sum, place_ref[...])
    cols = latent_grad.shape[1] // parts
    rope_cols = rope_sum.shape[1] // parts
    for k in range(parts):
        narrow_nat[:, :cols] = latent_grad[:, k * cols : (k + 1) * cols]
        narrow_nat[:, cols:] = rope_sum[:, k * rope_cols : (k + 1) * rope_cols]
        narrow[k][...] = narrow_nat[...].astype(narrow[k].dtype)
    up_part[...] = dot_tn(latent_normed_ref[...], kv_grad[...])
    half, up_rows, _ = up_far_ref.shape
    for i in range(2 * half):
        start = src_ref[i] * up_rows
        start = (start // cols ^ tensor) * cols + start % cols
        block = up_part[pl.ds(pl.multiple_of(start, up_rows), up_rows), :].astype(bf16)
        if i < half:
            up_far_ref[i] = block
        else:
            up_near_ref[i - half] = block


def normed_back_kernel(parts, tensor_ref, query_grad_ref, query_weight_ref, down_ref, rope_ref, *refs):
    narrow = refs[:parts]
    sums = refs[parts : 2 * parts]
    all_ref, natural = refs[2 * parts :]
    cols = down_ref.shape[1]
    natural[...] = total([ref[...] for ref in narrow])
    mine = jnp.concatenate(by_place(natural, tensor_ref[0], parts), axis=0).astype(bf16)
    all_ref[...] = mine
    rows = query_grad_ref.shape[0] // parts
    product = (
        dot_nt(query_grad_ref[...], query_weight_ref[...])
        + dot_nt(mine[:, :cols], down_ref[...])
        + dot(mine[:, cols:], rope_ref[...])
    )
    for r in range(parts):
        sums[r][...] = product[r * rows : (r + 1) * rows].astype(sums[r].dtype)


ANYWHERE = pl.BlockSpec(memory_space=pl.ANY)


def whole(array):
    rank = len(array.shape)
    return pl.BlockSpec(array.shape, lambda *_: (0,) * rank)


def params(mib):
    return pltpu.CompilerParams(vmem_limit_bytes=mib * MIB)


def cost(flops, bytes_accessed, transcendentals=0):
    return pl.CostEstimate(
        flops=int(flops), bytes_accessed=int(bytes_accessed), transcendentals=int(transcendentals)
    )


def pick_grads(src, tensor, parts, slots, grads, shared_down):
    count, experts, toks = slots.shape
    width = grads.shape[2]
    shared = shared_down.shape[0]
    return pl.pallas_call(
        functools.partial(pick_grad_kernel, parts),
        grid_spec=pltpu.PrefetchScalarGridSpec(
            num_scalar_prefetch=2,
            grid=(count,),
            in_specs=[
                pl.BlockSpec((1, experts, toks), lambda s, src, t: (s, 0, 0)),
                pl.BlockSpec((1, toks, width), lambda s, src, t: (src[s], 0, 0)),
                whole(shared_down),
            ],
            out_specs=[
                pl.BlockSpec((experts, CAP, width), lambda s, src, t: (0, s, 0)),
                pl.BlockSpec((toks, shared), lambda s, src, t: (s, 0)),
            ],
            scratch_shapes=[pltpu.VMEM((toks, width), bf16)],
        ),
        out_shape=[
            jax.ShapeDtypeStruct((experts, count * CAP, width), bf16),
            jax.ShapeDtypeStruct((count * toks, shared), f32),
        ],
        compiler_params=params(VMEM),
        cost_estimate=cost(
            2 * count * toks * width * (experts * CAP + shared), 4 * count * toks * width
        ),
    )(src, tensor, slots, grads, shared_down)


def pick_rows(blocks, first, slots, router, weights, dact, experts_all, results):
    count = len(blocks)
    every, experts, toks = slots.shape
    width = blocks[0].shape[1]
    shared = dact.shape[1]
    operands = [slots, router, weights, dact, *blocks, *results]
    return pl.pallas_call(
        functools.partial(pick_kernel, count, experts_all, len(results)),
        grid=(count,),
        in_specs=[
            pl.BlockSpec((1, experts, toks), lambda s: (s + first, 0, 0)),
            whole(router),
            whole(weights),
            pl.BlockSpec((toks, shared), lambda s: (s + first, 0)),
        ]
        + [ANYWHERE] * (count + len(results)),
        out_specs=[
            pl.BlockSpec((experts, CAP, width), lambda s: (0, s + first, 0)),
            pl.BlockSpec((experts, CAP, LANES), lambda s: (0, s + first, 0)),
            pl.BlockSpec((toks, shared), lambda s: (s + first, 0)),
            pl.BlockSpec((toks, 2 * shared), lambda s: (s + first, 0)),
        ],
        out_shape=[
            shape(bf16, experts, every * CAP, width),
            shape(f32, experts, every * CAP, LANES),
            shape(bf16, every * toks, shared),
            shape(bf16, every * toks, 2 * shared),
        ],
        input_output_aliases={len(operands) - len(results) + i: i for i in range(len(results))},
        scratch_shapes=[
            pltpu.VMEM((count, toks, width), bf16),
            pltpu.SemaphoreType.DMA((count,)),
        ],
        compiler_params=params(VMEM),
        cost_estimate=cost(
            2 * count * toks * width * (experts * CAP + router.shape[0] + 2 * shared),
            4 * count * toks * width,
        ),
    )(*operands)


def expert_hidden(first, rows, grads, gate, expert_gate, expert_up, expert_down, lanes):
    experts, slot_rows, width = rows.shape
    hidden = expert_gate.shape[1]

    def per_expert(array):
        return pl.BlockSpec((1,) + array.shape[1:], lambda e: (e, 0, 0))

    narrow = jax.ShapeDtypeStruct((experts, slot_rows, hidden), bf16)
    score = jax.ShapeDtypeStruct((experts, slot_rows, lanes), bf16)
    return pl.pallas_call(
        hidden_kernel,
        grid=(experts,),
        in_specs=[pl.BlockSpec(memory_space=pltpu.SMEM)]
        + [per_expert(a) for a in (rows, grads, gate, expert_gate, expert_up, expert_down)],
        out_specs=[per_expert(narrow)] * 3 + [per_expert(score)],
        out_shape=[narrow] * 3 + [score],
        compiler_params=params(VMEM),
        cost_estimate=cost(
            6 * experts * slot_rows * width * hidden,
            experts * (4 * slot_rows * width + 6 * hidden * width),
            experts * slot_rows * hidden,
        ),
    )(first, rows, grads, gate, expert_gate, expert_up, expert_down)


def return_rows(half, slots, deltas, weights, shared, shared_weight, score, start, size, other):
    experts, slot_rows, hidden = deltas[0].shape
    sources = slots.shape[0] // 2
    toks = slots.shape[2]
    chunk = min(512, size)
    steps = size // chunk
    first = start // chunk
    outputs = 1 + half
    lanes = 0 if score is None else score.shape[2]
    in_specs = (
        [pl.BlockSpec((sources,) + slots.shape[1:], lambda n: (half, 0, 0))]
        + [pl.BlockSpec((experts, slot_rows // 2, hidden), lambda n: (0, half, 0))] * len(deltas)
        + [pl.BlockSpec((experts, hidden, chunk), lambda n: (0, 0, n + first))] * len(weights)
        + [
            pl.BlockSpec((sources * toks, shared.shape[1]), lambda n: (half, 0)),
            pl.BlockSpec((shared.shape[1], chunk), lambda n: (0, n + first)),
        ]
    )
    operands = [slots, *deltas, *weights, shared, shared_weight]
    if score is not None:
        in_specs.append(pl.BlockSpec((experts, slot_rows // 2, lanes), lambda n: (0, half, 0)))
        operands.append(score)
    if other is not None:
        in_specs.append(whole(other))
        operands.append(other)
    out = jax.ShapeDtypeStruct((sources // outputs, toks, size + lanes), bf16)
    return pl.pallas_call(
        functools.partial(
            return_kernel, (len(deltas), score is not None, other is not None, outputs, steps)
        ),
        grid=(steps,),
        in_specs=in_specs,
        out_specs=[whole(out)] * outputs,
        out_shape=[out] * outputs,
        scratch_shapes=[
            pltpu.VMEM((sources, experts * CAP, toks), bf16),
            pltpu.VMEM((sources, experts * CAP, chunk), bf16),
        ],
        compiler_params=params(VMEM),
        cost_estimate=cost(
            2 * experts * slot_rows // 2 * size * (hidden * len(deltas) + toks)
            + 2 * sources * toks * size * shared.shape[1],
            2 * size * (experts * hidden * len(deltas) + sources * toks),
        ),
    )(*operands)


def expert_grads(rows, grads, act, gate_delta, up_delta):
    experts, slot_rows, width = rows.shape
    hidden = act.shape[2]

    def per_expert(array):
        return pl.BlockSpec((1,) + array.shape[1:], lambda e: (e, 0, 0))

    out = jax.ShapeDtypeStruct((experts, hidden, width), f32)
    return pl.pallas_call(
        expert_grad_kernel,
        grid=(experts,),
        in_specs=[per_expert(a) for a in (rows, grads, act, gate_delta, up_delta)],
        out_specs=[per_expert(out)] * 3,
        out_shape=[out] * 3,
        compiler_params=params(VMEM),
        cost_estimate=cost(
            6 * experts * slot_rows * width * hidden,
            experts * (4 * slot_rows * width + 12 * hidden * width),
        ),
    )(rows, grads, act, gate_delta, up_delta)


def shared_grads(src, tensor, parts, blocks, grads, delta, act, cols):
    count = grads.shape[0]
    toks, width = blocks[0].shape
    out = jax.ShapeDtypeStruct((count, 3 * cols, width // count), bf16)
    return pl.pallas_call(
        functools.partial(shared_grad_kernel, count, parts),
        grid_spec=pltpu.PrefetchScalarGridSpec(
            num_scalar_prefetch=2,
            grid=(count,),
            in_specs=[
                pl.BlockSpec((toks, delta.shape[1]), lambda s, src, t: (s, 0)),
                pl.BlockSpec((toks, act.shape[1]), lambda s, src, t: (s, 0)),
                pl.BlockSpec((1, toks, width), lambda s, src, t: (src[s], 0, 0)),
            ]
            + [ANYWHERE] * count,
            out_specs=whole(out),
            scratch_shapes=[
                pltpu.VMEM((count, toks, width), bf16),
                pltpu.VMEM((toks, width), bf16),
                pltpu.VMEM((delta.shape[1], width), f32),
                pltpu.VMEM((act.shape[1], width), f32),
                pltpu.SemaphoreType.DMA((count,)),
            ],
        ),
        out_shape=out,
        compiler_params=params(VMEM),
        cost_estimate=cost(
            2 * count * toks * width * (delta.shape[1] + act.shape[1]), 4 * count * toks * width
        ),
    )(src, tensor, delta, act, grads, *blocks)


def single(kernel, outs, operands, scalars=(), scratch=(), flops=0, transcendentals=0):
    return pl.pallas_call(
        kernel,
        grid_spec=pltpu.PrefetchScalarGridSpec(
            num_scalar_prefetch=len(scalars),
            grid=(1,),
            in_specs=[whole(a) for a in operands],
            out_specs=[whole(o) for o in outs],
            scratch_shapes=list(scratch),
        ),
        out_shape=list(outs),
        compiler_params=params(VMEM),
        cost_estimate=cost(flops, sum(a.size * a.dtype.itemsize for a in operands), transcendentals),
    )(*scalars, *operands)


def shape(dtype, *sizes):
    return jax.ShapeDtypeStruct(sizes, dtype)


def on_device(
    tokens,
    cotangent,
    attn_gain,
    q_weight,
    kv_down,
    k_rope_weight,
    kv_gain,
    kv_up,
    o_weight,
    ffn_gain,
    router_weight,
    expert_ids,
    expert_gate,
    expert_up,
    expert_down,
    shared_gate,
    shared_up,
    shared_down,
):
    n_t = lax.axis_size("tensor")
    n_d = lax.axis_size("dp")
    half = n_d // 2
    t_index = lax.axis_index("tensor")
    d_index = lax.axis_index("dp")
    toks, width = tokens.shape
    own_toks = toks // n_t
    rows_d = width // n_d
    q_cols = q_weight.shape[1]
    heads = q_cols // (HD + RD)
    experts_all = router_weight.shape[1]
    experts = expert_gate.shape[0]
    cosines, sines = rope_tables()
    order = partner_order()
    src = d_index.astype(jnp.int32) ^ order
    sources = [src[i] for i in range(n_d)]
    lat_cols = kv_down.shape[1]
    lat_rank = kv_up.shape[0]
    rope_cols = k_rope_weight.shape[1]
    narrow_cols = lat_cols + rope_cols
    expert_gate_t = expert_gate.transpose(0, 2, 1)
    expert_up_t = expert_up.transpose(0, 2, 1)

    tokens_p = by_partner(tokens, "tensor", 0)
    tokens_own = tokens_p[0].astype(f32)
    cot_own = block_at(cotangent, t_index, own_toks, 0).astype(f32)
    cot_all = lax.all_gather(cotangent, "dp")
    tensor = t_index.astype(jnp.int32).reshape(1)
    ids = reorder(expert_ids, "tensor", 0)
    every = jnp.arange(experts_all, dtype=jnp.int32)
    member = jnp.any(ids.T[:, None, :] == every[None, :, None], axis=0)
    before = (jnp.arange(toks)[:, None] < jnp.arange(toks)[None, :]).astype(bf16)
    rank = dot(member.astype(bf16), before)
    slots_own = jnp.where(member, rank, -1.0).astype(bf16)
    slots = jnp.stack([block_at(b, d_index, experts, 0) for b in gather_dp(slots_own)]).astype(
        jnp.int32
    )
    router_t = jnp.roll(router_weight.T, -d_index * experts, axis=0)
    router_parts = []
    rest = router_t
    for _ in range(3):
        part = lax.reduce_precision(rest, 8, 7)
        router_parts.append(part.astype(bf16))
        rest = rest - part
    router_parts = jnp.concatenate(router_parts, axis=0)
    shared_cols = shared_down.shape[0] // n_d
    shared_pad = -shared_cols % LANES
    shared_gate_t, shared_up_t, shared_out = [
        jnp.pad(block_at(w, d_index, shared_cols, 0), ((0, shared_pad), (0, 0)))
        for w in (shared_gate.T, shared_up.T, shared_down)
    ]
    shared_in = jnp.concatenate([shared_gate_t, shared_up_t], axis=0)
    grad_rows, shared_dact = pick_grads(src, tensor, n_t, slots, cot_all, shared_out)

    kv_up_p = reorder(kv_up, "tensor", 0)
    kv_gain_p = reorder(kv_gain, "tensor", 0)[None]
    rope_t = k_rope_weight.T
    rope_place = (
        (t_index ^ jnp.arange(n_t)[:, None, None]) * rope_cols + jnp.arange(rope_cols)[None, :, None]
        == jnp.arange(LANES)
    ).astype(bf16).reshape(RD, LANES)
    normed, inv_first, narrow_own = single(
        normed_kernel,
        [shape(bf16, toks, width), shape(f32, toks, 1), shape(bf16, toks, narrow_cols)],
        [tokens, attn_gain[None], kv_down, rope_t],
        flops=2 * toks * width * narrow_cols,
    )
    narrow_blocks = share(narrow_own, "tensor")
    query = single(
        query_kernel,
        [shape(bf16, toks, heads * HEAD)],
        [normed, q_weight, cosines, sines],
        flops=2 * toks * width * q_cols,
    )[0]
    results = single(
        functools.partial(attention_kernel, n_t),
        [shape(f32 if r == 0 else bf16, own_toks, width) for r in range(n_t)]
        + [
            shape(bf16, toks, heads * VD),
            shape(bf16, toks, lat_rank),
            shape(bf16, toks, lat_rank),
            shape(f32, toks, 1),
            shape(bf16, toks, heads * KV),
            shape(bf16, toks, LANES),
            shape(f32, toks, LANES),
        ],
        [query, cosines, sines, rope_place, kv_gain_p, kv_up_p, o_weight, *narrow_blocks],
        scalars=[tensor],
        scratch=[pltpu.VMEM((toks, heads * VD), bf16)],
        flops=2 * toks * heads * (KV * lat_rank + 2 * HEAD * toks + VD * width),
        transcendentals=2 * heads * toks * toks,
    )
    attn_part = results[:n_t]
    attended_p, latent, latent_normed, inv_latent, key_value, rope_rot, lse = results[n_t:]
    attn_sum = total(trade(attn_part, "tensor"))
    hidden_one = tokens_own + attn_sum
    ffn_normed_f, inv_second = rms_norm(hidden_one, ffn_gain)
    ffn_own = ffn_normed_f.astype(bf16)
    ffn_block = jnp.concatenate(share(ffn_own, "tensor"), axis=0)
    near_blocks = gather_chips(ffn_block)
    near_blocks = near_blocks[:-1] + [after(near_blocks[-1], grad_rows)]
    far_blocks = [swap(block, "dp", 1) for block in near_blocks]
    blocks = far_blocks + near_blocks

    results = []
    for side, first, start, stop in (
        (near_blocks, half, 0, half - 1),
        (far_blocks, 0, 0, half - 1),
        (near_blocks, half, half - 1, half),
        (far_blocks, 0, half - 1, half),
    ):
        results = pick_rows(
            side[start:stop], first + start, slots, router_parts, shared_in, shared_dact, experts_all,
            results,
        )
    rows, gate, shared_act, shared_delta = results
    lanes = -(-2 * experts_all // LANES) * LANES
    first = (d_index * experts).astype(jnp.int32).reshape(1)
    act, gate_delta, up_delta, score = expert_hidden(
        first, rows, grad_rows, gate, expert_gate_t, expert_up_t, expert_down, lanes
    )

    def send_back(sum_here):
        return trade(
            [sum_here[k * own_toks : (k + 1) * own_toks].astype(bf16) for k in range(n_t)], "tensor"
        )

    pieces = 2
    size = width // pieces
    deltas, delta_weights = [gate_delta, up_delta], [expert_gate_t, expert_up_t]
    others = [
        return_rows(
            0, slots, deltas, delta_weights, shared_delta, shared_in,
            score if i == pieces - 1 else None, i * size, size, None,
        )[0]
        for i in range(pieces)
    ]
    others = [swap(other, "dp", 1) for other in others]
    mine = [
        return_rows(
            1, slots, deltas, delta_weights, shared_delta, shared_in,
            score if i == pieces - 1 else None, i * size, size, others[i],
        )
        for i in range(pieces)
    ]
    sums, arrivals = sum_chips(mine)

    other = return_rows(
        0, slots, [after(act, mine)], [expert_down], shared_act, shared_out, None, 0, width, None
    )[0]
    other = swap(other, "dp", 1)
    out_pair = return_rows(
        1, slots, [act], [expert_down], shared_act, shared_out, None, 0, width,
        after(other, arrivals[0][0]),
    )
    shared_rows = shared_cols + -shared_cols % 16
    sums[0] = after(sums[0], out_pair)
    back_sums = [total(send_back(s)) for s in sums]
    back_sum = jnp.concatenate(back_sums[:-1] + [back_sums[-1][:, :size]], axis=1)
    score_sum = back_sums[-1][:, size:]
    shared_all = shared_grads(
        src, tensor, n_t, blocks, cot_all, *after((shared_delta, shared_act), arrivals[-1]), shared_rows
    )
    out_pair = after(out_pair, arrivals[-1])
    out_sums, out_arrivals = sum_chips([out_pair])
    out_here = out_sums[0]

    shared_all = lax.all_to_all(shared_all, "dp", 0, 0, tiled=True).astype(f32)
    shared_gate_grad, shared_up_grad, shared_down_grad = [
        shared_all[:, i * shared_rows : i * shared_rows + shared_cols].reshape(-1, rows_d)
        for i in range(3)
    ]

    logits = jnp.dot(ffn_own.astype(f32), router_weight, precision=lax.Precision.HIGHEST)
    router_prob = jax.nn.softmax(logits, axis=-1)
    prob_grad = score_sum[:, :experts_all] + score_sum[:, lanes // 2 : lanes // 2 + experts_all]
    logit_grad = (
        router_prob * (prob_grad - jnp.sum(router_prob * prob_grad, axis=-1, keepdims=True))
    ).astype(bf16)
    ffn_normed_grad = back_sum + jnp.dot(
        logit_grad.astype(f32), router_weight.T, precision=lax.Precision.HIGHEST
    )
    hidden_norm_grad, ffn_gain_part = rms_back(ffn_normed_grad, hidden_one, inv_second, ffn_gain)
    hidden_grad = cot_own + hidden_norm_grad
    flat_logits = logit_grad.reshape(-1, width)
    flat = flat_logits.shape[0]
    extra = jnp.concatenate(
        [
            flat_logits,
            ffn_gain_part.astype(bf16)[None],
            jnp.zeros((-(flat + 1) % 16, width), bf16),
        ],
        axis=0,
    )
    message = jnp.concatenate([hidden_grad.astype(bf16), extra], axis=0)
    message = after(message, out_arrivals[0])
    shared_grads_t = after(share(message, "tensor"), out_arrivals[-1])
    expert_gate_grad, expert_up_grad, expert_down_grad = expert_grads(
        rows, grad_rows, *after((act, gate_delta, up_delta), message)
    )
    out_sum = total(send_back(after(out_here, shared_grads_t)))
    output_own = (hidden_one + out_sum).astype(bf16)

    lat_rows = lat_rank // n_d
    results = single(
        functools.partial(attention_back_kernel, n_t),
        [shape(f32 if r == 0 else bf16, toks, narrow_cols) for r in range(n_t)]
        + [
            shape(bf16, toks, q_cols),
            shape(bf16, half, lat_rows, heads * KV),
            shape(bf16, half, lat_rows, heads * KV),
        ],
        [
            query, key_value, rope_rot, lse, latent, latent_normed, inv_latent, cosines, sines,
            rope_place, kv_gain_p, kv_up_p, o_weight, *shared_grads_t,
        ],
        scalars=[tensor, src],
        scratch=[
            pltpu.VMEM((toks, heads * VD), bf16),
            pltpu.VMEM((toks, q_cols), bf16),
            pltpu.VMEM((toks, heads * KV), bf16),
            pltpu.VMEM((toks, narrow_cols), f32),
            pltpu.VMEM((lat_rank, heads * KV), f32),
        ],
        flops=2 * toks * heads * (2 * KV * lat_rank + 5 * HEAD * toks + VD * width),
        transcendentals=heads * toks * toks,
    )
    latent_parts = results[:n_t]
    query_grad_p, kv_up_far, kv_up_near = results[n_t:]
    results = single(
        functools.partial(normed_back_kernel, n_t),
        [shape(f32 if r == 0 else bf16, own_toks, width) for r in range(n_t)]
        + [shape(bf16, toks, narrow_cols)],
        [query_grad_p, q_weight, kv_down, rope_t, *trade(latent_parts, "tensor")],
        scalars=[tensor],
        scratch=[pltpu.VMEM((toks, narrow_cols), f32)],
        flops=2 * toks * width * (q_cols + narrow_cols),
    )
    normed_part, narrow_p = results[:n_t], results[n_t]
    output_own = after(output_own, normed_part)
    output = reorder(jnp.concatenate(share(output_own, "tensor"), axis=0), "tensor", 0)
    normed_grad = total(trade(normed_part, "tensor"))
    inv_first_own = block_at(inv_first, t_index, own_toks, 0)
    input_norm_grad, _ = rms_back(normed_grad, tokens_own, inv_first_own, attn_gain)
    input_grad = hidden_grad + input_norm_grad

    logit_p = jnp.concatenate(
        [b[own_toks : own_toks + flat].reshape(own_toks, experts_all) for b in shared_grads_t], axis=0
    )
    gain_part = total([b[own_toks + flat] for b in shared_grads_t])[None]
    out_cols = attended_p.shape[1]
    height = out_cols + experts_all + 16
    columns = sum_dp(
        *single(
            functools.partial(columns_grad_kernel, n_t, flat),
            [shape(bf16, half, height, rows_d)] * 2,
            [attended_p, logit_p, ffn_block, gain_part, *shared_grads_t],
            scalars=[src],
            scratch=[pltpu.VMEM((toks, width), bf16)],
            flops=2 * toks * width * height,
        )
    )
    o_weight_grad = columns[:out_cols]
    device_rows = width // (n_d * n_t)
    router_grad = block_at(
        columns[out_cols : out_cols + experts_all], t_index, device_rows, 1
    ).T
    ffn_gain_grad = block_at(columns[out_cols + experts_all], t_index, device_rows, 0)

    def rows_grad(left, right):
        return sum_dp(
            *single(
                rows_grad_kernel,
                [shape(bf16, half, rows_d, right.shape[1])] * 2,
                [left, right],
                scalars=[src],
                flops=2 * toks * width * right.shape[1],
            )
        )

    normed_p = reorder(normed, "tensor", 0)
    q_weight_grad = rows_grad(normed_p, query_grad_p)
    narrow_grad = rows_grad(normed_p, narrow_p)
    kv_down_grad = narrow_grad[:, :lat_cols]
    k_rope_grad = narrow_grad[:, lat_cols:]
    kv_up_grad = sum_dp(kv_up_far, kv_up_near)

    attn_gain_part = jnp.sum(
        block_at(q_weight, d_index, rows_d, 0).astype(f32) * q_weight_grad, axis=1
    ) + jnp.sum(
        block_at(kv_down, d_index, rows_d, 0).astype(f32) * kv_down_grad, axis=1
    ) + jnp.sum(
        block_at(k_rope_weight, d_index, rows_d, 0).astype(f32) * k_rope_grad, axis=1
    )
    attn_gain_part = attn_gain_part / block_at(attn_gain, d_index, rows_d, 0)
    kv_gain_part = jnp.sum(
        block_at(kv_up, d_index, lat_rows, 0).astype(f32) * kv_up_grad, axis=1
    ) / block_at(kv_gain, d_index, lat_rows, 0)
    gains = jnp.concatenate(
        [attn_gain_part.reshape(n_t, 1, -1), kv_gain_part.reshape(n_t, 1, -1)], axis=2
    )
    gains = total(trade([b[0] for b in by_partner(gains, "tensor", 0)], "tensor"))[0]
    attn_gain_grad = gains[:device_rows]
    kv_gain_grad = gains[device_rows:]

    return (
        output,
        input_grad,
        attn_gain_grad,
        q_weight_grad,
        kv_down_grad,
        k_rope_grad,
        kv_gain_grad,
        kv_up_grad,
        o_weight_grad,
        ffn_gain_grad,
        router_grad,
        shared_gate_grad.T,
        shared_up_grad.T,
        shared_down_grad,
        expert_gate_grad.transpose(0, 2, 1),
        expert_up_grad.transpose(0, 2, 1),
        expert_down_grad,
    )


def solution(mesh):
    in_specs = (
        P("dp", None),
        P("dp", None),
        P(),
        P(None, "tensor"),
        P(None, "tensor"),
        P(None, "tensor"),
        P(),
        P(None, "tensor"),
        P("tensor", None),
        P(),
        P(),
        P("dp", None),
        P("dp", None, "tensor"),
        P("dp", None, "tensor"),
        P("dp", "tensor", None),
        P(None, "tensor"),
        P(None, "tensor"),
        P("tensor", None),
    )
    out_specs = (
        P("dp", None),
        P(("dp", "tensor"), None),
        P(("dp", "tensor")),
        P("dp", "tensor"),
        P("dp", "tensor"),
        P("dp", "tensor"),
        P(("dp", "tensor")),
        P("dp", "tensor"),
        P("tensor", "dp"),
        P(("dp", "tensor")),
        P(("dp", "tensor"), None),
        P("dp", "tensor"),
        P("dp", "tensor"),
        P("tensor", "dp"),
        P("dp", None, "tensor"),
        P("dp", None, "tensor"),
        P("dp", "tensor", None),
    )
    return jax.shard_map(
        on_device, mesh=mesh, in_specs=in_specs, out_specs=out_specs, check_vma=False
    )
```

time: 690 us -> 521 us (0.76)
  local copies, waits for them, and re-layouts: 120 us -> 32.3 us
  waiting for transfers between devices: 220 us -> 150 us
  Pallas kernels: 118 us -> 181 us
  starting transfers between devices: 137 us -> 86 us
  matrix products: 37.4 us -> 2 us
  between operations: 3.38 us -> 15.1 us
    ppermute x125 -> x48, waiting for transfers between devices: 220 us -> 95.6 us  [swap(): return lax.ppermute(array, axis, [(i, i ^ bits) for i in range(count)])]
    unnamed x357 -> x96, local copies, waits for them, and re-layouts: 80.8 us -> 12.1 us
    ppermute x125 -> x48, starting transfers between devices: 129 us -> 60.9 us  [swap(): return lax.ppermute(array, axis, [(i, i ^ bits) for i in range(count)])]
    pallas_call x10 -> x20, Pallas kernels: 76 us -> 142 us  [the longest x6 51.6 us: return_rows(): pl.pallas_call(functools.partial(return_kernel, (len(deltas), score is no...]
    ppermute x0 -> x20, waiting for transfers between devices: none -> 53.4 us  [swap_chips(): lax.ppermute(array, 'dp', [(i, i ^ chip_bits(i % 2)[step]) for i in range...]
    dot_general x13 -> x0, matrix products: 26.6 us -> none  [the longest x4 8.41 us: dot_tn(): lax.dot_general(a, b, (((0,), (0,)), ((), ())), preferred_element_type=f32)]
    ppermute x0 -> x20, starting transfers between devices: none -> 21.4 us  [swap_chips(): lax.ppermute(array, 'dp', [(i, i ^ chip_bits(i % 2)[step]) for i in range...]
    concatenate x7 -> x2, local copies, waits for them, and re-layouts: 13.7 us -> 0.8 us  [the longest x1 0.72 us: on_device(): jnp.concatenate(share(output_own, 'tensor'), axis=0)]
  transfers between devices with their start and end apart: 127 -> 70, of which waited for: 47 -> 26; matrix products, arithmetic and copies ran while one was open for 23% -> 13% of each run, Pallas kernels for 13% -> 27%
where the time goes in v2:
time: 521 us; the launch traced here: 514 us
  Pallas kernels  181 us (35%)
  waiting for transfers between devices  150 us (29%)
  starting transfers between devices  86 us (17%)
  other arithmetic  47.1 us (9%)
  local copies, waits for them, and re-layouts  32.3 us (6%)
  between operations  15.1 us (3%)
    ppermute x48, waiting for transfers between devices, swap(): return lax.ppermute(array, axis, [(i, i ^ bits) for i in range(count)])  95.6 us
    ppermute x48, starting transfers between devices, swap(): return lax.ppermute(array, axis, [(i, i ^ bits) for i in range(count)])  60.9 us
    ppermute x20, waiting for transfers between devices, swap_chips(): lax.ppermute(array, 'dp', [(i, i ^ chip_bits(i % 2)[step]) for i in range...  53.4 us
    pallas_call x6, Pallas kernels, return_rows(): pl.pallas_call(functools.partial(return_kernel, (len(deltas), score is no...  51.6 us
    pallas_call x8, Pallas kernels, single(): pl.pallas_call(kernel, grid_spec=pltpu.PrefetchScalarGridSpec(num_scalar_...  40.9 us
    pallas_call x4, Pallas kernels, pick_rows(): pl.pallas_call(functools.partial(pick_kernel, count, experts_all, len(res...  24.2 us
    ppermute x20, starting transfers between devices, swap_chips(): lax.ppermute(array, 'dp', [(i, i ^ chip_bits(i % 2)[step]) for i in range...  21.4 us
    pallas_call x1, Pallas kernels, expert_grads(): pl.pallas_call(expert_grad_kernel, grid=(experts,), in_specs=[per_expert(...  19.9 us
  transfers between devices with their start and end apart: 70, of which 26 were waited for; matrix products, arithmetic and copies ran while one was open for 13% of the time, Pallas kernels for 27%

profile of v2, /device:TPU:0, one launch (start us, length us, event | category | flops | bytes accessed | tf_op | source)
XLA Modules:
  0.0 513.6 jit_solution(1468912557341746975)
XLA Ops:
  38.3 8.7 %collective-permute-done.3 = bf16[64,2048]{1,0:T(8,128)(2,1)S(1)} collective-permute-done((bf16[64,2048]{1,0:T(8,128)(2,1)}, bf16[64,2048]{1,0:T(8,128)(2,1)S(1)}, u32[]{:S(2)}, u32[]{:S(2)}) %collective-permute-start.3) | collective-permute-done | bytes 262176 | tf_op jit(solution)/shard_map/ppermute | solution.py:74
  47.0 9.6 %collective-permute-done.4 = bf16[64,2048]{1,0:T(8,128)(2,1)S(1)} collective-permute-done((bf16[64,2048]{1,0:T(8,128)(2,1)}, bf16[64,2048]{1,0:T(8,128)(2,1)S(1)}, u32[]{:S(2)}, u32[]{:S(2)}) %collective-permute-start.4) | collective-permute-done | bytes 262176 | tf_op jit(solution)/shard_map/ppermute | solution.py:74
  65.8 11.3 %collective-permute-done.14 = bf16[64,2048]{1,0:T(8,128)(2,1)} collective-permute-done((bf16[64,2048]{1,0:T(8,128)(2,1)}, bf16[64,2048]{1,0:T(8,128)(2,1)}, u32[]{:S(2)}, u32[]{:S(2)}) %collective-permute-start.14) | collective-permute-done | bytes 262176 | tf_op jit(solution)/shard_map/ppermute | solution.py:74
  96.2 16.1 %collective-permute-done.11 = bf16[32,256]{1,0:T(8,128)(2,1)S(1)} collective-permute-done((bf16[32,256]{1,0:T(8,128)(2,1)S(1)}, bf16[32,256]{1,0:T(8,128)(2,1)S(1)}, u32[]{:S(2)}, u32[]{:S(2)}) %collective-permute-start.11) | collective-permute-done | bytes 16416 | tf_op jit(solution)/shard_map/ppermute | solution.py:91
  116.7 12.2 %shard_map.335 = (bf16[4,512,2048]{2,1,0:T(8,128)(2,1)}, f32[2048,128]{1,0:T(8,128)}) custom-call(s32[8]{0:T(128)} %add_xor_fusion.src_ref, s32[1]{0:T(128)} %bitcast.tensor_ref, s32[8,4,256]{2,1,0:T(4,128)} %convert_element_type.280.slots_ref, bf16[8,256,2048]{2,1,0:T(8,128)(2,1)} %bitcast.125, bf16[128,2048]{1,0:T(8,128)(2,1)} %pad.12.down_ref.refs_3_), custom_call_target="tpu_custom_call" | custom-call | flops 3221225472 | bytes 16777216 | tf_op jit(solution)/shard_map/pallas_call | solution.py:589
  132.5 7.3 %shard_map.336 = (bf16[4,512,2048]{2,1,0:T(8,128)(2,1)}, f32[4,512,128]{2,1,0:T(8,128)}, bf16[2048,128]{1,0:T(8,128)(2,1)}, bf16[2048,256]{1,0:T(8,128)(2,1)}) custom-call(s32[8,4,256]{2,1,0:T(4,128)} %convert_element_type.280.slots_ref, bf16[96,2048]{1,0:T(8,128)(2,1)} %pad_maximum_fusion.4.router_ref, bf16[256,2048]{1,0:T(8,128)(2,1)} %fusion.5.weights_ref.refs_5_, ...), custom_call_target="tpu_custom_call" | custom-call | flops 1912602624 | bytes 6291456 | tf_op jit(solution)/shard_map/pallas_call | solution.py:622
  140.8 7.3 %shard_map.337 = (bf16[4,512,2048]{2,1,0:T(8,128)(2,1)}, f32[4,512,128]{2,1,0:T(8,128)}, bf16[2048,128]{1,0:T(8,128)(2,1)}, bf16[2048,256]{1,0:T(8,128)(2,1)}) custom-call(s32[8,4,256]{2,1,0:T(4,128)} %convert_element_type.280.slots_ref, ...), custom_call_target="tpu_custom_call", output_to_operand_aliasing={{0}: (7, {}), {1}: (8, {}), {2}: (9, {}), {3}: (10, {})} | custom-call | flops 1912602624 | bytes 6291456 | tf_op jit(solution)/shard_map/pallas_call | solution.py:622
  157.8 19.8 %shard_map.340 = (bf16[4,512,352]{2,1,0:T(8,128)(2,1)}, bf16[4,512,352]{2,1,0:T(8,128)(2,1)}, bf16[4,512,352]{2,1,0:T(8,128)(2,1)}, bf16[4,512,128]{2,1,0:T(8,128)(2,1)}) custom-call(s32[1]{0:T(128)} %bitcast.13.first_ref, bf16[4,512,2048]{2,1,0:T(8,128)(2,1)} %get-tuple-element.119.rows_ref, bf16[4,512,2048]{2,1,0:T(8,128)(2,1)} %get-tuple-element.105.grads_ref, ...), custom_call_target="tpu_custom_call" | custom-call | flops 8858370048 | bytes 34078720 | tf_op jit(solution)/shard_map/pallas_call | solution.py:666
  177.6 8.0 %shard_map.343 = bf16[4,256,1152]{2,1,0:T(8,128)(2,1)} custom-call(s32[8,4,256]{2,1,0:T(4,128)} %convert_element_type.280.slots_ref, bf16[4,512,352]{2,1,0:T(8,128)(2,1)} %get-tuple-element.174.refs_0_.gate_delta_ref, bf16[4,512,352]{2,1,0:T(8,128)(2,1)} %get-tuple-element.175.refs_1_.up_delta_ref, bf16[4,352,2048]{2,1,0:T(8,128)(2,1)} %bitcast.116, ...), custom_call_target="tpu_custom_call" | custom-call | flops 2550136832 | bytes 7864320 | tf_op jit(solution)/shard_map/pallas_call | solution.py:708
  185.9 7.5 %shard_map.341 = bf16[4,256,1024]{2,1,0:T(8,128)(2,1)} custom-call(s32[8,4,256]{2,1,0:T(4,128)} %convert_element_type.280.slots_ref, bf16[4,512,352]{2,1,0:T(8,128)(2,1)} %get-tuple-element.174.refs_0_.gate_delta_ref, bf16[4,512,352]{2,1,0:T(8,128)(2,1)} %get-tuple-element.175.refs_1_.up_delta_ref, bf16[4,352,2048]{2,1,0:T(8,128)(2,1)} %bitcast.117, ...), custom_call_target="tpu_custom_call" | custom-call | flops 2550136832 | bytes 7864320 | tf_op jit(solution)/shard_map/pallas_call | solution.py:708
  197.9 8.0 %shard_map.342 = (bf16[2,256,1024]{2,1,0:T(8,128)(2,1)}, bf16[2,256,1024]{2,1,0:T(8,128)(2,1)}) custom-call(s32[8,4,256]{2,1,0:T(4,128)} %convert_element_type.280.slots_ref, bf16[4,512,352]{2,1,0:T(8,128)(2,1)} %get-tuple-element.174.refs_0_.gate_delta_ref, bf16[4,512,352]{2,1,0:T(8,128)(2,1)} %get-tuple-element.175.refs_1_.up_delta_ref, ...), custom_call_target="tpu_custom_call" | custom-call | flops 2550136832 | bytes 7864320 | tf_op jit(solution)/shard_map/pallas_call | solution.py:708
  208.5 9.0 %shard_map.344 = (bf16[2,256,1152]{2,1,0:T(8,128)(2,1)}, bf16[2,256,1152]{2,1,0:T(8,128)(2,1)}) custom-call(s32[8,4,256]{2,1,0:T(4,128)} %convert_element_type.280.slots_ref, bf16[4,512,352]{2,1,0:T(8,128)(2,1)} %get-tuple-element.174.refs_0_.gate_delta_ref, bf16[4,512,352]{2,1,0:T(8,128)(2,1)} %get-tuple-element.175.refs_1_.up_delta_ref, ...), custom_call_target="tpu_custom_call" | custom-call | flops 2550136832 | bytes 7864320 | tf_op jit(solution)/shard_map/pallas_call | solution.py:708
  218.3 9.1 %shard_map.345 = bf16[4,256,2048]{2,1,0:T(8,128)(2,1)} custom-call(s32[8,4,256]{2,1,0:T(4,128)} %convert_element_type.280.slots_ref, bf16[4,512,352]{2,1,0:T(8,128)(2,1)} %get-tuple-element.173.refs_0_.act_ref, bf16[4,352,2048]{2,1,0:T(8,128)(2,1)} %refs_1_.3, bf16[2048,128]{1,0:T(8,128)(2,1)} %get-tuple-element.172.refs_2_.act_ref, ...), custom_call_target="tpu_custom_call" | custom-call | flops 3087007744 | bytes 9961472 | tf_op jit(solution)/shard_map/pallas_call | solution.py:708
  254.8 12.7 %shard_map.352 = bf16[8,288,256]{2,1,0:T(8,128)(2,1)} custom-call(s32[8]{0:T(128)} %add_xor_fusion.src_ref, s32[1]{0:T(128)} %bitcast.tensor_ref, bf16[2048,256]{1,0:T(8,128)(2,1)} %get-tuple-element.171.refs_4_.delta_ref, bf16[2048,128]{1,0:T(8,128)(2,1)} %get-tuple-element.172.refs_2_.act_ref, bf16[8,256,2048]{2,1,0:T(8,128)(2,1)} %bitcast.126, ...), custom_call_target="tpu_custom_call" | custom-call | flops 3221225472 | bytes 16777216 | tf_op jit(solution)/shard_map/pallas_call | solution.py:755
  272.3 10.1 %shard_map.346 = (bf16[2,256,2048]{2,1,0:T(8,128)(2,1)}, bf16[2,256,2048]{2,1,0:T(8,128)(2,1)}) custom-call(s32[8,4,256]{2,1,0:T(4,128)} %convert_element_type.280.slots_ref, bf16[4,512,352]{2,1,0:T(8,128)(2,1)} %get-tuple-element.173.refs_0_.act_ref, bf16[4,352,2048]{2,1,0:T(8,128)(2,1)} %refs_1_.3, bf16[2048,128]{1,0:T(8,128)(2,1)} %get-tuple-element.172.refs_2_.act_ref, ...), custom_call_target="tpu_custom_call" | custom-call | flops 3087007744 | bytes 9961472 | tf_op jit(solution)/shard_map/pallas_call | solution.py:708
  291.5 7.3 %collective-permute-done.33 = bf16[64,1024]{1,0:T(8,128)(2,1)S(1)} collective-permute-done((bf16[64,1024]{1,0:T(8,128)(2,1)}, bf16[64,1024]{1,0:T(8,128)(2,1)S(1)}, u32[]{:S(2)}, u32[]{:S(2)}) %collective-permute-start.33) | collective-permute-done | bytes 131104 | tf_op jit(solution)/shard_map/ppermute | solution.py:74
  303.3 7.1 %collective-permute-done.30 = bf16[2,256,2048]{2,1,0:T(8,128)(2,1)} collective-permute-done((bf16[2,256,2048]{2,1,0:T(8,128)(2,1)}, bf16[2,256,2048]{2,1,0:T(8,128)(2,1)}, u32[]{:S(2)}, u32[]{:S(2)}) %collective-permute-start.30) | collective-permute-done | bytes 2097184 | tf_op jit(solution)/shard_map/ppermute | solution.py:91
  319.2 8.0 %collective-permute-done.39.refs_2_ = bf16[80,2048]{1,0:T(8,128)(2,1)S(1)} collective-permute-done((bf16[80,2048]{1,0:T(8,128)(2,1)S(1)}, bf16[80,2048]{1,0:T(8,128)(2,1)S(1)}, u32[]{:S(2)}, u32[]{:S(2)}) %collective-permute-start.39) | collective-permute-done | bytes 327712 | tf_op jit(solution)/shard_map/ppermute | solution.py:74
  327.2 19.9 %shard_map.353 = (f32[4,352,2048]{2,1,0:T(8,128)}, f32[4,352,2048]{2,1,0:T(8,128)}, f32[4,352,2048]{2,1,0:T(8,128)}) custom-call(bf16[4,512,2048]{2,1,0:T(8,128)(2,1)} %get-tuple-element.119.rows_ref, bf16[4,512,2048]{2,1,0:T(8,128)(2,1)} %get-tuple-element.105.grads_ref, bf16[4,512,352]{2,1,0:T(8,128)(2,1)} %get-tuple-element.173.refs_0_.act_ref, ...), custom_call_target="tpu_custom_call" | custom-call | flops 8858370048 | bytes 51380224 | tf_op jit(solution)/shard_map/pallas_call | solution.py:737
  350.5 10.5 %shard_map.347 = (f32[256,144]{1,0:T(8,128)}, bf16[256,144]{1,0:T(8,128)(2,1)}, bf16[256,144]{1,0:T(8,128)(2,1)}, bf16[256,144]{1,0:T(8,128)(2,1)}, bf16[256,768...) custom-call(s32[1]{0:T(128)} %bitcast.tensor_ref, s32[8]{0:T(128)} %add_xor_fusion.src_ref, ...), custom_call_target="tpu_custom_call" | custom-call | flops 1744830464 | bytes 6507520 | tf_op jit(solution)/shard_map/pallas_call | solution.py:784
  380.1 9.1 %collective-permute-done.46.refs_3_ = bf16[256,144]{1,0:T(8,128)(2,1)S(1)} collective-permute-done((bf16[256,144]{1,0:T(8,128)(2,1)S(1)}, bf16[256,144]{1,0:T(8,128)(2,1)S(1)}, u32[]{:S(2)}, u32[]{:S(2)}) %collective-permute-start.46) | collective-permute-done | bytes 73760 | tf_op jit(solution)/shard_map/ppermute | solution.py:74
  398.2 10.4 %collective-permute-start.50 = (bf16[64,2048]{1,0:T(8,128)(2,1)}, bf16[64,2048]{1,0:T(8,128)(2,1)S(1)}, u32[]{:S(2)}, u32[]{:S(2)}) collective-permute-start(bf16[64,2048]{1,0:T(8,128)(2,1)} %get-tuple-element.156), channel_id=1, source_target_pairs={{0,1},{1,0},{2,3},{3,2},{4,5},{5,4},{6,7},{7,6},{8,9},{9,8},{10,11... | collective-permute-start | bytes 786440 | tf_op jit(solution)/shard_map/ppermute | solution.py:74
  419.4 10.7 %collective-permute-done.51 = bf16[64,2048]{1,0:T(8,128)(2,1)S(1)} collective-permute-done((bf16[64,2048]{1,0:T(8,128)(2,1)}, bf16[64,2048]{1,0:T(8,128)(2,1)S(1)}, u32[]{:S(2)}, u32[]{:S(2)}) %collective-permute-start.51) | collective-permute-done | bytes 262176 | tf_op jit(solution)/shard_map/ppermute | solution.py:74
  473.9 11.0 %collective-permute-done.54 = bf16[2,256,768]{2,1,0:T(8,128)(2,1)} collective-permute-done((bf16[2,256,768]{2,1,0:T(8,128)(2,1)}, bf16[2,256,768]{2,1,0:T(8,128)(2,1)}, u32[]{:S(2)}, u32[]{:S(2)}) %collective-permute-start.54) | collective-permute-done | bytes 786464 | tf_op jit(solution)/shard_map/ppermute | solution.py:91
  (347 shorter events, 247.9 us)
Async XLA Ops:
  7.2 109.5 %all-gather.3.cloned.1.call-start = ((), (), s32[]{:S(2)}) async-start(), calls=%async_computation.1 | async-start | bytes 9437184 | tf_op jit(solution)/shard_map/all_gather | solution.py:849
  34.9 21.7 %collective-permute-start.4 = (bf16[64,2048]{1,0:T(8,128)(2,1)}, bf16[64,2048]{1,0:T(8,128)(2,1)S(1)}, u32[]{:S(2)}, u32[]{:S(2)}) collective-permute-start(bf16[64,2048]{1,0:T(8,128)(2,1)} %get-tuple-element.102), channel_id=1, source_target_pairs={{0,2},{1,3},{2,0},{3,1},{4,6},{5,7},{6,4},{7,5},{8,10},{9,11},{10,... | collective-permute-start | bytes 786440 | tf_op jit(solution)/shard_map/ppermute | solution.py:74
  87.8 26.2 %collective-permute-start.16 = (bf16[256,2048]{1,0:T(8,128)(2,1)}, bf16[256,2048]{1,0:T(8,128)(2,1)}, u32[]{:S(2)}, u32[]{:S(2)}) collective-permute-start(bf16[256,2048]{1,0:T(8,128)(2,1)} %pad_maximum_fusion.1.refs_0_.block_ref.refs_4_), channel_id=1, source_target_pairs={{0,8},{4,20},{8,0},{12,28},{16,24},{20,4},{24,16},{28,12},{1,9},{5... | collective-permute-start | bytes 3145736 | tf_op jit(solution)/shard_map/ppermute | solution.py:91
  91.2 25.5 %collective-permute-start.21 = (bf16[256,2048]{1,0:T(8,128)(2,1)}, bf16[256,2048]{1,0:T(8,128)(2,1)}, u32[]{:S(2)}, u32[]{:S(2)}) collective-permute-start(bf16[256,2048]{1,0:T(8,128)(2,1)} %pad_maximum_fusion.1.refs_0_.block_ref.refs_4_), channel_id=1, source_target_pairs={{0,16},{4,12},{8,24},{12,4},{16,0},{20,28},{24,8},{28,20},{1,17},{... | collective-permute-start | bytes 3145736 | tf_op jit(solution)/shard_map/ppermute | solution.py:91
  116.2 23.7 %collective-permute-start.19 = (bf16[256,2048]{1,0:T(8,128)(2,1)}, bf16[256,2048]{1,0:T(8,128)(2,1)S(1)}, u32[]{:S(2)}, u32[]{:S(2)}) collective-permute-start(bf16[256,2048]{1,0:T(8,128)(2,1)} %pad_maximum_fusion.1.refs_0_.block_ref.refs_4_), channel_id=1, source_target_pairs={{0,4},{4,0},{8,12},{12,8},{16,20},{20,16},{24,28},{28,24},{1,5},{5... | collective-permute-start | bytes 3145736 | tf_op jit(solution)/shard_map/ppermute | solution.py:74
  116.2 23.7 %collective-permute-start.20 = (bf16[256,2048]{1,0:T(8,128)(2,1)}, bf16[256,2048]{1,0:T(8,128)(2,1)}, u32[]{:S(2)}, u32[]{:S(2)}) collective-permute-start(bf16[256,2048]{1,0:T(8,128)(2,1)} %collective-permute-done.16.refs_1_.refs_5_), channel_id=1, source_target_pairs={{0,4},{4,0},{8,12},{12,8},{16,20},{20,16},{24,28},{28,24},{1,5},{5... | collective-permute-start | bytes 3145736 | tf_op jit(solution)/shard_map/ppermute | solution.py:74
  116.7 23.2 %collective-permute-start.22 = (bf16[256,2048]{1,0:T(8,128)(2,1)}, bf16[256,2048]{1,0:T(8,128)(2,1)}, u32[]{:S(2)}, u32[]{:S(2)}) collective-permute-start(bf16[256,2048]{1,0:T(8,128)(2,1)} %collective-permute-done.21.refs_2_.refs_6_), channel_id=1, source_target_pairs={{0,4},{4,0},{8,12},{12,8},{16,20},{20,16},{24,28},{28,24},{1,5},{5... | collective-permute-start | bytes 3145736 | tf_op jit(solution)/shard_map/ppermute | solution.py:74
  129.1 23.9 %collective-permute-start.18 = (bf16[256,2048]{1,0:T(8,128)(2,1)S(1)}, bf16[256,2048]{1,0:T(8,128)(2,1)}, u32[]{:S(2)}, u32[]{:S(2)}) collective-permute-start(bf16[256,2048]{1,0:T(8,128)(2,1)S(1)} %collective-permute-done.17.refs_0_.refs_7_), channel_id=1, source_target_pairs={{0,4},{4,0},{8,12},{12,8},{16,20},{20,16},{24,28},{28,24},{1,5},{5... | collective-permute-start | bytes 3145736 | tf_op jit(solution)/shard_map/ppermute | solution.py:74
  185.6 21.4 %collective-permute-start.24 = (bf16[4,256,1152]{2,1,0:T(8,128)(2,1)}, bf16[4,256,1152]{2,1,0:T(8,128)(2,1)S(1)}, u32[]{:S(2)}, u32[]{:S(2)}) collective-permute-start(bf16[4,256,1152]{2,1,0:T(8,128)(2,1)} %shard_map.343), channel_id=1, source_target_pairs={{0,4},{4,0},{8,12},{12,8},{16,20},{20,16},{24,28},{28,24},{1,5},{5... | collective-permute-start | bytes 7077896 | tf_op jit(solution)/shard_map/ppermute | solution.py:74
  205.9 24.4 %collective-permute-start.26 = (bf16[2,256,1024]{2,1,0:T(8,128)(2,1)}, bf16[2,256,1024]{2,1,0:T(8,128)(2,1)}, u32[]{:S(2)}, u32[]{:S(2)}) collective-permute-start(bf16[2,256,1024]{2,1,0:T(8,128)(2,1)} %get-tuple-element.127), channel_id=1, source_target_pairs={{0,16},{4,12},{8,24},{12,4},{16,0},{20,28},{24,8},{28,20},{1,17},{... | collective-permute-start | bytes 3145736 | tf_op jit(solution)/shard_map/ppermute | solution.py:91
  227.4 44.9 %collective-permute-start.25 = (bf16[4,256,2048]{2,1,0:T(8,128)(2,1)}, bf16[4,256,2048]{2,1,0:T(8,128)(2,1)}, u32[]{:S(2)}, u32[]{:S(2)}) collective-permute-start(bf16[4,256,2048]{2,1,0:T(8,128)(2,1)} %shard_map.345), channel_id=1, source_target_pairs={{0,4},{4,0},{8,12},{12,8},{16,20},{20,16},{24,28},{28,24},{1,5},{5... | collective-permute-start | bytes 12582920 | tf_op jit(solution)/shard_map/ppermute | solution.py:74
  267.5 49.3 %all-to-all-start = ((bf16[8,288,256]{2,1,0:T(8,128)(2,1)}), bf16[8,288,256]{2,1,0:T(8,128)(2,1)S(1)}, u32[]{:S(2)}, u32[]{:S(2)}) async-start(bf16[8,288,256]{2,1,0:T(8,128)(2,1)} %shard_map.352), calls=%async_computation | async-start | bytes 2359296 | tf_op jit(solution)/shard_map/all_to_all | solution.py:990
  282.4 28.0 %collective-permute-start.30 = (bf16[2,256,2048]{2,1,0:T(8,128)(2,1)}, bf16[2,256,2048]{2,1,0:T(8,128)(2,1)}, u32[]{:S(2)}, u32[]{:S(2)}) collective-permute-start(bf16[2,256,2048]{2,1,0:T(8,128)(2,1)} %get-tuple-element.136), channel_id=1, source_target_pairs={{0,16},{4,12},{8,24},{12,4},{16,0},{20,28},{24,8},{28,20},{1,17},{... | collective-permute-start | bytes 6291464 | tf_op jit(solution)/shard_map/ppermute | solution.py:91
  316.3 30.9 %collective-permute-start.31 = (bf16[1,256,2048]{2,1,0:T(8,128)(2,1)}, bf16[1,256,2048]{2,1,0:T(8,128)(2,1)}, u32[]{:S(2)}, u32[]{:S(2)}) collective-permute-start(bf16[1,256,2048]{2,1,0:T(8,128)(2,1)} %slice.365), channel_id=1, source_target_pairs={{0,8},{4,20},{8,0},{12,28},{16,24},{20,4},{24,16},{28,12},{1,9},{5... | collective-permute-start | bytes 3145736 | tf_op jit(solution)/shard_map/ppermute | solution.py:91
  318.2 29.0 %collective-permute-start.38 = (bf16[80,2048]{1,0:T(8,128)(2,1)S(1)}, bf16[80,2048]{1,0:T(8,128)(2,1)S(1)}, u32[]{:S(2)}, u32[]{:S(2)}) collective-permute-start(bf16[80,2048]{1,0:T(8,128)(2,1)S(1)} %maximum_maximum_fusion.refs_0_), channel_id=1, source_target_pairs={{0,1},{1,0},{2,3},{3,2},{4,5},{5,4},{6,7},{7,6},{8,9},{9,8},{10,11... | collective-permute-start | bytes 983048 | tf_op jit(solution)/shard_map/ppermute | solution.py:74
  363.8 34.3 %collective-permute-start.41 = (bf16[64,2048]{1,0:T(8,128)(2,1)}, bf16[64,2048]{1,0:T(8,128)(2,1)S(1)}, u32[]{:S(2)}, u32[]{:S(2)}) collective-permute-start(bf16[64,2048]{1,0:T(8,128)(2,1)} %get-tuple-element.274), channel_id=1, source_target_pairs={{0,1},{1,0},{2,3},{3,2},{4,5},{5,4},{6,7},{7,6},{8,9},{9,8},{10,11... | collective-permute-start | bytes 786440 | tf_op jit(solution)/shard_map/ppermute | solution.py:74
  365.3 43.2 %collective-permute-start.42 = (bf16[64,2048]{1,0:T(8,128)(2,1)}, bf16[64,2048]{1,0:T(8,128)(2,1)S(1)}, u32[]{:S(2)}, u32[]{:S(2)}) collective-permute-start(bf16[64,2048]{1,0:T(8,128)(2,1)} %get-tuple-element.275), channel_id=1, source_target_pairs={{0,2},{1,3},{2,0},{3,1},{4,6},{5,7},{6,4},{7,5},{8,10},{9,11},{10,... | collective-permute-start | bytes 786440 | tf_op jit(solution)/shard_map/ppermute | solution.py:74
  366.9 41.6 %collective-permute-start.43 = (bf16[64,2048]{1,0:T(8,128)(2,1)}, bf16[64,2048]{1,0:T(8,128)(2,1)S(1)}, u32[]{:S(2)}, u32[]{:S(2)}) collective-permute-start(bf16[64,2048]{1,0:T(8,128)(2,1)} %get-tuple-element.276), channel_id=1, source_target_pairs={{0,3},{1,2},{2,1},{3,0},{4,7},{5,6},{6,5},{7,4},{8,11},{9,10},{10,... | collective-permute-start | bytes 786440 | tf_op jit(solution)/shard_map/ppermute | solution.py:74
  380.1 61.8 %collective-permute-start.59 = (bf16[4,64,1024]{2,1,0:T(8,128)(2,1)}, bf16[4,64,1024]{2,1,0:T(8,128)(2,1)}, u32[]{:S(2)}, u32[]{:S(2)}) collective-permute-start(bf16[4,64,1024]{2,1,0:T(8,128)(2,1)} %get-tuple-element.167), channel_id=1, source_target_pairs={{0,4},{4,0},{8,12},{12,8},{16,20},{20,16},{24,28},{28,24},{1,5},{5... | collective-permute-start | bytes 1572872 | tf_op jit(solution)/shard_map/ppermute | solution.py:74
  389.2 71.6 %collective-permute-start.65 = (bf16[4,560,256]{2,1,0:T(8,128)(2,1)}, bf16[4,560,256]{2,1,0:T(8,128)(2,1)}, u32[]{:S(2)}, u32[]{:S(2)}) collective-permute-start(bf16[4,560,256]{2,1,0:T(8,128)(2,1)} %get-tuple-element.170), channel_id=1, source_target_pairs={{0,4},{4,0},{8,12},{12,8},{16,20},{20,16},{24,28},{28,24},{1,5},{5... | collective-permute-start | bytes 3440648 | tf_op jit(solution)/shard_map/ppermute | solution.py:74
  398.2 21.2 %collective-permute-start.50 = (bf16[64,2048]{1,0:T(8,128)(2,1)}, bf16[64,2048]{1,0:T(8,128)(2,1)S(1)}, u32[]{:S(2)}, u32[]{:S(2)}) collective-permute-start(bf16[64,2048]{1,0:T(8,128)(2,1)} %get-tuple-element.156), channel_id=1, source_target_pairs={{0,1},{1,0},{2,3},{3,2},{4,5},{5,4},{6,7},{7,6},{8,9},{9,8},{10,11... | collective-permute-start | bytes 786440 | tf_op jit(solution)/shard_map/ppermute | solution.py:74
  408.5 21.6 %collective-permute-start.51 = (bf16[64,2048]{1,0:T(8,128)(2,1)}, bf16[64,2048]{1,0:T(8,128)(2,1)S(1)}, u32[]{:S(2)}, u32[]{:S(2)}) collective-permute-start(bf16[64,2048]{1,0:T(8,128)(2,1)} %get-tuple-element.157), channel_id=1, source_target_pairs={{0,2},{1,3},{2,0},{3,1},{4,6},{5,7},{6,4},{7,5},{8,10},{9,11},{10,... | collective-permute-start | bytes 786440 | tf_op jit(solution)/shard_map/ppermute | solution.py:74
  409.2 20.9 %collective-permute-start.52 = (bf16[64,2048]{1,0:T(8,128)(2,1)}, bf16[64,2048]{1,0:T(8,128)(2,1)S(1)}, u32[]{:S(2)}, u32[]{:S(2)}) collective-permute-start(bf16[64,2048]{1,0:T(8,128)(2,1)} %get-tuple-element.158), channel_id=1, source_target_pairs={{0,3},{1,2},{2,1},{3,0},{4,7},{5,6},{6,5},{7,4},{8,11},{9,10},{10,... | collective-permute-start | bytes 786440 | tf_op jit(solution)/shard_map/ppermute | solution.py:74
  419.4 45.5 %collective-permute-start.53 = (bf16[4,256,768]{2,1,0:T(8,128)(2,1)}, bf16[4,256,768]{2,1,0:T(8,128)(2,1)}, u32[]{:S(2)}, u32[]{:S(2)}) collective-permute-start(bf16[4,256,768]{2,1,0:T(8,128)(2,1)} %get-tuple-element.162), channel_id=1, source_target_pairs={{0,4},{4,0},{8,12},{12,8},{16,20},{20,16},{24,28},{28,24},{1,5},{5... | collective-permute-start | bytes 4718600 | tf_op jit(solution)/shard_map/ppermute | solution.py:74
  (88 other events, 1182.0 us)
Sparse Core Ops, SparseCore 0:
  9.9 57.0 all-gather.2

commit v3 on v2

--- a/solution.py
+++ b/solution.py
@@ -113,10 +113,16 @@
 
 
 def share(array, axis):
+    return [array] + [swap(array, axis, r) for r in range(1, lax.axis_size(axis))]
+
+
+def share_far_first(array, axis):
     blocks = {0: array}
     bit = lax.axis_size(axis) // 2
     while bit:
-        blocks.update({r ^ bit: swap(block, axis, bit) for r, block in blocks.items()})
+        blocks.update(
+            {r ^ bit: swap(block, axis, bit) for r, block in blocks.items()}
+        )
         bit //= 2
     return [blocks[r] for r in range(len(blocks))]
 
@@ -125,36 +131,53 @@
     return [blocks[0]] + [swap(blocks[r], axis, r) for r in range(1, len(blocks))]
 
 
-def gather_chips(block):
+def sum_along(blocks, sent, axis):
+    bit, got = 1, sent
+    while True:
+        stay = [r for r in blocks if not r & bit]
+        rows = blocks[0].shape[0]
+        blocks = {
+            r: blocks[r].astype(f32) + got[i * rows : (i + 1) * rows].astype(f32)
+            for i, r in enumerate(stay)
+        }
+        bit *= 2
+        if bit == lax.axis_size(axis):
+            return blocks[0]
+        got = swap(
+            jnp.concatenate([blocks[r].astype(bf16) for r in blocks if r & bit], axis=0), axis, bit
+        )
+
+
+def gather_chips(block, between):
     own = [block]
     for step in range(len(chip_bits(0))):
-        own = own + [swap_chips(have, step) for have in own]
+        own = own + [
+            swap_chips(after(have, between) if i else have, step) for i, have in enumerate(own)
+        ]
     return own
 
 
-def both_cores(own):
-    return [swap(have, "dp", 1) for have in own] + list(own)
-
-
-def gather_dp(block):
-    return both_cores(gather_chips(block))
-
-
-def sum_chips(pairs):
+def sum_chips(pairs, hook=lambda step, arrived: arrived):
     arrivals = []
     for step in reversed(range(len(chip_bits(0)))):
-        got = [swap_chips(send, step) for _, send in pairs]
+        got = hook(len(arrivals) // 2, [swap_chips(send, step) for _, send in pairs])
         arrivals.append(got)
         size = got[0].shape[0]
         sums = [keep.astype(f32) + g.astype(f32) for (keep, _), g in zip(pairs, got)]
         pairs = [(s[: size // 2], s[size // 2 :].astype(bf16)) for s in sums]
+        arrivals.append([send for _, send in pairs])
     return [s[0] for s in sums], arrivals
 
 
-def sum_dp(far, near):
-    here = (near.astype(f32) + swap(far, "dp", 1).astype(f32)).astype(bf16)
-    half = here.shape[0] // 2
-    return sum_chips([(here[:half], here[half:])])[0][0]
+def sum_cores(terms):
+    pairs = []
+    for far, near in terms:
+        got = swap(far, "dp", 1)
+        half = near.shape[0] // 2
+        keep = near[:half].astype(f32) + got[:half].astype(f32)
+        send = (near[half:].astype(f32) + got[half:].astype(f32)).astype(bf16)
+        pairs.append((keep, send))
+    return pairs
 
 
 def total(blocks):
@@ -613,8 +636,14 @@
     )(src, tensor, slots, grads, shared_down)
 
 
-def pick_rows(blocks, first, slots, router, weights, dact, experts_all, results):
+def pick_rows(blocks, places, slots, router, weights, dact, experts_all, results):
     count = len(blocks)
+    run = next(i for i in range(1, count) if places[i] != places[i - 1] + 1)
+    first, skip = places[0], places[run] - places[0] - run
+
+    def place(s):
+        return s + first + jnp.where(s < run, 0, skip)
+
     every, experts, toks = slots.shape
     width = blocks[0].shape[1]
     shared = dact.shape[1]
@@ -623,17 +652,17 @@
         functools.partial(pick_kernel, count, experts_all, len(results)),
         grid=(count,),
         in_specs=[
-            pl.BlockSpec((1, experts, toks), lambda s: (s + first, 0, 0)),
+            pl.BlockSpec((1, experts, toks), lambda s: (place(s), 0, 0)),
             whole(router),
             whole(weights),
-            pl.BlockSpec((toks, shared), lambda s: (s + first, 0)),
+            pl.BlockSpec((toks, shared), lambda s: (place(s), 0)),
         ]
         + [ANYWHERE] * (count + len(results)),
         out_specs=[
-            pl.BlockSpec((experts, CAP, width), lambda s: (0, s + first, 0)),
-            pl.BlockSpec((experts, CAP, LANES), lambda s: (0, s + first, 0)),
-            pl.BlockSpec((toks, shared), lambda s: (s + first, 0)),
-            pl.BlockSpec((toks, 2 * shared), lambda s: (s + first, 0)),
+            pl.BlockSpec((experts, CAP, width), lambda s: (0, place(s), 0)),
+            pl.BlockSpec((experts, CAP, LANES), lambda s: (0, place(s), 0)),
+            pl.BlockSpec((toks, shared), lambda s: (place(s), 0)),
+            pl.BlockSpec((toks, 2 * shared), lambda s: (place(s), 0)),
         ],
         out_shape=[
             shape(bf16, experts, every * CAP, width),
@@ -846,17 +875,18 @@
     tokens_p = by_partner(tokens, "tensor", 0)
     tokens_own = tokens_p[0].astype(f32)
     cot_own = block_at(cotangent, t_index, own_toks, 0).astype(f32)
-    cot_all = lax.all_gather(cotangent, "dp")
     tensor = t_index.astype(jnp.int32).reshape(1)
-    ids = reorder(expert_ids, "tensor", 0)
     every = jnp.arange(experts_all, dtype=jnp.int32)
-    member = jnp.any(ids.T[:, None, :] == every[None, :, None], axis=0)
+    member = jnp.any(expert_ids.T[:, None, :] == every[None, :, None], axis=0)
     before = (jnp.arange(toks)[:, None] < jnp.arange(toks)[None, :]).astype(bf16)
     rank = dot(member.astype(bf16), before)
-    slots_own = jnp.where(member, rank, -1.0).astype(bf16)
-    slots = jnp.stack([block_at(b, d_index, experts, 0) for b in gather_dp(slots_own)]).astype(
-        jnp.int32
-    )
+    slots_own = jnp.where(member, rank, -1.0).astype(bf16).reshape(-1, width)
+    slot_rows = slots_own.shape[0]
+    slots_own = jnp.pad(slots_own, ((0, -slot_rows % 16), (0, 0)))
+    cot_all = lax.all_gather(jnp.concatenate([cotangent, slots_own], axis=0), "dp")
+    slots = cot_all[:, toks : toks + slot_rows].reshape(n_d, experts_all, toks)
+    slots = reorder(block_at(slots, d_index, experts, 1), "tensor", 2)
+    slots = jnp.concatenate([block_at(slots, s, 1, 0) for s in sources], axis=0).astype(jnp.int32)
     router_t = jnp.roll(router_weight.T, -d_index * experts, axis=0)
     router_parts = []
     rest = router_t
@@ -914,27 +944,28 @@
     )
     attn_part = results[:n_t]
     attended_p, latent, latent_normed, inv_latent, key_value, rope_rot, lse = results[n_t:]
-    attn_sum = total(trade(attn_part, "tensor"))
+    attn_sum = total(
+        after(trade(attn_part, "tensor"), router_parts, shared_in, shared_out, inv_first, kv_up_p)
+    )
     hidden_one = tokens_own + attn_sum
     ffn_normed_f, inv_second = rms_norm(hidden_one, ffn_gain)
     ffn_own = ffn_normed_f.astype(bf16)
-    ffn_block = jnp.concatenate(share(ffn_own, "tensor"), axis=0)
-    near_blocks = gather_chips(ffn_block)
-    near_blocks = near_blocks[:-1] + [after(near_blocks[-1], grad_rows)]
-    far_blocks = [swap(block, "dp", 1) for block in near_blocks]
+    ffn_block = jnp.concatenate(share_far_first(ffn_own, "tensor"), axis=0)
+    near_blocks = gather_chips(ffn_block, grad_rows)
+    far_blocks = [swap(block, "dp", 1) for block in near_blocks[:-1]]
+
+    def pick(places, blocks_here, results):
+        return pick_rows(
+            blocks_here, places, slots, router_parts, shared_in, shared_dact, experts_all, results
+        )
+
+    early = [0] + list(range(half, n_d - 1))
+    results = pick(early, far_blocks[:1] + near_blocks[:-1], [])
+    far_blocks.append(swap(after(near_blocks[-1], results), "dp", 1))
+    late = list(range(1, half)) + [n_d - 1]
     blocks = far_blocks + near_blocks
 
-    results = []
-    for side, first, start, stop in (
-        (near_blocks, half, 0, half - 1),
-        (far_blocks, 0, 0, half - 1),
-        (near_blocks, half, half - 1, half),
-        (far_blocks, 0, half - 1, half),
-    ):
-        results = pick_rows(
-            side[start:stop], first + start, slots, router_parts, shared_in, shared_dact, experts_all,
-            results,
-        )
+    results = pick(late, [blocks[i] for i in late], results)
     rows, gate, shared_act, shared_delta = results
     lanes = -(-2 * experts_all // LANES) * LANES
     first = (d_index * experts).astype(jnp.int32).reshape(1)
@@ -965,34 +996,28 @@
         )
         for i in range(pieces)
     ]
-    sums, arrivals = sum_chips(mine)
-
-    other = return_rows(
-        0, slots, [after(act, mine)], [expert_down], shared_act, shared_out, None, 0, width, None
-    )[0]
-    other = swap(other, "dp", 1)
+    out_other = []
+
+    def beside(step, arrived):
+        if step:
+            return arrived
+        out_other.extend(
+            return_rows(
+                0, slots, [after(act, arrived[0], mine[1:])], [expert_down], shared_act, shared_out,
+                None, 0, width, None,
+            )
+        )
+        return arrived[:1] + after(arrived[1:], out_other)
+
+    sums, arrivals = sum_chips(mine, beside)
     out_pair = return_rows(
         1, slots, [act], [expert_down], shared_act, shared_out, None, 0, width,
-        after(other, arrivals[0][0]),
+        after(swap(out_other[0], "dp", 1), arrivals[0]),
     )
     shared_rows = shared_cols + -shared_cols % 16
-    sums[0] = after(sums[0], out_pair)
     back_sums = [total(send_back(s)) for s in sums]
     back_sum = jnp.concatenate(back_sums[:-1] + [back_sums[-1][:, :size]], axis=1)
     score_sum = back_sums[-1][:, size:]
-    shared_all = shared_grads(
-        src, tensor, n_t, blocks, cot_all, *after((shared_delta, shared_act), arrivals[-1]), shared_rows
-    )
-    out_pair = after(out_pair, arrivals[-1])
-    out_sums, out_arrivals = sum_chips([out_pair])
-    out_here = out_sums[0]
-
-    shared_all = lax.all_to_all(shared_all, "dp", 0, 0, tiled=True).astype(f32)
-    shared_gate_grad, shared_up_grad, shared_down_grad = [
-        shared_all[:, i * shared_rows : i * shared_rows + shared_cols].reshape(-1, rows_d)
-        for i in range(3)
-    ]
-
     logits = jnp.dot(ffn_own.astype(f32), router_weight, precision=lax.Precision.HIGHEST)
     router_prob = jax.nn.softmax(logits, axis=-1)
     prob_grad = score_sum[:, :experts_all] + score_sum[:, lanes // 2 : lanes // 2 + experts_all]
@@ -1010,18 +1035,19 @@
         [
             flat_logits,
             ffn_gain_part.astype(bf16)[None],
-            jnp.zeros((-(flat + 1) % 16, width), bf16),
+            jnp.zeros((-(flat + 1) % 8, width), bf16),
         ],
         axis=0,
     )
     message = jnp.concatenate([hidden_grad.astype(bf16), extra], axis=0)
-    message = after(message, out_arrivals[0])
-    shared_grads_t = after(share(message, "tensor"), out_arrivals[-1])
+    message = after(message, out_pair)
+    shared_grads_t = share(message, "tensor")
     expert_gate_grad, expert_up_grad, expert_down_grad = expert_grads(
         rows, grad_rows, *after((act, gate_delta, up_delta), message)
     )
-    out_sum = total(send_back(after(out_here, shared_grads_t)))
-    output_own = (hidden_one + out_sum).astype(bf16)
+    out_sums, out_steps = sum_chips([out_pair], lambda step, arrived: after(arrived, expert_gate_grad))
+    out_here = out_sums[0]
+    shared_grads_t = after(shared_grads_t, expert_gate_grad, out_steps[1])
 
     lat_rows = lat_rank // n_d
     results = single(
@@ -1049,63 +1075,77 @@
     )
     latent_parts = results[:n_t]
     query_grad_p, kv_up_far, kv_up_near = results[n_t:]
+    normed_p = reorder(normed, "tensor", 0)
+
+    def rows_grad(left, right):
+        return single(
+            rows_grad_kernel,
+            [shape(bf16, half, rows_d, right.shape[1])] * 2,
+            [left, right],
+            scalars=[src],
+            flops=2 * toks * width * right.shape[1],
+        )
+
+    logit_p = jnp.concatenate(
+        [b[own_toks : own_toks + flat].reshape(own_toks, experts_all) for b in shared_grads_t], axis=0
+    )
+    gain_part = total([b[own_toks + flat] for b in shared_grads_t])[None]
+    out_cols = attended_p.shape[1]
+    height = out_cols + experts_all + 16
+    column_terms = single(
+        functools.partial(columns_grad_kernel, n_t, flat),
+        [shape(bf16, half, height, rows_d)] * 2,
+        [after(attended_p, query_grad_p), logit_p, ffn_block, gain_part, *shared_grads_t],
+        scalars=[src],
+        scratch=[pltpu.VMEM((toks, width), bf16)],
+        flops=2 * toks * width * height,
+    )
+    query_terms = rows_grad(after(normed_p, out_steps[2]), query_grad_p)
+    terms = [query_terms, column_terms, (kv_up_far, kv_up_near)]
+    out_rows = {r: out_here[r * own_toks : (r + 1) * own_toks] for r in range(n_t)}
+    out_sent = swap(
+        jnp.concatenate([out_rows[r].astype(bf16) for r in out_rows if r & 1], axis=0), "tensor", 1
+    )
+    latent_parts = after(trade(latent_parts, "tensor"), terms)
     results = single(
         functools.partial(normed_back_kernel, n_t),
         [shape(f32 if r == 0 else bf16, own_toks, width) for r in range(n_t)]
         + [shape(bf16, toks, narrow_cols)],
-        [query_grad_p, q_weight, kv_down, rope_t, *trade(latent_parts, "tensor")],
+        [query_grad_p, q_weight, kv_down, rope_t, *latent_parts],
         scalars=[tensor],
         scratch=[pltpu.VMEM((toks, narrow_cols), f32)],
         flops=2 * toks * width * (q_cols + narrow_cols),
     )
     normed_part, narrow_p = results[:n_t], results[n_t]
-    output_own = after(output_own, normed_part)
-    output = reorder(jnp.concatenate(share(output_own, "tensor"), axis=0), "tensor", 0)
-    normed_grad = total(trade(normed_part, "tensor"))
+    query_pairs = sum_cores(after(terms[:1], normed_part))
+    shared_all = shared_grads(
+        src, tensor, n_t, blocks, cot_all, *after((shared_delta, shared_act), out_sent, query_pairs[0][1]), shared_rows
+    )
+    shared_sent = lax.all_to_all(shared_all, "dp", 0, 0, tiled=True).astype(f32)
+    shared_gate_grad, shared_up_grad, shared_down_grad = [
+        shared_sent[:, i * shared_rows : i * shared_rows + shared_cols].reshape(-1, rows_d)
+        for i in range(3)
+    ]
+    (q_weight_grad,), term_arrivals = sum_chips(query_pairs)
+    terms = terms[1:] + [rows_grad(normed_p, narrow_p)]
+    (columns, kv_up_grad, narrow_grad), _ = sum_chips(sum_cores(after(terms, query_pairs[0][1])))
+    normed_arrived = after(trade(normed_part, "tensor"), term_arrivals[0], shared_all)
+    normed_grad = total(normed_arrived)
+    out_sum = sum_along(out_rows, after(out_sent, normed_arrived[1:]), "tensor")
+    output_own = (hidden_one + out_sum).astype(bf16)
+    output = reorder(jnp.concatenate(share_far_first(output_own, "tensor"), axis=0), "tensor", 0)
     inv_first_own = block_at(inv_first, t_index, own_toks, 0)
     input_norm_grad, _ = rms_back(normed_grad, tokens_own, inv_first_own, attn_gain)
     input_grad = hidden_grad + input_norm_grad
 
-    logit_p = jnp.concatenate(
-        [b[own_toks : own_toks + flat].reshape(own_toks, experts_all) for b in shared_grads_t], axis=0
-    )
-    gain_part = total([b[own_toks + flat] for b in shared_grads_t])[None]
-    out_cols = attended_p.shape[1]
-    height = out_cols + experts_all + 16
-    columns = sum_dp(
-        *single(
-            functools.partial(columns_grad_kernel, n_t, flat),
-            [shape(bf16, half, height, rows_d)] * 2,
-            [attended_p, logit_p, ffn_block, gain_part, *shared_grads_t],
-            scalars=[src],
-            scratch=[pltpu.VMEM((toks, width), bf16)],
-            flops=2 * toks * width * height,
-        )
-    )
     o_weight_grad = columns[:out_cols]
     device_rows = width // (n_d * n_t)
     router_grad = block_at(
         columns[out_cols : out_cols + experts_all], t_index, device_rows, 1
     ).T
     ffn_gain_grad = block_at(columns[out_cols + experts_all], t_index, device_rows, 0)
-
-    def rows_grad(left, right):
-        return sum_dp(
-            *single(
-                rows_grad_kernel,
-                [shape(bf16, half, rows_d, right.shape[1])] * 2,
-                [left, right],
-                scalars=[src],
-                flops=2 * toks * width * right.shape[1],
-            )
-        )
-
-    normed_p = reorder(normed, "tensor", 0)
-    q_weight_grad = rows_grad(normed_p, query_grad_p)
-    narrow_grad = rows_grad(normed_p, narrow_p)
     kv_down_grad = narrow_grad[:, :lat_cols]
     k_rope_grad = narrow_grad[:, lat_cols:]
-    kv_up_grad = sum_dp(kv_up_far, kv_up_near)
 
     attn_gain_part = jnp.sum(
         block_at(q_weight, d_index, rows_d, 0).astype(f32) * q_weight_grad, axis=1

time: 521 us -> 473 us (0.908)
  waiting for transfers between devices: 150 us -> 112 us
  between operations: 15.1 us -> 30.9 us
  starting transfers between devices: 86 us -> 71.6 us
  local copies, waits for them, and re-layouts: 32.3 us -> 24.7 us
  Pallas kernels: 181 us -> 174 us
    ppermute x48 -> x43, waiting for transfers between devices: 95.6 us -> 74.5 us  [swap(): return lax.ppermute(array, axis, [(i, i ^ bits) for i in range(count)])]
    ppermute x20 -> x17, waiting for transfers between devices: 53.4 us -> 37.7 us  [swap_chips(): lax.ppermute(array, 'dp', [(i, i ^ chip_bits(i % 2)[step]) for i in range...]
    ppermute x48 -> x43, starting transfers between devices: 60.9 us -> 47.5 us  [swap(): return lax.ppermute(array, axis, [(i, i ^ bits) for i in range(count)])]
    pallas_call x4 -> x2, Pallas kernels: 24.2 us -> 17.1 us  [pick_rows(): pl.pallas_call(functools.partial(pick_kernel, count, experts_all, len(res...]
    unnamed x96 -> x91, local copies, waits for them, and re-layouts: 12.1 us -> 8.31 us
    ppermute x20 -> x17, starting transfers between devices: 21.4 us -> 19.7 us  [swap_chips(): lax.ppermute(array, 'dp', [(i, i ^ chip_bits(i % 2)[step]) for i in range...]
  transfers between devices with their start and end apart: 70 -> 62, of which waited for: 26 -> 20; matrix products, arithmetic and copies ran while one was open for 13% -> 13% of each run, Pallas kernels for 27% -> 26%
where the time goes in v3:
time: 473 us; the launch traced here: 466 us
  Pallas kernels  174 us (37%)
  waiting for transfers between devices  112 us (24%)
  starting transfers between devices  71.6 us (15%)
  other arithmetic  51.6 us (11%)
  between operations  30.9 us (7%)
  local copies, waits for them, and re-layouts  24.7 us (5%)
    ppermute x43, waiting for transfers between devices, swap(): return lax.ppermute(array, axis, [(i, i ^ bits) for i in range(count)])  74.5 us
    pallas_call x6, Pallas kernels, return_rows(): pl.pallas_call(functools.partial(return_kernel, (len(deltas), score is no...  51.3 us
    ppermute x43, starting transfers between devices, swap(): return lax.ppermute(array, axis, [(i, i ^ bits) for i in range(count)])  47.5 us
    pallas_call x8, Pallas kernels, single(): pl.pallas_call(kernel, grid_spec=pltpu.PrefetchScalarGridSpec(num_scalar_...  40.5 us
    ppermute x17, waiting for transfers between devices, swap_chips(): lax.ppermute(array, 'dp', [(i, i ^ chip_bits(i % 2)[step]) for i in range...  37.7 us
    pallas_call x1, Pallas kernels, expert_grads(): pl.pallas_call(expert_grad_kernel, grid=(experts,), in_specs=[per_expert(...  19.9 us
    pallas_call x1, Pallas kernels, expert_hidden(): pl.pallas_call(hidden_kernel, grid=(experts,), in_specs=[pl.BlockSpec(mem...  19.8 us
    ppermute x17, starting transfers between devices, swap_chips(): lax.ppermute(array, 'dp', [(i, i ^ chip_bits(i % 2)[step]) for i in range...  19.7 us
  transfers between devices with their start and end apart: 62, of which 20 were waited for; matrix products, arithmetic and copies ran while one was open for 13% of the time, Pallas kernels for 26%

profile of v3, /device:TPU:0, one launch (start us, length us, event | category | flops | bytes accessed | tf_op | source)
XLA Modules:
  0.0 465.6 jit_solution(13288304827649280708)
XLA Ops:
  31.2 6.0 %shard_map.334 = (f32[64,2048]{1,0:T(8,128)}, bf16[64,2048]{1,0:T(8,128)(2,1)}, bf16[64,2048]{1,0:T(8,128)(2,1)}, bf16[64,2048]{1,0:T(8,128)(2,1)}, bf16[256,512...) custom-call(s32[1]{0:T(128)} %bitcast.tensor_ref, ...), custom_call_target="tpu_custom_call" | custom-call | flops 1073741824 | bytes 4245504 | tf_op jit(solution)/shard_map/pallas_call | solution.py:813
  49.4 11.0 %collective-permute-done.4 = bf16[64,2048]{1,0:T(8,128)(2,1)} collective-permute-done((bf16[64,2048]{1,0:T(8,128)(2,1)}, bf16[64,2048]{1,0:T(8,128)(2,1)}, u32[]{:S(2)}, u32[]{:S(2)}) %collective-permute-start.4) | collective-permute-done | bytes 262176 | tf_op jit(solution)/shard_map/ppermute | solution.py:74
  62.0 5.2 %collective-permute-start.7 = (bf16[64,2048]{1,0:T(8,128)(2,1)S(1)}, bf16[64,2048]{1,0:T(8,128)(2,1)S(1)}, u32[]{:S(2)}, u32[]{:S(2)}) collective-permute-start(bf16[64,2048]{1,0:T(8,128)(2,1)S(1)} %multiply_convert_fusion), channel_id=1, source_target_pairs={{0,2},{1,3},{2,0},{3,1},{4,6},{5,7},{6,4},{7,5},{8,10},{9,11},{10,... | collective-permute-start | bytes 786440 | tf_op jit(solution)/shard_map/ppermute | solution.py:74
  67.1 10.6 %collective-permute-done.7 = bf16[64,2048]{1,0:T(8,128)(2,1)S(1)} collective-permute-done((bf16[64,2048]{1,0:T(8,128)(2,1)S(1)}, bf16[64,2048]{1,0:T(8,128)(2,1)S(1)}, u32[]{:S(2)}, u32[]{:S(2)}) %collective-permute-start.7) | collective-permute-done | bytes 262176 | tf_op jit(solution)/shard_map/ppermute | solution.py:74
  99.3 12.3 %shard_map.335 = (bf16[4,512,2048]{2,1,0:T(8,128)(2,1)}, f32[2048,128]{1,0:T(8,128)}) custom-call(s32[8]{0:T(128)} %copy-done.35, s32[1]{0:T(128)} %bitcast.tensor_ref, s32[8,4,256]{2,1,0:T(4,128)} %convert_element_type.314.slots_ref, bf16[8,272,2048]{2,1,0:T(8,128)(2,1)} %bitcast.128, bf16[128,2048]{1,0:T(8,128)(2,1)} %pad.16.down_ref.refs_3_), custom_call_target="tpu_custom_call" | custom-call | flops 3221225472 | bytes 16777216 | tf_op jit(solution)/shard_map/pallas_call | solution.py:612
  111.5 6.8 %collective-permute-done.9.refs_2_.refs_5_ = bf16[256,2048]{1,0:T(8,128)(2,1)S(1)} collective-permute-done((bf16[256,2048]{1,0:T(8,128)(2,1)S(1)}, bf16[256,2048]{1,0:T(8,128)(2,1)S(1)}, u32[]{:S(2)}, u32[]{:S(2)}) %collective-permute-start.9) | collective-permute-done | bytes 1048608 | tf_op jit(solution)/shard_map/ppermute | solution.py:91
  122.2 8.6 %shard_map.336 = (bf16[4,512,2048]{2,1,0:T(8,128)(2,1)}, f32[4,512,128]{2,1,0:T(8,128)}, bf16[2048,128]{1,0:T(8,128)(2,1)}, bf16[2048,256]{1,0:T(8,128)(2,1)}) custom-call(s32[8,4,256]{2,1,0:T(4,128)} %convert_element_type.314.slots_ref, bf16[96,2048]{1,0:T(8,128)(2,1)} %pad_maximum_fusion.6.router_ref, bf16[256,2048]{1,0:T(8,128)(2,1)} %fusion.6.weights_ref.refs_5_, ...), custom_call_target="tpu_custom_call" | custom-call | flops 2550136832 | bytes 8388608 | tf_op jit(solution)/shard_map/pallas_call | solution.py:651
  138.1 8.5 %shard_map.337 = (bf16[4,512,2048]{2,1,0:T(8,128)(2,1)}, f32[4,512,128]{2,1,0:T(8,128)}, bf16[2048,128]{1,0:T(8,128)(2,1)}, bf16[2048,256]{1,0:T(8,128)(2,1)}) custom-call(s32[8,4,256]{2,1,0:T(4,128)} %convert_element_type.314.slots_ref, ...), custom_call_target="tpu_custom_call", output_to_operand_aliasing={{0}: (8, {}), {1}: (9, {}), {2}: (10, {}), {3}: (11, {})} | custom-call | flops 2550136832 | bytes 8388608 | tf_op jit(solution)/shard_map/pallas_call | solution.py:651
  146.7 19.8 %shard_map.338 = (bf16[4,512,352]{2,1,0:T(8,128)(2,1)}, bf16[4,512,352]{2,1,0:T(8,128)(2,1)}, bf16[4,512,352]{2,1,0:T(8,128)(2,1)}, bf16[4,512,128]{2,1,0:T(8,128)(2,1)}) custom-call(s32[1]{0:T(128)} %bitcast.19.first_ref, bf16[4,512,2048]{2,1,0:T(8,128)(2,1)} %get-tuple-element.131.rows_ref, bf16[4,512,2048]{2,1,0:T(8,128)(2,1)} %get-tuple-element.124.grads_ref, ...), custom_call_target="tpu_custom_call" | custom-call | flops 8858370048 | bytes 34078720 | tf_op jit(solution)/shard_map/pallas_call | solution.py:695
  166.5 7.6 %shard_map.339 = bf16[4,256,1024]{2,1,0:T(8,128)(2,1)} custom-call(s32[8,4,256]{2,1,0:T(4,128)} %convert_element_type.314.slots_ref, bf16[4,512,352]{2,1,0:T(8,128)(2,1)} %get-tuple-element.150.refs_0_.gate_delta_ref, bf16[4,512,352]{2,1,0:T(8,128)(2,1)} %get-tuple-element.151.refs_1_.up_delta_ref, bf16[4,352,2048]{2,1,0:T(8,128)(2,1)} %bitcast.118, ...), custom_call_target="tpu_custom_call" | custom-call | flops 2550136832 | bytes 7864320 | tf_op jit(solution)/shard_map/pallas_call | solution.py:737
  174.4 8.0 %shard_map.341 = bf16[4,256,1152]{2,1,0:T(8,128)(2,1)} custom-call(s32[8,4,256]{2,1,0:T(4,128)} %convert_element_type.314.slots_ref, bf16[4,512,352]{2,1,0:T(8,128)(2,1)} %get-tuple-element.150.refs_0_.gate_delta_ref, bf16[4,512,352]{2,1,0:T(8,128)(2,1)} %get-tuple-element.151.refs_1_.up_delta_ref, bf16[4,352,2048]{2,1,0:T(8,128)(2,1)} %bitcast.119, ...), custom_call_target="tpu_custom_call" | custom-call | flops 2550136832 | bytes 7864320 | tf_op jit(solution)/shard_map/pallas_call | solution.py:737
  183.9 8.0 %shard_map.340 = (bf16[2,256,1024]{2,1,0:T(8,128)(2,1)}, bf16[2,256,1024]{2,1,0:T(8,128)(2,1)}) custom-call(s32[8,4,256]{2,1,0:T(4,128)} %convert_element_type.314.slots_ref, bf16[4,512,352]{2,1,0:T(8,128)(2,1)} %get-tuple-element.150.refs_0_.gate_delta_ref, bf16[4,512,352]{2,1,0:T(8,128)(2,1)} %get-tuple-element.151.refs_1_.up_delta_ref, ...), custom_call_target="tpu_custom_call" | custom-call | flops 2550136832 | bytes 7864320 | tf_op jit(solution)/shard_map/pallas_call | solution.py:737
  193.8 8.8 %shard_map.342 = (bf16[2,256,1152]{2,1,0:T(8,128)(2,1)}, bf16[2,256,1152]{2,1,0:T(8,128)(2,1)}) custom-call(s32[8,4,256]{2,1,0:T(4,128)} %convert_element_type.314.slots_ref, bf16[4,512,352]{2,1,0:T(8,128)(2,1)} %get-tuple-element.150.refs_0_.gate_delta_ref, bf16[4,512,352]{2,1,0:T(8,128)(2,1)} %get-tuple-element.151.refs_1_.up_delta_ref, ...), custom_call_target="tpu_custom_call" | custom-call | flops 2550136832 | bytes 7864320 | tf_op jit(solution)/shard_map/pallas_call | solution.py:737
  206.9 9.0 %shard_map.343 = bf16[4,256,2048]{2,1,0:T(8,128)(2,1)} custom-call(s32[8,4,256]{2,1,0:T(4,128)} %convert_element_type.314.slots_ref, bf16[4,512,352]{2,1,0:T(8,128)(2,1)} %get-tuple-element.149.refs_0_.act_ref, bf16[4,352,2048]{2,1,0:T(8,128)(2,1)} %refs_1_.3, bf16[2048,128]{1,0:T(8,128)(2,1)} %get-tuple-element.190.refs_2_.act_ref, ...), custom_call_target="tpu_custom_call" | custom-call | flops 3087007744 | bytes 9961472 | tf_op jit(solution)/shard_map/pallas_call | solution.py:737
  236.8 6.4 %collective-permute-done.24 = bf16[64,1024]{1,0:T(8,128)(2,1)S(1)} collective-permute-done((bf16[64,1024]{1,0:T(8,128)(2,1)S(1)}, bf16[64,1024]{1,0:T(8,128)(2,1)S(1)}, u32[]{:S(2)}, u32[]{:S(2)}) %collective-permute-start.24) | collective-permute-done | bytes 131104 | tf_op jit(solution)/shard_map/ppermute | solution.py:74
  244.2 10.7 %collective-permute-done.28 = bf16[64,1152]{1,0:T(8,128)(2,1)S(1)} collective-permute-done((bf16[64,1152]{1,0:T(8,128)(2,1)S(1)}, bf16[64,1152]{1,0:T(8,128)(2,1)S(1)}, u32[]{:S(2)}, u32[]{:S(2)}) %collective-permute-start.28) | collective-permute-done | bytes 147488 | tf_op jit(solution)/shard_map/ppermute | solution.py:74
  255.3 10.0 %shard_map.344 = (bf16[2,256,2048]{2,1,0:T(8,128)(2,1)}, bf16[2,256,2048]{2,1,0:T(8,128)(2,1)}) custom-call(s32[8,4,256]{2,1,0:T(4,128)} %convert_element_type.314.slots_ref, bf16[4,512,352]{2,1,0:T(8,128)(2,1)} %get-tuple-element.149.refs_0_.act_ref, bf16[4,352,2048]{2,1,0:T(8,128)(2,1)} %refs_1_.3, bf16[2048,128]{1,0:T(8,128)(2,1)} %get-tuple-element.190.refs_2_.act_ref, ...), custom_call_target="tpu_custom_call" | custom-call | flops 3087007744 | bytes 9961472 | tf_op jit(solution)/shard_map/pallas_call | solution.py:737
  274.4 19.9 %shard_map.345 = (f32[4,352,2048]{2,1,0:T(8,128)}, f32[4,352,2048]{2,1,0:T(8,128)}, f32[4,352,2048]{2,1,0:T(8,128)}) custom-call(bf16[4,512,2048]{2,1,0:T(8,128)(2,1)} %get-tuple-element.131.rows_ref, bf16[4,512,2048]{2,1,0:T(8,128)(2,1)} %get-tuple-element.124.grads_ref, bf16[4,512,352]{2,1,0:T(8,128)(2,1)} %get-tuple-element.149.refs_0_.act_ref, ...), custom_call_target="tpu_custom_call" | custom-call | flops 8858370048 | bytes 51380224 | tf_op jit(solution)/shard_map/pallas_call | solution.py:766
  302.1 10.4 %shard_map.346 = (f32[256,144]{1,0:T(8,128)}, bf16[256,144]{1,0:T(8,128)(2,1)}, bf16[256,144]{1,0:T(8,128)(2,1)}, bf16[256,144]{1,0:T(8,128)(2,1)}, bf16[256,768...) custom-call(s32[1]{0:T(128)} %bitcast.tensor_ref, s32[8]{0:T(128)} %copy-done.35, ...), custom_call_target="tpu_custom_call" | custom-call | flops 1744830464 | bytes 6376448 | tf_op jit(solution)/shard_map/pallas_call | solution.py:813
  351.5 13.2 %collective-permute-done.31 = bf16[128,2048]{1,0:T(8,128)(2,1)S(1)} collective-permute-done((bf16[128,2048]{1,0:T(8,128)(2,1)}, bf16[128,2048]{1,0:T(8,128)(2,1)S(1)}, u32[]{:S(2)}, u32[]{:S(2)}) %collective-permute-start.31) | collective-permute-done | bytes 524320 | tf_op jit(solution)/shard_map/ppermute | solution.py:74
  366.7 12.7 %shard_map.350 = bf16[8,288,256]{2,1,0:T(8,128)(2,1)} custom-call(s32[8]{0:T(128)} %copy-done.35, s32[1]{0:T(128)} %bitcast.tensor_ref, bf16[2048,256]{1,0:T(8,128)(2,1)} %get-tuple-element.189.refs_4_.delta_ref, bf16[2048,128]{1,0:T(8,128)(2,1)} %get-tuple-element.190.refs_2_.act_ref, bf16[8,272,2048]{2,1,0:T(8,128)(2,1)} %bitcast.129, ...), custom_call_target="tpu_custom_call" | custom-call | flops 3221225472 | bytes 16777216 | tf_op jit(solution)/shard_map/pallas_call | solution.py:784
  392.4 9.9 %collective-permute-done.52 = bf16[2,64,1024]{2,1,0:T(8,128)(2,1)S(1)} collective-permute-done((bf16[2,64,1024]{2,1,0:T(8,128)(2,1)S(1)}, bf16[2,64,1024]{2,1,0:T(8,128)(2,1)S(1)}, u32[]{:S(2)}, u32[]{:S(2)}) %collective-permute-start.52) | collective-permute-done | bytes 262176 | tf_op jit(solution)/shard_map/ppermute | solution.py:91
  415.0 7.4 %collective-permute-done.43 = bf16[64,2048]{1,0:T(8,128)(2,1)} collective-permute-done((bf16[64,2048]{1,0:T(8,128)(2,1)}, bf16[64,2048]{1,0:T(8,128)(2,1)}, u32[]{:S(2)}, u32[]{:S(2)}) %collective-permute-start.43) | collective-permute-done | bytes 262176 | tf_op jit(solution)/shard_map/ppermute | solution.py:74
  440.8 5.5 %collective-permute-done.46 = bf16[64,2048]{1,0:T(8,128)(2,1)S(1)} collective-permute-done((bf16[64,2048]{1,0:T(8,128)(2,1)S(1)}, bf16[64,2048]{1,0:T(8,128)(2,1)S(1)}, u32[]{:S(2)}, u32[]{:S(2)}) %collective-permute-start.46) | collective-permute-done | bytes 262176 | tf_op jit(solution)/shard_map/ppermute | solution.py:74
  (327 shorter events, 198.4 us)
Async XLA Ops:
  7.2 90.0 %all-gather.3.cloned.1.call-start = ((), (), s32[]{:S(2)}) async-start(), calls=%async_computation.1 | async-start | bytes 10027008 | tf_op jit(solution)/shard_map/all_gather | solution.py:886
  38.1 22.3 %collective-permute-start.4 = (bf16[64,2048]{1,0:T(8,128)(2,1)}, bf16[64,2048]{1,0:T(8,128)(2,1)}, u32[]{:S(2)}, u32[]{:S(2)}) collective-permute-start(bf16[64,2048]{1,0:T(8,128)(2,1)} %get-tuple-element.116), channel_id=1, source_target_pairs={{0,2},{1,3},{2,0},{3,1},{4,6},{5,7},{6,4},{7,5},{8,10},{9,11},{10,... | collective-permute-start | bytes 786440 | tf_op jit(solution)/shard_map/ppermute | solution.py:74
  41.7 18.8 %collective-permute-start.5 = (bf16[64,2048]{1,0:T(8,128)(2,1)}, bf16[64,2048]{1,0:T(8,128)(2,1)}, u32[]{:S(2)}, u32[]{:S(2)}) collective-permute-start(bf16[64,2048]{1,0:T(8,128)(2,1)} %get-tuple-element.117), channel_id=1, source_target_pairs={{0,3},{1,2},{2,1},{3,0},{4,7},{5,6},{6,5},{7,4},{8,11},{9,10},{10,... | collective-permute-start | bytes 786440 | tf_op jit(solution)/shard_map/ppermute | solution.py:74
  67.1 26.8 %collective-permute-start.6 = (bf16[64,2048]{1,0:T(8,128)(2,1)S(1)}, bf16[64,2048]{1,0:T(8,128)(2,1)S(1)}, u32[]{:S(2)}, u32[]{:S(2)}) collective-permute-start(bf16[64,2048]{1,0:T(8,128)(2,1)S(1)} %multiply_convert_fusion), channel_id=1, source_target_pairs={{0,1},{1,0},{2,3},{3,2},{4,5},{5,4},{6,7},{7,6},{8,9},{9,8},{10,11... | collective-permute-start | bytes 786440 | tf_op jit(solution)/shard_map/ppermute | solution.py:74
  94.1 28.1 %collective-permute-start.11 = (bf16[256,2048]{1,0:T(8,128)(2,1)S(1)}, bf16[256,2048]{1,0:T(8,128)(2,1)}, u32[]{:S(2)}, u32[]{:S(2)}) collective-permute-start(bf16[256,2048]{1,0:T(8,128)(2,1)S(1)} %pad_maximum_fusion.1.refs_1_.block_ref.refs_4_), channel_id=1, source_target_pairs={{0,16},{4,12},{8,24},{12,4},{16,0},{20,28},{24,8},{28,20},{1,17},{... | collective-permute-start | bytes 3145736 | tf_op jit(solution)/shard_map/ppermute | solution.py:91
  95.7 26.5 %collective-permute-start.14 = (bf16[256,2048]{1,0:T(8,128)(2,1)S(1)}, bf16[256,2048]{1,0:T(8,128)(2,1)}, u32[]{:S(2)}, u32[]{:S(2)}) collective-permute-start(bf16[256,2048]{1,0:T(8,128)(2,1)S(1)} %pad_maximum_fusion.1.refs_1_.block_ref.refs_4_), channel_id=1, source_target_pairs={{0,4},{4,0},{8,12},{12,8},{16,20},{20,16},{24,28},{28,24},{1,5},{5... | collective-permute-start | bytes 3145736 | tf_op jit(solution)/shard_map/ppermute | solution.py:74
  95.7 22.7 %collective-permute-start.9 = (bf16[256,2048]{1,0:T(8,128)(2,1)S(1)}, bf16[256,2048]{1,0:T(8,128)(2,1)S(1)}, u32[]{:S(2)}, u32[]{:S(2)}) collective-permute-start(bf16[256,2048]{1,0:T(8,128)(2,1)S(1)} %pad_maximum_fusion.1.refs_1_.block_ref.refs_4_), channel_id=1, source_target_pairs={{0,8},{4,20},{8,0},{12,28},{16,24},{20,4},{24,16},{28,12},{1,9},{5... | collective-permute-start | bytes 3145736 | tf_op jit(solution)/shard_map/ppermute | solution.py:91
  202.5 18.0 %collective-permute-start.20 = (bf16[2,256,1152]{2,1,0:T(8,128)(2,1)}, bf16[2,256,1152]{2,1,0:T(8,128)(2,1)}, u32[]{:S(2)}, u32[]{:S(2)}) collective-permute-start(bf16[2,256,1152]{2,1,0:T(8,128)(2,1)} %get-tuple-element.141), channel_id=1, source_target_pairs={{0,16},{4,12},{8,24},{12,4},{16,0},{20,28},{24,8},{28,20},{1,17},{... | collective-permute-start | bytes 3538952 | tf_op jit(solution)/shard_map/ppermute | solution.py:91
  215.9 39.4 %collective-permute-start.19 = (bf16[4,256,2048]{2,1,0:T(8,128)(2,1)}, bf16[4,256,2048]{2,1,0:T(8,128)(2,1)}, u32[]{:S(2)}, u32[]{:S(2)}) collective-permute-start(bf16[4,256,2048]{2,1,0:T(8,128)(2,1)} %shard_map.343), channel_id=1, source_target_pairs={{0,4},{4,0},{8,12},{12,8},{16,20},{20,16},{24,28},{28,24},{1,5},{5... | collective-permute-start | bytes 12582920 | tf_op jit(solution)/shard_map/ppermute | solution.py:74
  236.8 18.1 %collective-permute-start.28 = (bf16[64,1152]{1,0:T(8,128)(2,1)S(1)}, bf16[64,1152]{1,0:T(8,128)(2,1)S(1)}, u32[]{:S(2)}, u32[]{:S(2)}) collective-permute-start(bf16[64,1152]{1,0:T(8,128)(2,1)S(1)} %get-tuple-element.312), channel_id=1, source_target_pairs={{0,2},{1,3},{2,0},{3,1},{4,6},{5,7},{6,4},{7,5},{8,10},{9,11},{10,... | collective-permute-start | bytes 442376 | tf_op jit(solution)/shard_map/ppermute | solution.py:74
  265.3 29.0 %collective-permute-start.21 = (bf16[2,256,2048]{2,1,0:T(8,128)(2,1)}, bf16[2,256,2048]{2,1,0:T(8,128)(2,1)}, u32[]{:S(2)}, u32[]{:S(2)}) collective-permute-start(bf16[2,256,2048]{2,1,0:T(8,128)(2,1)} %get-tuple-element.146), channel_id=1, source_target_pairs={{0,16},{4,12},{8,24},{12,4},{16,0},{20,28},{24,8},{28,20},{1,17},{... | collective-permute-start | bytes 6291464 | tf_op jit(solution)/shard_map/ppermute | solution.py:91
  269.1 32.0 %collective-permute-start.32 = (bf16[72,2048]{1,0:T(8,128)(2,1)S(1)}, bf16[72,2048]{1,0:T(8,128)(2,1)S(1)}, u32[]{:S(2)}, u32[]{:S(2)}) collective-permute-start(bf16[72,2048]{1,0:T(8,128)(2,1)S(1)} %maximum_maximum_fusion.refs_0_), channel_id=1, source_target_pairs={{0,1},{1,0},{2,3},{3,2},{4,5},{5,4},{6,7},{7,6},{8,9},{9,8},{10,11... | collective-permute-start | bytes 884744 | tf_op jit(solution)/shard_map/ppermute | solution.py:74
  271.9 29.2 %collective-permute-start.33 = (bf16[72,2048]{1,0:T(8,128)(2,1)S(1)}, bf16[72,2048]{1,0:T(8,128)(2,1)S(1)}, u32[]{:S(2)}, u32[]{:S(2)}) collective-permute-start(bf16[72,2048]{1,0:T(8,128)(2,1)S(1)} %maximum_maximum_fusion.refs_0_), channel_id=1, source_target_pairs={{0,2},{1,3},{2,0},{3,1},{4,6},{5,7},{6,4},{7,5},{8,10},{9,11},{10,... | collective-permute-start | bytes 884744 | tf_op jit(solution)/shard_map/ppermute | solution.py:74
  271.9 29.2 %collective-permute-start.34 = (bf16[72,2048]{1,0:T(8,128)(2,1)S(1)}, bf16[72,2048]{1,0:T(8,128)(2,1)S(1)}, u32[]{:S(2)}, u32[]{:S(2)}) collective-permute-start(bf16[72,2048]{1,0:T(8,128)(2,1)S(1)} %maximum_maximum_fusion.refs_0_), channel_id=1, source_target_pairs={{0,3},{1,2},{2,1},{3,0},{4,7},{5,6},{6,5},{7,4},{8,11},{9,10},{10,... | collective-permute-start | bytes 884744 | tf_op jit(solution)/shard_map/ppermute | solution.py:74
  299.5 23.9 %collective-permute-start.30 = (bf16[1,256,2048]{2,1,0:T(8,128)(2,1)S(1)}, bf16[1,256,2048]{2,1,0:T(8,128)(2,1)}, u32[]{:S(2)}, u32[]{:S(2)}) collective-permute-start(bf16[1,256,2048]{2,1,0:T(8,128)(2,1)S(1)} %slice.486), channel_id=1, source_target_pairs={{0,8},{4,20},{8,0},{12,28},{16,24},{20,4},{24,16},{28,12},{1,9},{5... | collective-permute-start | bytes 3145736 | tf_op jit(solution)/shard_map/ppermute | solution.py:91
  344.1 20.6 %collective-permute-start.31 = (bf16[128,2048]{1,0:T(8,128)(2,1)}, bf16[128,2048]{1,0:T(8,128)(2,1)S(1)}, u32[]{:S(2)}, u32[]{:S(2)}) collective-permute-start(bf16[128,2048]{1,0:T(8,128)(2,1)} %pad_maximum_fusion.5), channel_id=1, source_target_pairs={{0,1},{1,0},{2,3},{3,2},{4,5},{5,4},{6,7},{7,6},{8,9},{9,8},{10,11... | collective-permute-start | bytes 1572872 | tf_op jit(solution)/shard_map/ppermute | solution.py:74
  344.9 20.2 %collective-permute-start.49 = (bf16[2,256,144]{2,1,0:T(8,128)(2,1)S(1)}, bf16[2,256,144]{2,1,0:T(8,128)(2,1)}, u32[]{:S(2)}, u32[]{:S(2)}) collective-permute-start(bf16[2,256,144]{2,1,0:T(8,128)(2,1)S(1)} %add_convert_fusion.3), channel_id=1, source_target_pairs={{0,16},{4,12},{8,24},{12,4},{16,0},{20,28},{24,8},{28,20},{1,17},{... | collective-permute-start | bytes 442376 | tf_op jit(solution)/shard_map/ppermute | solution.py:91
  347.1 57.8 %collective-permute-start.38 = (bf16[64,2048]{1,0:T(8,128)(2,1)}, bf16[64,2048]{1,0:T(8,128)(2,1)}, u32[]{:S(2)}, u32[]{:S(2)}) collective-permute-start(bf16[64,2048]{1,0:T(8,128)(2,1)} %get-tuple-element.184), channel_id=1, source_target_pairs={{0,1},{1,0},{2,3},{3,2},{4,5},{5,4},{6,7},{7,6},{8,9},{9,8},{10,11... | collective-permute-start | bytes 786440 | tf_op jit(solution)/shard_map/ppermute | solution.py:74
  348.4 57.1 %collective-permute-start.39 = (bf16[64,2048]{1,0:T(8,128)(2,1)}, bf16[64,2048]{1,0:T(8,128)(2,1)}, u32[]{:S(2)}, u32[]{:S(2)}) collective-permute-start(bf16[64,2048]{1,0:T(8,128)(2,1)} %get-tuple-element.185), channel_id=1, source_target_pairs={{0,2},{1,3},{2,0},{3,1},{4,6},{5,7},{6,4},{7,5},{8,10},{9,11},{10,... | collective-permute-start | bytes 786440 | tf_op jit(solution)/shard_map/ppermute | solution.py:74
  349.0 56.5 %collective-permute-start.40 = (bf16[64,2048]{1,0:T(8,128)(2,1)}, bf16[64,2048]{1,0:T(8,128)(2,1)}, u32[]{:S(2)}, u32[]{:S(2)}) collective-permute-start(bf16[64,2048]{1,0:T(8,128)(2,1)} %get-tuple-element.186), channel_id=1, source_target_pairs={{0,3},{1,2},{2,1},{3,0},{4,7},{5,6},{6,5},{7,4},{8,11},{9,10},{10,... | collective-permute-start | bytes 786440 | tf_op jit(solution)/shard_map/ppermute | solution.py:74
  364.7 22.9 %collective-permute-start.42 = (bf16[2,256,768]{2,1,0:T(8,128)(2,1)}, bf16[2,256,768]{2,1,0:T(8,128)(2,1)}, u32[]{:S(2)}, u32[]{:S(2)}) collective-permute-start(bf16[2,256,768]{2,1,0:T(8,128)(2,1)} %add_convert_fusion), channel_id=1, source_target_pairs={{0,16},{4,12},{8,24},{12,4},{16,0},{20,28},{24,8},{28,20},{1,17},{... | collective-permute-start | bytes 2359304 | tf_op jit(solution)/shard_map/ppermute | solution.py:91
  379.4 34.3 %all-to-all-start = ((bf16[8,288,256]{2,1,0:T(8,128)(2,1)}), bf16[8,288,256]{2,1,0:T(8,128)(2,1)S(1)}, u32[]{:S(2)}, u32[]{:S(2)}) async-start(bf16[8,288,256]{2,1,0:T(8,128)(2,1)} %shard_map.350), calls=%async_computation | async-start | bytes 2359296 | tf_op jit(solution)/shard_map/all_to_all | solution.py:1124
  386.5 44.6 %collective-permute-start.57 = (bf16[4,560,256]{2,1,0:T(8,128)(2,1)}, bf16[4,560,256]{2,1,0:T(8,128)(2,1)}, u32[]{:S(2)}, u32[]{:S(2)}) collective-permute-start(bf16[4,560,256]{2,1,0:T(8,128)(2,1)} %get-tuple-element.204), channel_id=1, source_target_pairs={{0,4},{4,0},{8,12},{12,8},{16,20},{20,16},{24,28},{28,24},{1,5},{5... | collective-permute-start | bytes 3440648 | tf_op jit(solution)/shard_map/ppermute | solution.py:74
  402.3 24.1 %collective-permute-start.47 = (bf16[1,256,768]{2,1,0:T(8,128)(2,1)}, bf16[1,256,768]{2,1,0:T(8,128)(2,1)}, u32[]{:S(2)}, u32[]{:S(2)}) collective-permute-start(bf16[1,256,768]{2,1,0:T(8,128)(2,1)} %slice.489), channel_id=1, source_target_pairs={{0,8},{4,20},{8,0},{12,28},{16,24},{20,4},{24,16},{28,12},{1,9},{5... | collective-permute-start | bytes 1179656 | tf_op jit(solution)/shard_map/ppermute | solution.py:91
  (79 other events, 821.0 us)
Sparse Core Ops, SparseCore 0:
  10.8 59.2 all-gather.2

commit v4 on v3

--- a/solution.py
+++ b/solution.py
@@ -116,22 +116,11 @@
     return [array] + [swap(array, axis, r) for r in range(1, lax.axis_size(axis))]
 
 
-def share_far_first(array, axis):
-    blocks = {0: array}
-    bit = lax.axis_size(axis) // 2
-    while bit:
-        blocks.update(
-            {r ^ bit: swap(block, axis, bit) for r, block in blocks.items()}
-        )
-        bit //= 2
-    return [blocks[r] for r in range(len(blocks))]
-
-
 def trade(blocks, axis):
     return [blocks[0]] + [swap(blocks[r], axis, r) for r in range(1, len(blocks))]
 
 
-def sum_along(blocks, sent, axis):
+def sum_along(blocks, sent, axis, others):
     bit, got = 1, sent
     while True:
         stay = [r for r in blocks if not r & bit]
@@ -146,6 +135,7 @@
         got = swap(
             jnp.concatenate([blocks[r].astype(bf16) for r in blocks if r & bit], axis=0), axis, bit
         )
+        got = after(got, others)
 
 
 def gather_chips(block, between):
@@ -950,7 +940,7 @@
     hidden_one = tokens_own + attn_sum
     ffn_normed_f, inv_second = rms_norm(hidden_one, ffn_gain)
     ffn_own = ffn_normed_f.astype(bf16)
-    ffn_block = jnp.concatenate(share_far_first(ffn_own, "tensor"), axis=0)
+    ffn_block = jnp.concatenate(share(ffn_own, "tensor"), axis=0)
     near_blocks = gather_chips(ffn_block, grad_rows)
     far_blocks = [swap(block, "dp", 1) for block in near_blocks[:-1]]
 
@@ -1010,10 +1000,6 @@
         return arrived[:1] + after(arrived[1:], out_other)
 
     sums, arrivals = sum_chips(mine, beside)
-    out_pair = return_rows(
-        1, slots, [act], [expert_down], shared_act, shared_out, None, 0, width,
-        after(swap(out_other[0], "dp", 1), arrivals[0]),
-    )
     shared_rows = shared_cols + -shared_cols % 16
     back_sums = [total(send_back(s)) for s in sums]
     back_sum = jnp.concatenate(back_sums[:-1] + [back_sums[-1][:, :size]], axis=1)
@@ -1040,14 +1026,15 @@
         axis=0,
     )
     message = jnp.concatenate([hidden_grad.astype(bf16), extra], axis=0)
-    message = after(message, out_pair)
     shared_grads_t = share(message, "tensor")
-    expert_gate_grad, expert_up_grad, expert_down_grad = expert_grads(
-        rows, grad_rows, *after((act, gate_delta, up_delta), message)
-    )
-    out_sums, out_steps = sum_chips([out_pair], lambda step, arrived: after(arrived, expert_gate_grad))
-    out_here = out_sums[0]
-    shared_grads_t = after(shared_grads_t, expert_gate_grad, out_steps[1])
+    out_pair = return_rows(
+        1, slots, [act], [expert_down], shared_act, shared_out, None, 0, width,
+        after(swap(out_other[0], "dp", 1), message),
+    )
+    shared_all = shared_grads(
+        src, tensor, n_t, blocks, cot_all, *after((shared_delta, shared_act), out_pair), shared_rows
+    )
+    shared_grads_t = after(shared_grads_t, shared_all)
 
     lat_rows = lat_rank // n_d
     results = single(
@@ -1100,13 +1087,12 @@
         scratch=[pltpu.VMEM((toks, width), bf16)],
         flops=2 * toks * width * height,
     )
-    query_terms = rows_grad(after(normed_p, out_steps[2]), query_grad_p)
+    query_terms = rows_grad(normed_p, query_grad_p)
     terms = [query_terms, column_terms, (kv_up_far, kv_up_near)]
+    latent_parts = after(trade(latent_parts, "tensor"), terms)
+    out_sums, out_steps = sum_chips([out_pair], lambda step, arrived: after(arrived, latent_parts))
+    out_here = out_sums[0]
     out_rows = {r: out_here[r * own_toks : (r + 1) * own_toks] for r in range(n_t)}
-    out_sent = swap(
-        jnp.concatenate([out_rows[r].astype(bf16) for r in out_rows if r & 1], axis=0), "tensor", 1
-    )
-    latent_parts = after(trade(latent_parts, "tensor"), terms)
     results = single(
         functools.partial(normed_back_kernel, n_t),
         [shape(f32 if r == 0 else bf16, own_toks, width) for r in range(n_t)]
@@ -1118,22 +1104,33 @@
     )
     normed_part, narrow_p = results[:n_t], results[n_t]
     query_pairs = sum_cores(after(terms[:1], normed_part))
-    shared_all = shared_grads(
-        src, tensor, n_t, blocks, cot_all, *after((shared_delta, shared_act), out_sent, query_pairs[0][1]), shared_rows
-    )
-    shared_sent = lax.all_to_all(shared_all, "dp", 0, 0, tiled=True).astype(f32)
+    expert_gate_grad, expert_up_grad, expert_down_grad = expert_grads(
+        rows, grad_rows, *after((act, gate_delta, up_delta), query_pairs[0][1], out_steps[1])
+    )
+    shared_sent = lax.all_to_all(after(shared_all, expert_gate_grad), "dp", 0, 0, tiled=True).astype(f32)
     shared_gate_grad, shared_up_grad, shared_down_grad = [
         shared_sent[:, i * shared_rows : i * shared_rows + shared_cols].reshape(-1, rows_d)
         for i in range(3)
     ]
+    out_message = after(
+        jnp.concatenate([out_rows[r].astype(bf16) for r in out_rows if r & 1], axis=0),
+        expert_gate_grad,
+    )
+    out_sent = swap(out_message, "tensor", 1)
+    normed_arrived = after(trade(normed_part, "tensor"), expert_gate_grad)
+    normed_grad = total(normed_arrived)
     (q_weight_grad,), term_arrivals = sum_chips(query_pairs)
-    terms = terms[1:] + [rows_grad(normed_p, narrow_p)]
-    (columns, kv_up_grad, narrow_grad), _ = sum_chips(sum_cores(after(terms, query_pairs[0][1])))
-    normed_arrived = after(trade(normed_part, "tensor"), term_arrivals[0], shared_all)
-    normed_grad = total(normed_arrived)
-    out_sum = sum_along(out_rows, after(out_sent, normed_arrived[1:]), "tensor")
+    terms = terms[1:] + [rows_grad(normed_p, after(narrow_p, expert_gate_grad))]
+    pairs = after(sum_cores(after(terms, expert_gate_grad, out_message)), term_arrivals[0])
+    (columns, kv_up_grad, narrow_grad), chain = sum_chips(
+        pairs, lambda step, arrived: after(arrived, term_arrivals[min(2 * step + 2, len(term_arrivals) - 2)])
+    )
+    sends = [send for _, send in pairs] + term_arrivals[1]
+    out_sum = sum_along(
+        out_rows, after(out_sent, normed_arrived[1:], sends), "tensor", chain[1] or sends
+    )
     output_own = (hidden_one + out_sum).astype(bf16)
-    output = reorder(jnp.concatenate(share_far_first(output_own, "tensor"), axis=0), "tensor", 0)
+    output_blocks = share(after(output_own, chain[-2]), "tensor")
     inv_first_own = block_at(inv_first, t_index, own_toks, 0)
     input_norm_grad, _ = rms_back(normed_grad, tokens_own, inv_first_own, attn_gain)
     input_grad = hidden_grad + input_norm_grad
@@ -1162,6 +1159,7 @@
         [attn_gain_part.reshape(n_t, 1, -1), kv_gain_part.reshape(n_t, 1, -1)], axis=2
     )
     gains = total(trade([b[0] for b in by_partner(gains, "tensor", 0)], "tensor"))[0]
+    output = reorder(jnp.concatenate(after(output_blocks, gains), axis=0), "tensor", 0)
     attn_gain_grad = gains[:device_rows]
     kv_gain_grad = gains[device_rows:]
 

time: 473 us -> 451 us (0.953)
  waiting for transfers between devices: 112 us -> 81.8 us
  starting transfers between devices: 71.6 us -> 80.6 us
    ppermute x43, waiting for transfers between devices: 74.5 us -> 53.6 us  [swap(): return lax.ppermute(array, axis, [(i, i ^ bits) for i in range(count)])]
    ppermute x17, waiting for transfers between devices: 37.7 us -> 28.1 us  [swap_chips(): lax.ppermute(array, 'dp', [(i, i ^ chip_bits(i % 2)[step]) for i in range...]
    ppermute x43, starting transfers between devices: 47.5 us -> 55.9 us  [swap(): return lax.ppermute(array, axis, [(i, i ^ bits) for i in range(count)])]
    unnamed x91 -> x102, local copies, waits for them, and re-layouts: 8.31 us -> 10.5 us
  transfers between devices with their start and end apart: 62 -> 62, of which waited for: 20 -> 18; matrix products, arithmetic and copies ran while one was open for 13% -> 14% of each run, Pallas kernels for 26% -> 31%
where the time goes in v4:
time: 451 us; the launch traced here: 444 us
  Pallas kernels  174 us (39%)
  waiting for transfers between devices  81.8 us (18%)
  starting transfers between devices  80.6 us (18%)
  other arithmetic  48.9 us (11%)
  between operations  30.8 us (7%)
  local copies, waits for them, and re-layouts  26.6 us (6%)
    ppermute x43, starting transfers between devices, swap(): return lax.ppermute(array, axis, [(i, i ^ bits) for i in range(count)])  55.9 us
    ppermute x43, waiting for transfers between devices, swap(): return lax.ppermute(array, axis, [(i, i ^ bits) for i in range(count)])  53.6 us
    pallas_call x6, Pallas kernels, return_rows(): pl.pallas_call(functools.partial(return_kernel, (len(deltas), score is no...  51.5 us
    pallas_call x8, Pallas kernels, single(): pl.pallas_call(kernel, grid_spec=pltpu.PrefetchScalarGridSpec(num_scalar_...  40.6 us
    ppermute x17, waiting for transfers between devices, swap_chips(): lax.ppermute(array, 'dp', [(i, i ^ chip_bits(i % 2)[step]) for i in range...  28.1 us
    ppermute x17, starting transfers between devices, swap_chips(): lax.ppermute(array, 'dp', [(i, i ^ chip_bits(i % 2)[step]) for i in range...  20.8 us
    pallas_call x1, Pallas kernels, expert_hidden(): pl.pallas_call(hidden_kernel, grid=(experts,), in_specs=[pl.BlockSpec(mem...  19.8 us
    pallas_call x1, Pallas kernels, expert_grads(): pl.pallas_call(expert_grad_kernel, grid=(experts,), in_specs=[per_expert(...  19.7 us
  transfers between devices with their start and end apart: 62, of which 18 were waited for; matrix products, arithmetic and copies ran while one was open for 14% of the time, Pallas kernels for 31%

profile of v4, /device:TPU:0, one launch (start us, length us, event | category | flops | bytes accessed | tf_op | source)
XLA Modules:
  0.0 443.6 jit_solution(5391502534912496158)
XLA Ops:
  13.7 5.0 %collective-permute-start.2 = (bf16[256,144]{1,0:T(8,128)(2,1)}, bf16[256,144]{1,0:T(8,128)(2,1)S(1)}, u32[]{:S(2)}, u32[]{:S(2)}) collective-permute-start(bf16[256,144]{1,0:T(8,128)(2,1)} %get-tuple-element.132.refs_0_), channel_id=1, source_target_pairs={{0,3},{1,2},{2,1},{3,0},{4,7},{5,6},{6,5},{7,4},{8,11},{9,10},{10,... | collective-permute-start | bytes 221192 | tf_op jit(solution)/shard_map/ppermute | solution.py:74
  31.2 6.0 %shard_map.334 = (f32[64,2048]{1,0:T(8,128)}, bf16[64,2048]{1,0:T(8,128)(2,1)}, bf16[64,2048]{1,0:T(8,128)(2,1)}, bf16[64,2048]{1,0:T(8,128)(2,1)}, bf16[256,512...) custom-call(s32[1]{0:T(128)} %bitcast.tensor_ref, ...), custom_call_target="tpu_custom_call" | custom-call | flops 1073741824 | bytes 4245504 | tf_op jit(solution)/shard_map/pallas_call | solution.py:803
  49.4 11.0 %collective-permute-done.4 = bf16[64,2048]{1,0:T(8,128)(2,1)} collective-permute-done((bf16[64,2048]{1,0:T(8,128)(2,1)}, bf16[64,2048]{1,0:T(8,128)(2,1)}, u32[]{:S(2)}, u32[]{:S(2)}) %collective-permute-start.4) | collective-permute-done | bytes 262176 | tf_op jit(solution)/shard_map/ppermute | solution.py:74
  64.5 6.0 %collective-permute-start.7 = (bf16[64,2048]{1,0:T(8,128)(2,1)S(1)}, bf16[64,2048]{1,0:T(8,128)(2,1)S(1)}, u32[]{:S(2)}, u32[]{:S(2)}) collective-permute-start(bf16[64,2048]{1,0:T(8,128)(2,1)S(1)} %multiply_convert_fusion), channel_id=1, source_target_pairs={{0,2},{1,3},{2,0},{3,1},{4,6},{5,7},{6,4},{7,5},{8,10},{9,11},{10,... | collective-permute-start | bytes 786440 | tf_op jit(solution)/shard_map/ppermute | solution.py:74
  92.4 12.3 %shard_map.335 = (bf16[4,512,2048]{2,1,0:T(8,128)(2,1)}, f32[2048,128]{1,0:T(8,128)}) custom-call(s32[8]{0:T(128)} %copy-done.37, s32[1]{0:T(128)} %bitcast.tensor_ref, s32[8,4,256]{2,1,0:T(4,128)} %convert_element_type.314.slots_ref, bf16[8,272,2048]{2,1,0:T(8,128)(2,1)} %bitcast.128, bf16[128,2048]{1,0:T(8,128)(2,1)} %pad.16.down_ref.refs_3_), custom_call_target="tpu_custom_call" | custom-call | flops 3221225472 | bytes 16777216 | tf_op jit(solution)/shard_map/pallas_call | solution.py:602
  104.7 8.1 %collective-permute-done.9.refs_2_.refs_5_ = bf16[256,2048]{1,0:T(8,128)(2,1)S(1)} collective-permute-done((bf16[256,2048]{1,0:T(8,128)(2,1)S(1)}, bf16[256,2048]{1,0:T(8,128)(2,1)S(1)}, u32[]{:S(2)}, u32[]{:S(2)}) %collective-permute-start.9) | collective-permute-done | bytes 1048608 | tf_op jit(solution)/shard_map/ppermute | solution.py:91
  115.8 8.6 %shard_map.336 = (bf16[4,512,2048]{2,1,0:T(8,128)(2,1)}, f32[4,512,128]{2,1,0:T(8,128)}, bf16[2048,128]{1,0:T(8,128)(2,1)}, bf16[2048,256]{1,0:T(8,128)(2,1)}) custom-call(s32[8,4,256]{2,1,0:T(4,128)} %convert_element_type.314.slots_ref, bf16[96,2048]{1,0:T(8,128)(2,1)} %pad_maximum_fusion.5.router_ref, bf16[256,2048]{1,0:T(8,128)(2,1)} %fusion.6.weights_ref.refs_5_, ...), custom_call_target="tpu_custom_call" | custom-call | flops 2550136832 | bytes 8388608 | tf_op jit(solution)/shard_map/pallas_call | solution.py:641
  132.5 8.5 %shard_map.337 = (bf16[4,512,2048]{2,1,0:T(8,128)(2,1)}, f32[4,512,128]{2,1,0:T(8,128)}, bf16[2048,128]{1,0:T(8,128)(2,1)}, bf16[2048,256]{1,0:T(8,128)(2,1)}) custom-call(s32[8,4,256]{2,1,0:T(4,128)} %convert_element_type.314.slots_ref, ...), custom_call_target="tpu_custom_call", output_to_operand_aliasing={{0}: (8, {}), {1}: (9, {}), {2}: (10, {}), {3}: (11, {})} | custom-call | flops 2550136832 | bytes 8388608 | tf_op jit(solution)/shard_map/pallas_call | solution.py:641
  141.0 19.8 %shard_map.338 = (bf16[4,512,352]{2,1,0:T(8,128)(2,1)}, bf16[4,512,352]{2,1,0:T(8,128)(2,1)}, bf16[4,512,352]{2,1,0:T(8,128)(2,1)}, bf16[4,512,128]{2,1,0:T(8,128)(2,1)}) custom-call(s32[1]{0:T(128)} %bitcast.19.first_ref, bf16[4,512,2048]{2,1,0:T(8,128)(2,1)} %get-tuple-element.150.rows_ref, bf16[4,512,2048]{2,1,0:T(8,128)(2,1)} %get-tuple-element.143.grads_ref, ...), custom_call_target="tpu_custom_call" | custom-call | flops 8858370048 | bytes 34078720 | tf_op jit(solution)/shard_map/pallas_call | solution.py:685
  160.8 7.6 %shard_map.339 = bf16[4,256,1024]{2,1,0:T(8,128)(2,1)} custom-call(s32[8,4,256]{2,1,0:T(4,128)} %convert_element_type.314.slots_ref, bf16[4,512,352]{2,1,0:T(8,128)(2,1)} %get-tuple-element.205.refs_0_.gate_delta_ref, bf16[4,512,352]{2,1,0:T(8,128)(2,1)} %get-tuple-element.206.refs_1_.up_delta_ref, bf16[4,352,2048]{2,1,0:T(8,128)(2,1)} %bitcast.118, ...), custom_call_target="tpu_custom_call" | custom-call | flops 2550136832 | bytes 7864320 | tf_op jit(solution)/shard_map/pallas_call | solution.py:727
  168.5 8.0 %shard_map.341 = bf16[4,256,1152]{2,1,0:T(8,128)(2,1)} custom-call(s32[8,4,256]{2,1,0:T(4,128)} %convert_element_type.314.slots_ref, bf16[4,512,352]{2,1,0:T(8,128)(2,1)} %get-tuple-element.205.refs_0_.gate_delta_ref, bf16[4,512,352]{2,1,0:T(8,128)(2,1)} %get-tuple-element.206.refs_1_.up_delta_ref, bf16[4,352,2048]{2,1,0:T(8,128)(2,1)} %bitcast.119, ...), custom_call_target="tpu_custom_call" | custom-call | flops 2550136832 | bytes 7864320 | tf_op jit(solution)/shard_map/pallas_call | solution.py:727
  178.2 8.0 %shard_map.340 = (bf16[2,256,1024]{2,1,0:T(8,128)(2,1)}, bf16[2,256,1024]{2,1,0:T(8,128)(2,1)}) custom-call(s32[8,4,256]{2,1,0:T(4,128)} %convert_element_type.314.slots_ref, bf16[4,512,352]{2,1,0:T(8,128)(2,1)} %get-tuple-element.205.refs_0_.gate_delta_ref, bf16[4,512,352]{2,1,0:T(8,128)(2,1)} %get-tuple-element.206.refs_1_.up_delta_ref, ...), custom_call_target="tpu_custom_call" | custom-call | flops 2550136832 | bytes 7864320 | tf_op jit(solution)/shard_map/pallas_call | solution.py:727
  187.7 9.0 %shard_map.342 = (bf16[2,256,1152]{2,1,0:T(8,128)(2,1)}, bf16[2,256,1152]{2,1,0:T(8,128)(2,1)}) custom-call(s32[8,4,256]{2,1,0:T(4,128)} %convert_element_type.314.slots_ref, bf16[4,512,352]{2,1,0:T(8,128)(2,1)} %get-tuple-element.205.refs_0_.gate_delta_ref, bf16[4,512,352]{2,1,0:T(8,128)(2,1)} %get-tuple-element.206.refs_1_.up_delta_ref, ...), custom_call_target="tpu_custom_call" | custom-call | flops 2550136832 | bytes 7864320 | tf_op jit(solution)/shard_map/pallas_call | solution.py:727
  205.8 9.0 %shard_map.343 = bf16[4,256,2048]{2,1,0:T(8,128)(2,1)} custom-call(s32[8,4,256]{2,1,0:T(4,128)} %convert_element_type.314.slots_ref, bf16[4,512,352]{2,1,0:T(8,128)(2,1)} %get-tuple-element.204.refs_0_.act_ref, bf16[4,352,2048]{2,1,0:T(8,128)(2,1)} %refs_1_.3, bf16[2048,128]{1,0:T(8,128)(2,1)} %get-tuple-element.174.refs_2_.act_ref, ...), custom_call_target="tpu_custom_call" | custom-call | flops 3087007744 | bytes 9961472 | tf_op jit(solution)/shard_map/pallas_call | solution.py:727
  239.2 7.5 %collective-permute-done.22 = bf16[64,1024]{1,0:T(8,128)(2,1)S(1)} collective-permute-done((bf16[64,1024]{1,0:T(8,128)(2,1)S(1)}, bf16[64,1024]{1,0:T(8,128)(2,1)S(1)}, u32[]{:S(2)}, u32[]{:S(2)}) %collective-permute-start.22) | collective-permute-done | bytes 131104 | tf_op jit(solution)/shard_map/ppermute | solution.py:74
  246.8 4.9 %collective-permute-done.27 = bf16[64,1152]{1,0:T(8,128)(2,1)S(1)} collective-permute-done((bf16[64,1152]{1,0:T(8,128)(2,1)S(1)}, bf16[64,1152]{1,0:T(8,128)(2,1)S(1)}, u32[]{:S(2)}, u32[]{:S(2)}) %collective-permute-start.27) | collective-permute-done | bytes 147488 | tf_op jit(solution)/shard_map/ppermute | solution.py:74
  258.5 10.0 %shard_map.344 = (bf16[2,256,2048]{2,1,0:T(8,128)(2,1)}, bf16[2,256,2048]{2,1,0:T(8,128)(2,1)}) custom-call(s32[8,4,256]{2,1,0:T(4,128)} %convert_element_type.314.slots_ref, bf16[4,512,352]{2,1,0:T(8,128)(2,1)} %get-tuple-element.204.refs_0_.act_ref, bf16[4,352,2048]{2,1,0:T(8,128)(2,1)} %refs_1_.3, bf16[2048,128]{1,0:T(8,128)(2,1)} %get-tuple-element.174.refs_2_.act_ref, ...), custom_call_target="tpu_custom_call" | custom-call | flops 3087007744 | bytes 9961472 | tf_op jit(solution)/shard_map/pallas_call | solution.py:727
  268.6 12.8 %shard_map.345 = bf16[8,288,256]{2,1,0:T(8,128)(2,1)} custom-call(s32[8]{0:T(128)} %copy-done.37, s32[1]{0:T(128)} %bitcast.tensor_ref, bf16[2048,256]{1,0:T(8,128)(2,1)} %get-tuple-element.173.refs_4_.delta_ref, bf16[2048,128]{1,0:T(8,128)(2,1)} %get-tuple-element.174.refs_2_.act_ref, bf16[8,272,2048]{2,1,0:T(8,128)(2,1)} %bitcast.129, ...), custom_call_target="tpu_custom_call" | custom-call | flops 3221225472 | bytes 16777216 | tf_op jit(solution)/shard_map/pallas_call | solution.py:774
  283.2 10.5 %shard_map.346 = (f32[256,144]{1,0:T(8,128)}, bf16[256,144]{1,0:T(8,128)(2,1)}, bf16[256,144]{1,0:T(8,128)(2,1)}, bf16[256,144]{1,0:T(8,128)(2,1)}, bf16[256,768...) custom-call(s32[1]{0:T(128)} %bitcast.tensor_ref, s32[8]{0:T(128)} %copy-done.37, ...), custom_call_target="tpu_custom_call" | custom-call | flops 1744830464 | bytes 6376448 | tf_op jit(solution)/shard_map/pallas_call | solution.py:803
  308.1 4.9 %shard_map.349 = (f32[64,2048]{1,0:T(8,128)}, bf16[64,2048]{1,0:T(8,128)(2,1)}, bf16[64,2048]{1,0:T(8,128)(2,1)}, bf16[64,2048]{1,0:T(8,128)(2,1)}, bf16[256,144]{1,0:T(8,128)(2,1)}) custom-call(s32[1]{0:T(128)} %bitcast.tensor_ref, bf16[256,768]{1,0:T(8,128)(2,1)} %get-tuple-element.183.right_ref.query_grad_ref, bf16[2048,768]{1,0:T(8,128)(2,1)} %query_weight_ref.1, ...), custom_call_target="tpu_custom_call" | custom-call | flops 956301312 | bytes 4497408 | tf_op jit(solution)/shard_map/pallas_call | solution.py:803
  329.7 19.7 %shard_map.350 = (f32[4,352,2048]{2,1,0:T(8,128)}, f32[4,352,2048]{2,1,0:T(8,128)}, f32[4,352,2048]{2,1,0:T(8,128)}) custom-call(bf16[4,512,2048]{2,1,0:T(8,128)(2,1)} %get-tuple-element.150.rows_ref, bf16[4,512,2048]{2,1,0:T(8,128)(2,1)} %get-tuple-element.143.grads_ref, bf16[4,512,352]{2,1,0:T(8,128)(2,1)} %get-tuple-element.204.refs_0_.act_ref, ...), custom_call_target="tpu_custom_call" | custom-call | flops 8858370048 | bytes 51380224 | tf_op jit(solution)/shard_map/pallas_call | solution.py:756
  383.3 6.3 %collective-permute-done.38 = bf16[128,2048]{1,0:T(8,128)(2,1)} collective-permute-done((bf16[128,2048]{1,0:T(8,128)(2,1)}, bf16[128,2048]{1,0:T(8,128)(2,1)}, u32[]{:S(2)}, u32[]{:S(2)}) %collective-permute-start.38) | collective-permute-done | bytes 524320 | tf_op jit(solution)/shard_map/ppermute | solution.py:74
  397.8 6.7 %collective-permute-done.46 = bf16[64,2048]{1,0:T(8,128)(2,1)S(1)} collective-permute-done((bf16[64,2048]{1,0:T(8,128)(2,1)S(1)}, bf16[64,2048]{1,0:T(8,128)(2,1)S(1)}, u32[]{:S(2)}, u32[]{:S(2)}) %collective-permute-start.46) | collective-permute-done | bytes 262176 | tf_op jit(solution)/shard_map/ppermute | solution.py:74
  423.0 8.0 %collective-permute-done.58 = f32[1,80]{1,0:T(1,128)S(1)} collective-permute-done((f32[1,80]{1,0:T(1,128)S(1)}, f32[1,80]{1,0:T(1,128)S(1)}, u32[]{:S(2)}, u32[]{:S(2)}) %collective-permute-start.58) | collective-permute-done | bytes 352 | tf_op jit(solution)/shard_map/ppermute | solution.py:74
  (338 shorter events, 194.6 us)
Async XLA Ops:
  7.2 83.1 %all-gather.3.cloned.1.call-start = ((), (), s32[]{:S(2)}) async-start(), calls=%async_computation.1 | async-start | bytes 10027008 | tf_op jit(solution)/shard_map/all_gather | solution.py:876
  38.7 21.7 %collective-permute-start.4 = (bf16[64,2048]{1,0:T(8,128)(2,1)}, bf16[64,2048]{1,0:T(8,128)(2,1)}, u32[]{:S(2)}, u32[]{:S(2)}) collective-permute-start(bf16[64,2048]{1,0:T(8,128)(2,1)} %get-tuple-element.135), channel_id=1, source_target_pairs={{0,2},{1,3},{2,0},{3,1},{4,6},{5,7},{6,4},{7,5},{8,10},{9,11},{10,... | collective-permute-start | bytes 786440 | tf_op jit(solution)/shard_map/ppermute | solution.py:74
  41.7 18.8 %collective-permute-start.5 = (bf16[64,2048]{1,0:T(8,128)(2,1)}, bf16[64,2048]{1,0:T(8,128)(2,1)}, u32[]{:S(2)}, u32[]{:S(2)}) collective-permute-start(bf16[64,2048]{1,0:T(8,128)(2,1)} %get-tuple-element.136), channel_id=1, source_target_pairs={{0,3},{1,2},{2,1},{3,0},{4,7},{5,6},{6,5},{7,4},{8,11},{9,10},{10,... | collective-permute-start | bytes 786440 | tf_op jit(solution)/shard_map/ppermute | solution.py:74
  62.0 24.8 %collective-permute-start.8 = (bf16[64,2048]{1,0:T(8,128)(2,1)S(1)}, bf16[64,2048]{1,0:T(8,128)(2,1)S(1)}, u32[]{:S(2)}, u32[]{:S(2)}) collective-permute-start(bf16[64,2048]{1,0:T(8,128)(2,1)S(1)} %multiply_convert_fusion), channel_id=1, source_target_pairs={{0,3},{1,2},{2,1},{3,0},{4,7},{5,6},{6,5},{7,4},{8,11},{9,10},{10,... | collective-permute-start | bytes 786440 | tf_op jit(solution)/shard_map/ppermute | solution.py:74
  64.5 22.6 %collective-permute-start.7 = (bf16[64,2048]{1,0:T(8,128)(2,1)S(1)}, bf16[64,2048]{1,0:T(8,128)(2,1)S(1)}, u32[]{:S(2)}, u32[]{:S(2)}) collective-permute-start(bf16[64,2048]{1,0:T(8,128)(2,1)S(1)} %multiply_convert_fusion), channel_id=1, source_target_pairs={{0,2},{1,3},{2,0},{3,1},{4,6},{5,7},{6,4},{7,5},{8,10},{9,11},{10,... | collective-permute-start | bytes 786440 | tf_op jit(solution)/shard_map/ppermute | solution.py:74
  87.2 28.7 %collective-permute-start.14 = (bf16[256,2048]{1,0:T(8,128)(2,1)S(1)}, bf16[256,2048]{1,0:T(8,128)(2,1)}, u32[]{:S(2)}, u32[]{:S(2)}) collective-permute-start(bf16[256,2048]{1,0:T(8,128)(2,1)S(1)} %pad_maximum_fusion.1.refs_1_.refs_4_.block_ref), channel_id=1, source_target_pairs={{0,4},{4,0},{8,12},{12,8},{16,20},{20,16},{24,28},{28,24},{1,5},{5... | collective-permute-start | bytes 3145736 | tf_op jit(solution)/shard_map/ppermute | solution.py:74
  87.3 28.1 %collective-permute-start.11 = (bf16[256,2048]{1,0:T(8,128)(2,1)S(1)}, bf16[256,2048]{1,0:T(8,128)(2,1)}, u32[]{:S(2)}, u32[]{:S(2)}) collective-permute-start(bf16[256,2048]{1,0:T(8,128)(2,1)S(1)} %pad_maximum_fusion.1.refs_1_.refs_4_.block_ref), channel_id=1, source_target_pairs={{0,16},{4,12},{8,24},{12,4},{16,0},{20,28},{24,8},{28,20},{1,17},{... | collective-permute-start | bytes 3145736 | tf_op jit(solution)/shard_map/ppermute | solution.py:91
  88.9 24.0 %collective-permute-start.9 = (bf16[256,2048]{1,0:T(8,128)(2,1)S(1)}, bf16[256,2048]{1,0:T(8,128)(2,1)S(1)}, u32[]{:S(2)}, u32[]{:S(2)}) collective-permute-start(bf16[256,2048]{1,0:T(8,128)(2,1)S(1)} %pad_maximum_fusion.1.refs_1_.refs_4_.block_ref), channel_id=1, source_target_pairs={{0,8},{4,20},{8,0},{12,28},{16,24},{20,4},{24,16},{28,12},{1,9},{5... | collective-permute-start | bytes 3145736 | tf_op jit(solution)/shard_map/ppermute | solution.py:91
  196.7 22.8 %collective-permute-start.24 = (bf16[2,256,1152]{2,1,0:T(8,128)(2,1)}, bf16[2,256,1152]{2,1,0:T(8,128)(2,1)}, u32[]{:S(2)}, u32[]{:S(2)}) collective-permute-start(bf16[2,256,1152]{2,1,0:T(8,128)(2,1)} %get-tuple-element.160), channel_id=1, source_target_pairs={{0,16},{4,12},{8,24},{12,4},{16,0},{20,28},{24,8},{28,20},{1,17},{... | collective-permute-start | bytes 3538952 | tf_op jit(solution)/shard_map/ppermute | solution.py:91
  204.2 19.0 %collective-permute-start.20 = (bf16[1,256,1024]{2,1,0:T(8,128)(2,1)S(1)}, bf16[1,256,1024]{2,1,0:T(8,128)(2,1)}, u32[]{:S(2)}, u32[]{:S(2)}) collective-permute-start(bf16[1,256,1024]{2,1,0:T(8,128)(2,1)S(1)} %slice.488), channel_id=1, source_target_pairs={{0,8},{4,20},{8,0},{12,28},{16,24},{20,4},{24,16},{28,12},{1,9},{5... | collective-permute-start | bytes 1572872 | tf_op jit(solution)/shard_map/ppermute | solution.py:91
  214.8 43.8 %collective-permute-start.19 = (bf16[4,256,2048]{2,1,0:T(8,128)(2,1)}, bf16[4,256,2048]{2,1,0:T(8,128)(2,1)}, u32[]{:S(2)}, u32[]{:S(2)}) collective-permute-start(bf16[4,256,2048]{2,1,0:T(8,128)(2,1)} %shard_map.343), channel_id=1, source_target_pairs={{0,4},{4,0},{8,12},{12,8},{16,20},{20,16},{24,28},{28,24},{1,5},{5... | collective-permute-start | bytes 12582920 | tf_op jit(solution)/shard_map/ppermute | solution.py:74
  228.7 18.0 %collective-permute-start.22 = (bf16[64,1024]{1,0:T(8,128)(2,1)S(1)}, bf16[64,1024]{1,0:T(8,128)(2,1)S(1)}, u32[]{:S(2)}, u32[]{:S(2)}) collective-permute-start(bf16[64,1024]{1,0:T(8,128)(2,1)S(1)} %get-tuple-element.359), channel_id=1, source_target_pairs={{0,2},{1,3},{2,0},{3,1},{4,6},{5,7},{6,4},{7,5},{8,10},{9,11},{10,... | collective-permute-start | bytes 393224 | tf_op jit(solution)/shard_map/ppermute | solution.py:74
  254.1 27.3 %collective-permute-start.32 = (bf16[72,2048]{1,0:T(8,128)(2,1)S(1)}, bf16[72,2048]{1,0:T(8,128)(2,1)S(1)}, u32[]{:S(2)}, u32[]{:S(2)}) collective-permute-start(bf16[72,2048]{1,0:T(8,128)(2,1)S(1)} %maximum_maximum_fusion.refs_0_), channel_id=1, source_target_pairs={{0,3},{1,2},{2,1},{3,0},{4,7},{5,6},{6,5},{7,4},{8,11},{9,10},{10,... | collective-permute-start | bytes 884744 | tf_op jit(solution)/shard_map/ppermute | solution.py:74
  256.3 25.1 %collective-permute-start.31 = (bf16[72,2048]{1,0:T(8,128)(2,1)S(1)}, bf16[72,2048]{1,0:T(8,128)(2,1)S(1)}, u32[]{:S(2)}, u32[]{:S(2)}) collective-permute-start(bf16[72,2048]{1,0:T(8,128)(2,1)S(1)} %maximum_maximum_fusion.refs_0_), channel_id=1, source_target_pairs={{0,2},{1,3},{2,0},{3,1},{4,6},{5,7},{6,4},{7,5},{8,10},{9,11},{10,... | collective-permute-start | bytes 884744 | tf_op jit(solution)/shard_map/ppermute | solution.py:74
  256.3 25.1 %collective-permute-start.30 = (bf16[72,2048]{1,0:T(8,128)(2,1)S(1)}, bf16[72,2048]{1,0:T(8,128)(2,1)S(1)}, u32[]{:S(2)}, u32[]{:S(2)}) collective-permute-start(bf16[72,2048]{1,0:T(8,128)(2,1)S(1)} %maximum_maximum_fusion.refs_0_), channel_id=1, source_target_pairs={{0,1},{1,0},{2,3},{3,2},{4,5},{5,4},{6,7},{7,6},{8,9},{9,8},{10,11... | collective-permute-start | bytes 884744 | tf_op jit(solution)/shard_map/ppermute | solution.py:74
  282.3 41.0 %collective-permute-start.29 = (bf16[2,256,2048]{2,1,0:T(8,128)(2,1)}, bf16[2,256,2048]{2,1,0:T(8,128)(2,1)}, u32[]{:S(2)}, u32[]{:S(2)}) collective-permute-start(bf16[2,256,2048]{2,1,0:T(8,128)(2,1)} %get-tuple-element.166), channel_id=1, source_target_pairs={{0,16},{4,12},{8,24},{12,4},{16,0},{20,28},{24,8},{28,20},{1,17},{... | collective-permute-start | bytes 6291464 | tf_op jit(solution)/shard_map/ppermute | solution.py:91
  314.9 34.4 %collective-permute-start.39 = (bf16[64,2048]{1,0:T(8,128)(2,1)}, bf16[64,2048]{1,0:T(8,128)(2,1)}, u32[]{:S(2)}, u32[]{:S(2)}) collective-permute-start(bf16[64,2048]{1,0:T(8,128)(2,1)} %get-tuple-element.199), channel_id=1, source_target_pairs={{0,1},{1,0},{2,3},{3,2},{4,5},{5,4},{6,7},{7,6},{8,9},{9,8},{10,11... | collective-permute-start | bytes 786440 | tf_op jit(solution)/shard_map/ppermute | solution.py:74
  315.5 33.9 %collective-permute-start.40 = (bf16[64,2048]{1,0:T(8,128)(2,1)}, bf16[64,2048]{1,0:T(8,128)(2,1)}, u32[]{:S(2)}, u32[]{:S(2)}) collective-permute-start(bf16[64,2048]{1,0:T(8,128)(2,1)} %get-tuple-element.200), channel_id=1, source_target_pairs={{0,2},{1,3},{2,0},{3,1},{4,6},{5,7},{6,4},{7,5},{8,10},{9,11},{10,... | collective-permute-start | bytes 786440 | tf_op jit(solution)/shard_map/ppermute | solution.py:74
  317.7 31.7 %collective-permute-start.41 = (bf16[64,2048]{1,0:T(8,128)(2,1)}, bf16[64,2048]{1,0:T(8,128)(2,1)}, u32[]{:S(2)}, u32[]{:S(2)}) collective-permute-start(bf16[64,2048]{1,0:T(8,128)(2,1)} %get-tuple-element.201), channel_id=1, source_target_pairs={{0,3},{1,2},{2,1},{3,0},{4,7},{5,6},{6,5},{7,4},{8,11},{9,10},{10,... | collective-permute-start | bytes 786440 | tf_op jit(solution)/shard_map/ppermute | solution.py:74
  321.8 36.4 %collective-permute-start.45 = (bf16[2,256,768]{2,1,0:T(8,128)(2,1)}, bf16[2,256,768]{2,1,0:T(8,128)(2,1)}, u32[]{:S(2)}, u32[]{:S(2)}) collective-permute-start(bf16[2,256,768]{2,1,0:T(8,128)(2,1)} %add_convert_fusion), channel_id=1, source_target_pairs={{0,16},{4,12},{8,24},{12,4},{16,0},{20,28},{24,8},{28,20},{1,17},{... | collective-permute-start | bytes 2359304 | tf_op jit(solution)/shard_map/ppermute | solution.py:91
  328.8 33.5 %collective-permute-start.36 = (bf16[1,256,2048]{2,1,0:T(8,128)(2,1)}, bf16[1,256,2048]{2,1,0:T(8,128)(2,1)}, u32[]{:S(2)}, u32[]{:S(2)}) collective-permute-start(bf16[1,256,2048]{2,1,0:T(8,128)(2,1)} %slice.486), channel_id=1, source_target_pairs={{0,8},{4,20},{8,0},{12,28},{16,24},{20,4},{24,16},{28,12},{1,9},{5... | collective-permute-start | bytes 3145736 | tf_op jit(solution)/shard_map/ppermute | solution.py:91
  349.4 30.5 %all-to-all-start = ((bf16[8,288,256]{2,1,0:T(8,128)(2,1)}), bf16[8,288,256]{2,1,0:T(8,128)(2,1)S(1)}, u32[]{:S(2)}, u32[]{:S(2)}) async-start(bf16[8,288,256]{2,1,0:T(8,128)(2,1)} %shard_map.345), calls=%async_computation | async-start | bytes 2359296 | tf_op jit(solution)/shard_map/all_to_all | solution.py:1110
  406.6 25.6 %collective-permute-start.56 = (bf16[64,2048]{1,0:T(8,128)(2,1)S(1)}, bf16[64,2048]{1,0:T(8,128)(2,1)S(1)}, u32[]{:S(2)}, u32[]{:S(2)}) collective-permute-start(bf16[64,2048]{1,0:T(8,128)(2,1)S(1)} %fusion.18), channel_id=1, source_target_pairs={{0,3},{1,2},{2,1},{3,0},{4,7},{5,6},{6,5},{7,4},{8,11},{9,10},{10,... | collective-permute-start | bytes 786440 | tf_op jit(solution)/shard_map/ppermute | solution.py:74
  409.1 23.0 %collective-permute-start.55 = (bf16[64,2048]{1,0:T(8,128)(2,1)S(1)}, bf16[64,2048]{1,0:T(8,128)(2,1)S(1)}, u32[]{:S(2)}, u32[]{:S(2)}) collective-permute-start(bf16[64,2048]{1,0:T(8,128)(2,1)S(1)} %fusion.18), channel_id=1, source_target_pairs={{0,2},{1,3},{2,0},{3,1},{4,6},{5,7},{6,4},{7,5},{8,10},{9,11},{10,... | collective-permute-start | bytes 786440 | tf_op jit(solution)/shard_map/ppermute | solution.py:74
  (83 other events, 773.6 us)
Sparse Core Ops, SparseCore 0:
  10.8 59.2 all-gather.2

commit v5 on v4

--- a/solution.py
+++ b/solution.py
@@ -591,7 +591,9 @@
 
 def cost(flops, bytes_accessed, transcendentals=0):
     return pl.CostEstimate(
-        flops=int(flops), bytes_accessed=int(bytes_accessed), transcendentals=int(transcendentals)
+        flops=int(flops * 4),
+        bytes_accessed=int(bytes_accessed * 4),
+        transcendentals=int(transcendentals * 4),
     )
 
 

time: 451 us -> 450 us (level)
    unnamed x102 -> x84, local copies, waits for them, and re-layouts: 10.5 us -> 7.62 us
where the time goes in v5:
time: 450 us; the launch traced here: 443 us
  Pallas kernels  174 us (39%)
  waiting for transfers between devices  83.2 us (18%)
  starting transfers between devices  80.5 us (18%)
  other arithmetic  49.4 us (11%)
  between operations  30.8 us (7%)
  local copies, waits for them, and re-layouts  23.7 us (5%)
    ppermute x43, starting transfers between devices, swap(): return lax.ppermute(array, axis, [(i, i ^ bits) for i in range(count)])  55.7 us
    ppermute x43, waiting for transfers between devices, swap(): return lax.ppermute(array, axis, [(i, i ^ bits) for i in range(count)])  52.9 us
    pallas_call x6, Pallas kernels, return_rows(): pl.pallas_call(functools.partial(return_kernel, (len(deltas), score is no...  51.6 us
    pallas_call x8, Pallas kernels, single(): pl.pallas_call(kernel, grid_spec=pltpu.PrefetchScalarGridSpec(num_scalar_...  40.5 us
    ppermute x17, waiting for transfers between devices, swap_chips(): lax.ppermute(array, 'dp', [(i, i ^ chip_bits(i % 2)[step]) for i in range...  30.2 us
    ppermute x17, starting transfers between devices, swap_chips(): lax.ppermute(array, 'dp', [(i, i ^ chip_bits(i % 2)[step]) for i in range...  20.8 us
    pallas_call x1, Pallas kernels, expert_hidden(): pl.pallas_call(hidden_kernel, grid=(experts,), in_specs=[pl.BlockSpec(mem...  19.9 us
    pallas_call x1, Pallas kernels, expert_grads(): pl.pallas_call(expert_grad_kernel, grid=(experts,), in_specs=[per_expert(...  19.7 us
  transfers between devices with their start and end apart: 62, of which 18 were waited for; matrix products, arithmetic and copies ran while one was open for 14% of the time, Pallas kernels for 31%

profile of v5, /device:TPU:0, one launch (start us, length us, event | category | flops | bytes accessed | tf_op | source)
XLA Modules:
  0.0 442.5 jit_solution(15184246298110000015)
XLA Ops:
  13.7 5.0 %collective-permute-start.2 = (bf16[256,144]{1,0:T(8,128)(2,1)}, bf16[256,144]{1,0:T(8,128)(2,1)}, u32[]{:S(2)}, u32[]{:S(2)}) collective-permute-start(bf16[256,144]{1,0:T(8,128)(2,1)} %get-tuple-element.132.refs_0_), channel_id=1, source_target_pairs={{0,3},{1,2},{2,1},{3,0},{4,7},{5,6},{6,5},{7,4},{8,11},{9,10},{10,... | collective-permute-start | bytes 221192 | tf_op jit(solution)/shard_map/ppermute | solution.py:74
  30.5 6.0 %shard_map.334 = (f32[64,2048]{1,0:T(8,128)}, bf16[64,2048]{1,0:T(8,128)(2,1)}, bf16[64,2048]{1,0:T(8,128)(2,1)}, bf16[64,2048]{1,0:T(8,128)(2,1)}, bf16[256,512...) custom-call(s32[1]{0:T(128)} %bitcast.tensor_ref, ...), custom_call_target="tpu_custom_call" | custom-call | flops 4294967296 | bytes 16982016 | tf_op jit(solution)/shard_map/pallas_call | solution.py:805
  48.9 10.8 %collective-permute-done.4 = bf16[64,2048]{1,0:T(8,128)(2,1)} collective-permute-done((bf16[64,2048]{1,0:T(8,128)(2,1)}, bf16[64,2048]{1,0:T(8,128)(2,1)}, u32[]{:S(2)}, u32[]{:S(2)}) %collective-permute-start.4) | collective-permute-done | bytes 262176 | tf_op jit(solution)/shard_map/ppermute | solution.py:74
  63.8 6.0 %collective-permute-start.7 = (bf16[64,2048]{1,0:T(8,128)(2,1)S(1)}, bf16[64,2048]{1,0:T(8,128)(2,1)S(1)}, u32[]{:S(2)}, u32[]{:S(2)}) collective-permute-start(bf16[64,2048]{1,0:T(8,128)(2,1)S(1)} %multiply_convert_fusion), channel_id=1, source_target_pairs={{0,2},{1,3},{2,0},{3,1},{4,6},{5,7},{6,4},{7,5},{8,10},{9,11},{10,... | collective-permute-start | bytes 786440 | tf_op jit(solution)/shard_map/ppermute | solution.py:74
  91.8 12.3 %shard_map.335 = (bf16[4,512,2048]{2,1,0:T(8,128)(2,1)}, f32[2048,128]{1,0:T(8,128)}) custom-call(s32[8]{0:T(128)} %copy-done.21, s32[1]{0:T(128)} %bitcast.tensor_ref, s32[8,4,256]{2,1,0:T(4,128)} %convert_element_type.314.slots_ref, bf16[8,272,2048]{2,1,0:T(8,128)(2,1)} %bitcast.128, bf16[128,2048]{1,0:T(8,128)(2,1)} %pad.16.down_ref.refs_3_), custom_call_target="tpu_custom_call" | custom-call | flops 12884901888 | bytes 67108864 | tf_op jit(solution)/shard_map/pallas_call | solution.py:604
  104.1 8.3 %collective-permute-done.9.refs_2_.refs_5_ = bf16[256,2048]{1,0:T(8,128)(2,1)} collective-permute-done((bf16[256,2048]{1,0:T(8,128)(2,1)S(1)}, bf16[256,2048]{1,0:T(8,128)(2,1)}, u32[]{:S(2)}, u32[]{:S(2)}) %collective-permute-start.9) | collective-permute-done | bytes 1048608 | tf_op jit(solution)/shard_map/ppermute | solution.py:91
  114.3 8.6 %shard_map.336 = (bf16[4,512,2048]{2,1,0:T(8,128)(2,1)}, f32[4,512,128]{2,1,0:T(8,128)}, bf16[2048,128]{1,0:T(8,128)(2,1)}, bf16[2048,256]{1,0:T(8,128)(2,1)}) custom-call(s32[8,4,256]{2,1,0:T(4,128)} %convert_element_type.314.slots_ref, bf16[96,2048]{1,0:T(8,128)(2,1)} %pad_maximum_fusion.5.router_ref, bf16[256,2048]{1,0:T(8,128)(2,1)} %fusion.6.weights_ref.refs_5_, ...), custom_call_target="tpu_custom_call" | custom-call | flops 10200547328 | bytes 33554432 | tf_op jit(solution)/shard_map/pallas_call | solution.py:643
  131.0 8.6 %shard_map.337 = (bf16[4,512,2048]{2,1,0:T(8,128)(2,1)}, f32[4,512,128]{2,1,0:T(8,128)}, bf16[2048,128]{1,0:T(8,128)(2,1)}, bf16[2048,256]{1,0:T(8,128)(2,1)}) custom-call(s32[8,4,256]{2,1,0:T(4,128)} %convert_element_type.314.slots_ref, ...), custom_call_target="tpu_custom_call", output_to_operand_aliasing={{0}: (8, {}), {1}: (9, {}), {2}: (10, {}), {3}: (11, {})} | custom-call | flops 10200547328 | bytes 33554432 | tf_op jit(solution)/shard_map/pallas_call | solution.py:643
  139.6 19.9 %shard_map.338 = (bf16[4,512,352]{2,1,0:T(8,128)(2,1)}, bf16[4,512,352]{2,1,0:T(8,128)(2,1)}, bf16[4,512,352]{2,1,0:T(8,128)(2,1)}, bf16[4,512,128]{2,1,0:T(8,128)(2,1)}) custom-call(s32[1]{0:T(128)} %bitcast.19.first_ref, bf16[4,512,2048]{2,1,0:T(8,128)(2,1)} %get-tuple-element.150.rows_ref, bf16[4,512,2048]{2,1,0:T(8,128)(2,1)} %get-tuple-element.143.grads_ref, ...), custom_call_target="tpu_custom_call" | custom-call | flops 35433480192 | bytes 136314880 | tf_op jit(solution)/shard_map/pallas_call | solution.py:687
  159.4 7.6 %shard_map.339 = bf16[4,256,1024]{2,1,0:T(8,128)(2,1)} custom-call(s32[8,4,256]{2,1,0:T(4,128)} %convert_element_type.314.slots_ref, bf16[4,512,352]{2,1,0:T(8,128)(2,1)} %get-tuple-element.205.refs_0_.gate_delta_ref, bf16[4,512,352]{2,1,0:T(8,128)(2,1)} %get-tuple-element.206.refs_1_.up_delta_ref, bf16[4,352,2048]{2,1,0:T(8,128)(2,1)} %bitcast.133, ...), custom_call_target="tpu_custom_call" | custom-call | flops 10200547328 | bytes 31457280 | tf_op jit(solution)/shard_map/pallas_call | solution.py:729
  167.1 8.1 %shard_map.341 = bf16[4,256,1152]{2,1,0:T(8,128)(2,1)} custom-call(s32[8,4,256]{2,1,0:T(4,128)} %convert_element_type.314.slots_ref, bf16[4,512,352]{2,1,0:T(8,128)(2,1)} %get-tuple-element.205.refs_0_.gate_delta_ref, bf16[4,512,352]{2,1,0:T(8,128)(2,1)} %get-tuple-element.206.refs_1_.up_delta_ref, bf16[4,352,2048]{2,1,0:T(8,128)(2,1)} %bitcast.134, ...), custom_call_target="tpu_custom_call" | custom-call | flops 10200547328 | bytes 31457280 | tf_op jit(solution)/shard_map/pallas_call | solution.py:729
  176.8 8.1 %shard_map.340 = (bf16[2,256,1024]{2,1,0:T(8,128)(2,1)}, bf16[2,256,1024]{2,1,0:T(8,128)(2,1)}) custom-call(s32[8,4,256]{2,1,0:T(4,128)} %convert_element_type.314.slots_ref, bf16[4,512,352]{2,1,0:T(8,128)(2,1)} %get-tuple-element.205.refs_0_.gate_delta_ref, bf16[4,512,352]{2,1,0:T(8,128)(2,1)} %get-tuple-element.206.refs_1_.up_delta_ref, ...), custom_call_target="tpu_custom_call" | custom-call | flops 10200547328 | bytes 31457280 | tf_op jit(solution)/shard_map/pallas_call | solution.py:729
  186.8 8.8 %shard_map.342 = (bf16[2,256,1152]{2,1,0:T(8,128)(2,1)}, bf16[2,256,1152]{2,1,0:T(8,128)(2,1)}) custom-call(s32[8,4,256]{2,1,0:T(4,128)} %convert_element_type.314.slots_ref, bf16[4,512,352]{2,1,0:T(8,128)(2,1)} %get-tuple-element.205.refs_0_.gate_delta_ref, bf16[4,512,352]{2,1,0:T(8,128)(2,1)} %get-tuple-element.206.refs_1_.up_delta_ref, ...), custom_call_target="tpu_custom_call" | custom-call | flops 10200547328 | bytes 31457280 | tf_op jit(solution)/shard_map/pallas_call | solution.py:729
  204.4 9.1 %shard_map.343 = bf16[4,256,2048]{2,1,0:T(8,128)(2,1)} custom-call(s32[8,4,256]{2,1,0:T(4,128)} %convert_element_type.314.slots_ref, bf16[4,512,352]{2,1,0:T(8,128)(2,1)} %get-tuple-element.204.refs_0_.act_ref, bf16[4,352,2048]{2,1,0:T(8,128)(2,1)} %refs_1_.3, bf16[2048,128]{1,0:T(8,128)(2,1)} %get-tuple-element.174.refs_2_.act_ref, ...), custom_call_target="tpu_custom_call" | custom-call | flops 12348030976 | bytes 39845888 | tf_op jit(solution)/shard_map/pallas_call | solution.py:729
  237.8 7.4 %collective-permute-done.22 = bf16[64,1024]{1,0:T(8,128)(2,1)S(1)} collective-permute-done((bf16[64,1024]{1,0:T(8,128)(2,1)S(1)}, bf16[64,1024]{1,0:T(8,128)(2,1)S(1)}, u32[]{:S(2)}, u32[]{:S(2)}) %collective-permute-start.22) | collective-permute-done | bytes 131104 | tf_op jit(solution)/shard_map/ppermute | solution.py:74
  245.3 4.9 %collective-permute-done.27 = bf16[64,1152]{1,0:T(8,128)(2,1)S(1)} collective-permute-done((bf16[64,1152]{1,0:T(8,128)(2,1)S(1)}, bf16[64,1152]{1,0:T(8,128)(2,1)S(1)}, u32[]{:S(2)}, u32[]{:S(2)}) %collective-permute-start.27) | collective-permute-done | bytes 147488 | tf_op jit(solution)/shard_map/ppermute | solution.py:74
  257.0 10.0 %shard_map.344 = (bf16[2,256,2048]{2,1,0:T(8,128)(2,1)}, bf16[2,256,2048]{2,1,0:T(8,128)(2,1)}) custom-call(s32[8,4,256]{2,1,0:T(4,128)} %convert_element_type.314.slots_ref, bf16[4,512,352]{2,1,0:T(8,128)(2,1)} %get-tuple-element.204.refs_0_.act_ref, bf16[4,352,2048]{2,1,0:T(8,128)(2,1)} %refs_1_.3, bf16[2048,128]{1,0:T(8,128)(2,1)} %get-tuple-element.174.refs_2_.act_ref, ...), custom_call_target="tpu_custom_call" | custom-call | flops 12348030976 | bytes 39845888 | tf_op jit(solution)/shard_map/pallas_call | solution.py:729
  267.1 12.9 %shard_map.345 = bf16[8,288,256]{2,1,0:T(8,128)(2,1)} custom-call(s32[8]{0:T(128)} %copy-done.21, s32[1]{0:T(128)} %bitcast.tensor_ref, bf16[2048,256]{1,0:T(8,128)(2,1)} %get-tuple-element.173.refs_4_.delta_ref, bf16[2048,128]{1,0:T(8,128)(2,1)} %get-tuple-element.174.refs_2_.act_ref, bf16[8,272,2048]{2,1,0:T(8,128)(2,1)} %bitcast.129, ...), custom_call_target="tpu_custom_call" | custom-call | flops 12884901888 | bytes 67108864 | tf_op jit(solution)/shard_map/pallas_call | solution.py:776
  281.4 10.4 %shard_map.346 = (f32[256,144]{1,0:T(8,128)}, bf16[256,144]{1,0:T(8,128)(2,1)}, bf16[256,144]{1,0:T(8,128)(2,1)}, bf16[256,144]{1,0:T(8,128)(2,1)}, bf16[256,768...) custom-call(s32[1]{0:T(128)} %bitcast.tensor_ref, s32[8]{0:T(128)} %copy-done.21, ...), custom_call_target="tpu_custom_call" | custom-call | flops 6979321856 | bytes 25505792 | tf_op jit(solution)/shard_map/pallas_call | solution.py:805
  306.6 4.9 %shard_map.349 = (f32[64,2048]{1,0:T(8,128)}, bf16[64,2048]{1,0:T(8,128)(2,1)}, bf16[64,2048]{1,0:T(8,128)(2,1)}, bf16[64,2048]{1,0:T(8,128)(2,1)}, bf16[256,144]{1,0:T(8,128)(2,1)}) custom-call(s32[1]{0:T(128)} %bitcast.tensor_ref, bf16[256,768]{1,0:T(8,128)(2,1)} %get-tuple-element.183.right_ref.query_grad_ref, bf16[2048,768]{1,0:T(8,128)(2,1)} %query_weight_ref.1, ...), custom_call_target="tpu_custom_call" | custom-call | flops 3825205248 | bytes 17989632 | tf_op jit(solution)/shard_map/pallas_call | solution.py:805
  328.3 19.7 %shard_map.350 = (f32[4,352,2048]{2,1,0:T(8,128)}, f32[4,352,2048]{2,1,0:T(8,128)}, f32[4,352,2048]{2,1,0:T(8,128)}) custom-call(bf16[4,512,2048]{2,1,0:T(8,128)(2,1)} %get-tuple-element.150.rows_ref, bf16[4,512,2048]{2,1,0:T(8,128)(2,1)} %get-tuple-element.143.grads_ref, bf16[4,512,352]{2,1,0:T(8,128)(2,1)} %get-tuple-element.204.refs_0_.act_ref, ...), custom_call_target="tpu_custom_call" | custom-call | flops 35433480192 | bytes 205520896 | tf_op jit(solution)/shard_map/pallas_call | solution.py:758
  382.0 6.3 %collective-permute-done.38 = bf16[128,2048]{1,0:T(8,128)(2,1)} collective-permute-done((bf16[128,2048]{1,0:T(8,128)(2,1)}, bf16[128,2048]{1,0:T(8,128)(2,1)}, u32[]{:S(2)}, u32[]{:S(2)}) %collective-permute-start.38) | collective-permute-done | bytes 524320 | tf_op jit(solution)/shard_map/ppermute | solution.py:74
  396.6 6.7 %collective-permute-done.46 = bf16[64,2048]{1,0:T(8,128)(2,1)S(1)} collective-permute-done((bf16[64,2048]{1,0:T(8,128)(2,1)S(1)}, bf16[64,2048]{1,0:T(8,128)(2,1)S(1)}, u32[]{:S(2)}, u32[]{:S(2)}) %collective-permute-start.46) | collective-permute-done | bytes 262176 | tf_op jit(solution)/shard_map/ppermute | solution.py:74
  421.6 8.0 %collective-permute-done.58 = f32[1,80]{1,0:T(1,128)S(1)} collective-permute-done((f32[1,80]{1,0:T(1,128)S(1)}, f32[1,80]{1,0:T(1,128)S(1)}, u32[]{:S(2)}, u32[]{:S(2)}) %collective-permute-start.58) | collective-permute-done | bytes 352 | tf_op jit(solution)/shard_map/ppermute | solution.py:74
  (320 shorter events, 193.5 us)
Async XLA Ops:
  7.2 82.5 %all-gather.3.cloned.1.call-start = ((), (), s32[]{:S(2)}) async-start(), calls=%async_computation.1 | async-start | bytes 10027008 | tf_op jit(solution)/shard_map/all_gather | solution.py:878
  38.0 21.7 %collective-permute-start.4 = (bf16[64,2048]{1,0:T(8,128)(2,1)}, bf16[64,2048]{1,0:T(8,128)(2,1)}, u32[]{:S(2)}, u32[]{:S(2)}) collective-permute-start(bf16[64,2048]{1,0:T(8,128)(2,1)} %get-tuple-element.135), channel_id=1, source_target_pairs={{0,2},{1,3},{2,0},{3,1},{4,6},{5,7},{6,4},{7,5},{8,10},{9,11},{10,... | collective-permute-start | bytes 786440 | tf_op jit(solution)/shard_map/ppermute | solution.py:74
  40.9 18.8 %collective-permute-start.5 = (bf16[64,2048]{1,0:T(8,128)(2,1)}, bf16[64,2048]{1,0:T(8,128)(2,1)}, u32[]{:S(2)}, u32[]{:S(2)}) collective-permute-start(bf16[64,2048]{1,0:T(8,128)(2,1)} %get-tuple-element.136), channel_id=1, source_target_pairs={{0,3},{1,2},{2,1},{3,0},{4,7},{5,6},{6,5},{7,4},{8,11},{9,10},{10,... | collective-permute-start | bytes 786440 | tf_op jit(solution)/shard_map/ppermute | solution.py:74
  61.4 24.7 %collective-permute-start.8 = (bf16[64,2048]{1,0:T(8,128)(2,1)S(1)}, bf16[64,2048]{1,0:T(8,128)(2,1)S(1)}, u32[]{:S(2)}, u32[]{:S(2)}) collective-permute-start(bf16[64,2048]{1,0:T(8,128)(2,1)S(1)} %multiply_convert_fusion), channel_id=1, source_target_pairs={{0,3},{1,2},{2,1},{3,0},{4,7},{5,6},{6,5},{7,4},{8,11},{9,10},{10,... | collective-permute-start | bytes 786440 | tf_op jit(solution)/shard_map/ppermute | solution.py:74
  63.8 22.6 %collective-permute-start.7 = (bf16[64,2048]{1,0:T(8,128)(2,1)S(1)}, bf16[64,2048]{1,0:T(8,128)(2,1)S(1)}, u32[]{:S(2)}, u32[]{:S(2)}) collective-permute-start(bf16[64,2048]{1,0:T(8,128)(2,1)S(1)} %multiply_convert_fusion), channel_id=1, source_target_pairs={{0,2},{1,3},{2,0},{3,1},{4,6},{5,7},{6,4},{7,5},{8,10},{9,11},{10,... | collective-permute-start | bytes 786440 | tf_op jit(solution)/shard_map/ppermute | solution.py:74
  86.6 27.7 %collective-permute-start.14 = (bf16[256,2048]{1,0:T(8,128)(2,1)S(1)}, bf16[256,2048]{1,0:T(8,128)(2,1)}, u32[]{:S(2)}, u32[]{:S(2)}) collective-permute-start(bf16[256,2048]{1,0:T(8,128)(2,1)S(1)} %pad_maximum_fusion.1.refs_1_.refs_4_.block_ref), channel_id=1, source_target_pairs={{0,4},{4,0},{8,12},{12,8},{16,20},{20,16},{24,28},{28,24},{1,5},{5... | collective-permute-start | bytes 3145736 | tf_op jit(solution)/shard_map/ppermute | solution.py:74
  86.7 27.1 %collective-permute-start.11 = (bf16[256,2048]{1,0:T(8,128)(2,1)S(1)}, bf16[256,2048]{1,0:T(8,128)(2,1)}, u32[]{:S(2)}, u32[]{:S(2)}) collective-permute-start(bf16[256,2048]{1,0:T(8,128)(2,1)S(1)} %pad_maximum_fusion.1.refs_1_.refs_4_.block_ref), channel_id=1, source_target_pairs={{0,16},{4,12},{8,24},{12,4},{16,0},{20,28},{24,8},{28,20},{1,17},{... | collective-permute-start | bytes 3145736 | tf_op jit(solution)/shard_map/ppermute | solution.py:91
  88.2 24.1 %collective-permute-start.9 = (bf16[256,2048]{1,0:T(8,128)(2,1)S(1)}, bf16[256,2048]{1,0:T(8,128)(2,1)}, u32[]{:S(2)}, u32[]{:S(2)}) collective-permute-start(bf16[256,2048]{1,0:T(8,128)(2,1)S(1)} %pad_maximum_fusion.1.refs_1_.refs_4_.block_ref), channel_id=1, source_target_pairs={{0,8},{4,20},{8,0},{12,28},{16,24},{20,4},{24,16},{28,12},{1,9},{5... | collective-permute-start | bytes 3145736 | tf_op jit(solution)/shard_map/ppermute | solution.py:91
  195.6 22.6 %collective-permute-start.24 = (bf16[2,256,1152]{2,1,0:T(8,128)(2,1)}, bf16[2,256,1152]{2,1,0:T(8,128)(2,1)}, u32[]{:S(2)}, u32[]{:S(2)}) collective-permute-start(bf16[2,256,1152]{2,1,0:T(8,128)(2,1)} %get-tuple-element.160), channel_id=1, source_target_pairs={{0,16},{4,12},{8,24},{12,4},{16,0},{20,28},{24,8},{28,20},{1,17},{... | collective-permute-start | bytes 3538952 | tf_op jit(solution)/shard_map/ppermute | solution.py:91
  202.9 19.1 %collective-permute-start.20 = (bf16[1,256,1024]{2,1,0:T(8,128)(2,1)S(1)}, bf16[1,256,1024]{2,1,0:T(8,128)(2,1)}, u32[]{:S(2)}, u32[]{:S(2)}) collective-permute-start(bf16[1,256,1024]{2,1,0:T(8,128)(2,1)S(1)} %slice.488), channel_id=1, source_target_pairs={{0,8},{4,20},{8,0},{12,28},{16,24},{20,4},{24,16},{28,12},{1,9},{5... | collective-permute-start | bytes 1572872 | tf_op jit(solution)/shard_map/ppermute | solution.py:91
  213.5 43.5 %collective-permute-start.19 = (bf16[4,256,2048]{2,1,0:T(8,128)(2,1)}, bf16[4,256,2048]{2,1,0:T(8,128)(2,1)}, u32[]{:S(2)}, u32[]{:S(2)}) collective-permute-start(bf16[4,256,2048]{2,1,0:T(8,128)(2,1)} %shard_map.343), channel_id=1, source_target_pairs={{0,4},{4,0},{8,12},{12,8},{16,20},{20,16},{24,28},{28,24},{1,5},{5... | collective-permute-start | bytes 12582920 | tf_op jit(solution)/shard_map/ppermute | solution.py:74
  227.2 18.0 %collective-permute-start.22 = (bf16[64,1024]{1,0:T(8,128)(2,1)S(1)}, bf16[64,1024]{1,0:T(8,128)(2,1)S(1)}, u32[]{:S(2)}, u32[]{:S(2)}) collective-permute-start(bf16[64,1024]{1,0:T(8,128)(2,1)S(1)} %get-tuple-element.359), channel_id=1, source_target_pairs={{0,2},{1,3},{2,0},{3,1},{4,6},{5,7},{6,4},{7,5},{8,10},{9,11},{10,... | collective-permute-start | bytes 393224 | tf_op jit(solution)/shard_map/ppermute | solution.py:74
  252.6 27.4 %collective-permute-start.32 = (bf16[72,2048]{1,0:T(8,128)(2,1)S(1)}, bf16[72,2048]{1,0:T(8,128)(2,1)S(1)}, u32[]{:S(2)}, u32[]{:S(2)}) collective-permute-start(bf16[72,2048]{1,0:T(8,128)(2,1)S(1)} %maximum_maximum_fusion.refs_0_), channel_id=1, source_target_pairs={{0,3},{1,2},{2,1},{3,0},{4,7},{5,6},{6,5},{7,4},{8,11},{9,10},{10,... | collective-permute-start | bytes 884744 | tf_op jit(solution)/shard_map/ppermute | solution.py:74
  254.8 25.2 %collective-permute-start.31 = (bf16[72,2048]{1,0:T(8,128)(2,1)S(1)}, bf16[72,2048]{1,0:T(8,128)(2,1)S(1)}, u32[]{:S(2)}, u32[]{:S(2)}) collective-permute-start(bf16[72,2048]{1,0:T(8,128)(2,1)S(1)} %maximum_maximum_fusion.refs_0_), channel_id=1, source_target_pairs={{0,2},{1,3},{2,0},{3,1},{4,6},{5,7},{6,4},{7,5},{8,10},{9,11},{10,... | collective-permute-start | bytes 884744 | tf_op jit(solution)/shard_map/ppermute | solution.py:74
  254.8 25.3 %collective-permute-start.30 = (bf16[72,2048]{1,0:T(8,128)(2,1)S(1)}, bf16[72,2048]{1,0:T(8,128)(2,1)S(1)}, u32[]{:S(2)}, u32[]{:S(2)}) collective-permute-start(bf16[72,2048]{1,0:T(8,128)(2,1)S(1)} %maximum_maximum_fusion.refs_0_), channel_id=1, source_target_pairs={{0,1},{1,0},{2,3},{3,2},{4,5},{5,4},{6,7},{7,6},{8,9},{9,8},{10,11... | collective-permute-start | bytes 884744 | tf_op jit(solution)/shard_map/ppermute | solution.py:74
  280.9 40.9 %collective-permute-start.29 = (bf16[2,256,2048]{2,1,0:T(8,128)(2,1)}, bf16[2,256,2048]{2,1,0:T(8,128)(2,1)}, u32[]{:S(2)}, u32[]{:S(2)}) collective-permute-start(bf16[2,256,2048]{2,1,0:T(8,128)(2,1)} %get-tuple-element.166), channel_id=1, source_target_pairs={{0,16},{4,12},{8,24},{12,4},{16,0},{20,28},{24,8},{28,20},{1,17},{... | collective-permute-start | bytes 6291464 | tf_op jit(solution)/shard_map/ppermute | solution.py:91
  313.4 34.6 %collective-permute-start.39 = (bf16[64,2048]{1,0:T(8,128)(2,1)}, bf16[64,2048]{1,0:T(8,128)(2,1)S(1)}, u32[]{:S(2)}, u32[]{:S(2)}) collective-permute-start(bf16[64,2048]{1,0:T(8,128)(2,1)} %get-tuple-element.199), channel_id=1, source_target_pairs={{0,1},{1,0},{2,3},{3,2},{4,5},{5,4},{6,7},{7,6},{8,9},{9,8},{10,11... | collective-permute-start | bytes 786440 | tf_op jit(solution)/shard_map/ppermute | solution.py:74
  314.4 33.6 %collective-permute-start.40 = (bf16[64,2048]{1,0:T(8,128)(2,1)}, bf16[64,2048]{1,0:T(8,128)(2,1)}, u32[]{:S(2)}, u32[]{:S(2)}) collective-permute-start(bf16[64,2048]{1,0:T(8,128)(2,1)} %get-tuple-element.200), channel_id=1, source_target_pairs={{0,2},{1,3},{2,0},{3,1},{4,6},{5,7},{6,4},{7,5},{8,10},{9,11},{10,... | collective-permute-start | bytes 786440 | tf_op jit(solution)/shard_map/ppermute | solution.py:74
  316.1 31.9 %collective-permute-start.41 = (bf16[64,2048]{1,0:T(8,128)(2,1)}, bf16[64,2048]{1,0:T(8,128)(2,1)}, u32[]{:S(2)}, u32[]{:S(2)}) collective-permute-start(bf16[64,2048]{1,0:T(8,128)(2,1)} %get-tuple-element.201), channel_id=1, source_target_pairs={{0,3},{1,2},{2,1},{3,0},{4,7},{5,6},{6,5},{7,4},{8,11},{9,10},{10,... | collective-permute-start | bytes 786440 | tf_op jit(solution)/shard_map/ppermute | solution.py:74
  320.3 36.6 %collective-permute-start.45 = (bf16[2,256,768]{2,1,0:T(8,128)(2,1)}, bf16[2,256,768]{2,1,0:T(8,128)(2,1)}, u32[]{:S(2)}, u32[]{:S(2)}) collective-permute-start(bf16[2,256,768]{2,1,0:T(8,128)(2,1)} %add_convert_fusion), channel_id=1, source_target_pairs={{0,16},{4,12},{8,24},{12,4},{16,0},{20,28},{24,8},{28,20},{1,17},{... | collective-permute-start | bytes 2359304 | tf_op jit(solution)/shard_map/ppermute | solution.py:91
  327.2 33.6 %collective-permute-start.36 = (bf16[1,256,2048]{2,1,0:T(8,128)(2,1)}, bf16[1,256,2048]{2,1,0:T(8,128)(2,1)}, u32[]{:S(2)}, u32[]{:S(2)}) collective-permute-start(bf16[1,256,2048]{2,1,0:T(8,128)(2,1)} %slice.486), channel_id=1, source_target_pairs={{0,8},{4,20},{8,0},{12,28},{16,24},{20,4},{24,16},{28,12},{1,9},{5... | collective-permute-start | bytes 3145736 | tf_op jit(solution)/shard_map/ppermute | solution.py:91
  348.0 30.6 %all-to-all-start = ((bf16[8,288,256]{2,1,0:T(8,128)(2,1)}), bf16[8,288,256]{2,1,0:T(8,128)(2,1)S(1)}, u32[]{:S(2)}, u32[]{:S(2)}) async-start(bf16[8,288,256]{2,1,0:T(8,128)(2,1)} %shard_map.345), calls=%async_computation | async-start | bytes 2359296 | tf_op jit(solution)/shard_map/all_to_all | solution.py:1112
  405.4 25.5 %collective-permute-start.56 = (bf16[64,2048]{1,0:T(8,128)(2,1)S(1)}, bf16[64,2048]{1,0:T(8,128)(2,1)S(1)}, u32[]{:S(2)}, u32[]{:S(2)}) collective-permute-start(bf16[64,2048]{1,0:T(8,128)(2,1)S(1)} %fusion.18), channel_id=1, source_target_pairs={{0,3},{1,2},{2,1},{3,0},{4,7},{5,6},{6,5},{7,4},{8,11},{9,10},{10,... | collective-permute-start | bytes 786440 | tf_op jit(solution)/shard_map/ppermute | solution.py:74
  407.8 23.0 %collective-permute-start.55 = (bf16[64,2048]{1,0:T(8,128)(2,1)S(1)}, bf16[64,2048]{1,0:T(8,128)(2,1)S(1)}, u32[]{:S(2)}, u32[]{:S(2)}) collective-permute-start(bf16[64,2048]{1,0:T(8,128)(2,1)S(1)} %fusion.18), channel_id=1, source_target_pairs={{0,2},{1,3},{2,0},{3,1},{4,6},{5,7},{6,4},{7,5},{8,10},{9,11},{10,... | collective-permute-start | bytes 786440 | tf_op jit(solution)/shard_map/ppermute | solution.py:74
  (74 other events, 735.9 us)
Sparse Core Ops, SparseCore 0:
  10.8 59.3 all-gather.2
